TPU v7x, 256 devices: a whole 4x4x8 slice. The times are simulated.
256 devices in a mesh: grp: 4 (over z_lo), row: 8 (over z_hi, x), col: 8 (over y, core).
Axes of the slice: x: 4, y: 4, z: 8 (z_hi: 2, z_lo: 4; z = z_hi * 4 + z_lo), core: 2. Of those that a mesh axis runs over, the one named last changes fastest.
Arguments:
- dec_input: bfloat16 [3, 8, 64, 128, 128], P(None, None, 'row', 'col'), may hold values from -6 to 6
- target: bfloat16 [3, 3, 8, 64, 128], P(None, None, 'col', 'row'), may hold values from -5 to 5
- conv_first: bfloat16 [3456, 128], replicated, may hold values from -0.109375 to 0.109375
- conv_second: bfloat16 [3456, 128], replicated, may hold values from -0.109375 to 0.109375
- rgb_weight: bfloat16 [3, 128], replicated, may hold values from -0.5 to 0.5
- vgg_first: bfloat16 [27, 64], replicated, may hold values from -1.25 to 1.25
- vgg_second: bfloat16 [576, 64], replicated, may hold values from -0.25 to 0.25
- vgg_third: bfloat16 [576, 128], replicated, may hold values from -0.25 to 0.25
Outputs:
- grad_first: float32 [442368], P(('grp', 'row', 'col'))
- grad_second: float32 [442368], P(('grp', 'row', 'col'))
All inputs are finite; a program needn't handle non-finite values.
Results may differ from a plain program's by a relative error of at most 0.015.
Values may be sent and summed in bfloat16 or wider, within the bound.
A program may use at most 128 MiB of HBM per device.

v0:
```python
import functools

import jax
import jax.numpy as jnp
from jax import lax
from jax.experimental import pallas as pl
from jax.experimental.pallas import tpu as pltpu
from jax.sharding import PartitionSpec as P

MESH = pl.DeviceIdType.MESH

gelu_scale = 0.7978845608028654
gelu_cubic = 0.044715


def reduce_kernel(
    a_ref, b_ref, out_ref, core_in, held, x_in, y_in, mid_a, mid_b, last, z_in, send_sem, recv_sem
):
    g, r, c = lax.axis_index("grp"), lax.axis_index("row"), lax.axis_index("col")
    zh, x, y, core = r // 4, lax.rem(r, 4), c // 2, lax.rem(c, 2)
    z = g * 2 + zh
    other = 1 - core

    def at_x(step):
        return (g, zh * 4 + lax.rem(x + step, 4), c)

    def at_y(step):
        return (g, r, lax.rem(y + step, 4) * 2 + core)

    def at_z(step):
        to = lax.rem(z + step, 8)
        return (to // 2, lax.rem(to, 2) * 4 + x, c)

    partner = (g, r, y * 2 + other)
    barrier = pltpu.get_barrier_semaphore()
    everyone = [partner] + [at_x(s) for s in (1, 2, 3)] + [at_y(s) for s in (1, 2, 3)]
    everyone += [at_z(s) for s in range(1, 8)]
    for peer in everyone:
        pl.semaphore_signal(barrier, inc=1, device_id=peer, device_id_type=MESH)
    pl.semaphore_wait(barrier, len(everyone))

    def send(src, dst, slot, peer):
        copy = pltpu.make_async_remote_copy(
            src_ref=src,
            dst_ref=dst,
            send_sem=send_sem.at[slot],
            recv_sem=recv_sem.at[slot],
            device_id=peer,
            device_id_type=MESH,
        )
        copy.start()
        return copy

    f32, b16 = jnp.float32, jnp.bfloat16
    first = [
        send(a_ref.at[other], core_in.at[0], 0, partner),
        send(b_ref.at[other], core_in.at[1], 1, partner),
    ]
    first[0].wait()
    held[0] = (a_ref[core].astype(f32) + core_in[0].astype(f32)).astype(b16)
    step_a = [
        send(held.at[0, :, lax.rem(x + s, 4)], x_in.at[s - 1], 1 + s, at_x(s)) for s in (1, 2, 3)
    ]
    first[1].wait()
    held[1] = (b_ref[core].astype(f32) + core_in[1].astype(f32)).astype(b16)
    step_b = [
        send(held.at[1, :, :, lax.rem(y + s, 4)], y_in.at[s - 1], 4 + s, at_y(s)) for s in (1, 2, 3)
    ]
    for copy in step_a:
        copy.wait()
    total = held[0, :, x].astype(f32)
    for s in range(3):
        total += x_in[s].astype(f32)
    mid_a[...] = total.astype(b16)
    next_a = [
        send(mid_a.at[:, lax.rem(y + s, 4)], last.at[0, s - 1], 7 + s, at_y(s)) for s in (1, 2, 3)
    ]
    for copy in step_b:
        copy.wait()
    total = held[1, :, :, y].astype(f32)
    for s in range(3):
        total += y_in[s].astype(f32)
    mid_b[...] = total.astype(b16)
    next_b = [
        send(mid_b.at[:, lax.rem(x + s, 4)], last.at[1, s - 1], 10 + s, at_x(s)) for s in (1, 2, 3)
    ]
    for copy in next_a:
        copy.wait()
    total = mid_a[:, y].astype(f32)
    for s in range(3):
        total += last[0, s].astype(f32)
    last[0, 3] = total.astype(b16)
    final_a = [
        send(last.at[0, 3, lax.rem(z + s, 8)], z_in.at[0, s - 1], 13 + s, at_z(s)) for s in range(1, 8)
    ]
    for copy in next_b:
        copy.wait()
    total = mid_b[:, x].astype(f32)
    for s in range(3):
        total += last[1, s].astype(f32)
    last[1, 3] = total.astype(b16)
    final_b = [
        send(last.at[1, 3, lax.rem(z + s, 8)], z_in.at[1, s - 1], 20 + s, at_z(s)) for s in range(1, 8)
    ]
    for which, copies in ((0, final_a), (1, final_b)):
        for copy in copies:
            copy.wait()
        total = last[which, 3, z].astype(f32)
        for s in range(7):
            total += z_in[which, s].astype(f32)
        out_ref[which] = total


def scattered_sums(first_terms, second_terms):
    b16 = jnp.bfloat16
    sums = pl.pallas_call(
        reduce_kernel,
        out_shape=jax.ShapeDtypeStruct((2, 16, 128), jnp.float32),
        in_specs=[pl.BlockSpec(memory_space=pltpu.VMEM)] * 2,
        out_specs=pl.BlockSpec(memory_space=pltpu.VMEM),
        scratch_shapes=[
            pltpu.VMEM((2, 8, 4, 4, 16, 128), b16),
            pltpu.VMEM((2, 8, 4, 4, 16, 128), b16),
            pltpu.VMEM((3, 8, 4, 16, 128), b16),
            pltpu.VMEM((3, 8, 4, 16, 128), b16),
            pltpu.VMEM((8, 4, 16, 128), b16),
            pltpu.VMEM((8, 4, 16, 128), b16),
            pltpu.VMEM((2, 4, 8, 16, 128), b16),
            pltpu.VMEM((2, 7, 16, 128), b16),
            pltpu.SemaphoreType.DMA((28,)),
            pltpu.SemaphoreType.DMA((28,)),
        ],
        compiler_params=pltpu.CompilerParams(
            collective_id=1, has_side_effects=True, vmem_limit_bytes=40 * 2**20
        ),
    )(first_terms.reshape(2, 8, 4, 4, 16, 128), second_terms.reshape(2, 8, 4, 4, 16, 128))
    flat = sums[:, :14].reshape(2, 14 * 128)
    start = lax.rem(lax.axis_index("col"), 2) * 64
    own = lax.dynamic_slice_in_dim(flat, start, 1728, axis=1)
    return own[0], own[1]


def position():
    return lax.axis_index("grp"), lax.axis_index("row"), lax.axis_index("col")


def same_place(one, other):
    return (one[0] == other[0]) & (one[1] == other[1]) & (one[2] == other[2])


def row_count(r):
    return 1 + jnp.where(r > 0, 1, 0) + jnp.where(r < 7, 1, 0)


def remote(src, dst, sems, slot, peer):
    return pltpu.make_async_remote_copy(
        src_ref=src,
        dst_ref=dst,
        send_sem=sems[0].at[slot],
        recv_sem=sems[1].at[slot],
        device_id=peer,
        device_id_type=MESH,
    )


def halo_kernel(
    own_ref, left_ref, right_ref, guide_ref,
    top_out, bottom_out, left_out, right_out, corner_out, guide_out, send_sem, recv_sem,
):
    g, r, c = position()
    sems = (send_sem, recv_sem)
    west, east = (g, r, lax.rem(c + 7, 8)), (g, r, lax.rem(c + 1, 8))
    has_up, has_down = r > 0, r < 7
    barrier = pltpu.get_barrier_semaphore()

    def greet(row_index):
        for step in (7, 0, 1):
            peer = (g, row_index, lax.rem(c + step, 8))
            pl.semaphore_signal(barrier, inc=1, device_id=peer, device_id_type=MESH)

    for peer in (west, east):
        pl.semaphore_signal(barrier, inc=1, device_id=peer, device_id_type=MESH)
    pl.when(has_up)(lambda: greet(r - 1))
    pl.when(has_down)(lambda: greet(r + 1))
    pl.semaphore_wait(barrier, 3 * row_count(r) - 1)
    sideways = [
        remote(left_ref, right_out, sems, 0, west),
        remote(right_ref, left_out, sems, 1, east),
    ]

    def to_row(row_index, rows, strip_out, corners, guide_slot, first_slot):
        west_peer = (g, row_index, west[2])
        east_peer = (g, row_index, east[2])
        here = (g, row_index, c)
        return [
            remote(own_ref.at[:, rows], strip_out, sems, first_slot, here),
            remote(guide_ref, guide_out.at[guide_slot], sems, first_slot + 1, here),
            remote(left_ref.at[rows], corner_out.at[corners + 1], sems, first_slot + 2, west_peer),
            remote(right_ref.at[rows], corner_out.at[corners], sems, first_slot + 3, east_peer),
        ]

    upward = to_row(r - 1, pl.ds(0, 3), bottom_out, 2, 1, 2)
    downward = to_row(r + 1, pl.ds(5, 3), top_out, 0, 0, 6)

    def start(copies):
        for copy in copies:
            copy.start()

    def sent(copies):
        for copy in copies:
            copy.wait_send()

    def landed(copies):
        for copy in copies:
            copy.wait_recv()

    pl.when(has_up)(lambda: start(upward))
    pl.when(has_down)(lambda: start(downward))
    start(sideways)
    landed(sideways)
    pl.when(has_down)(lambda: landed(upward))
    pl.when(has_up)(lambda: landed(downward))
    sent(sideways)
    pl.when(has_up)(lambda: sent(upward))
    pl.when(has_down)(lambda: sent(downward))


def colour_kernel(colour_ref, out_ref, send_sem, recv_sem, own_sem):
    g, r, c = position()
    me = (g, r, c)
    barrier = pltpu.get_barrier_semaphore()
    perceives = g < 3
    source_group = (8 * g + c) // 6

    def signal(peer):
        @pl.when(jnp.logical_not(same_place(peer, me)))
        def _():
            pl.semaphore_signal(barrier, inc=1, device_id=peer, device_id_type=MESH)

    def on_rows(do):
        for step in (-1, 0, 1):
            pl.when((r + step >= 0) & (r + step < 8))(functools.partial(do, step))

    def greet(step):
        for column in range(8):
            signal((source_group, r + step, column))

    def targets(step):
        for slot in range(6):
            frame = 6 * g + slot
            yield slot, (frame // 8, r + step, lax.rem(frame, 8))

    pl.when(perceives)(lambda: on_rows(greet))
    to_itself = jnp.where(perceives & (2 * g + c < 6), 1, 0)
    pl.semaphore_wait(barrier, 6 * row_count(r) - to_itself)

    def outgoing(step, slot, peer):
        return pltpu.make_async_remote_copy(
            src_ref=colour_ref.at[slot + 1],
            dst_ref=out_ref.at[1 - step, c],
            send_sem=send_sem.at[step + 1, slot],
            recv_sem=recv_sem.at[1 - step, c],
            device_id=peer,
            device_id_type=MESH,
        )

    def kept(slot):
        return pltpu.make_async_copy(colour_ref.at[slot + 1], out_ref.at[1, c], own_sem)

    def start(step):
        for slot, peer in targets(step):
            away = jnp.logical_not(same_place(peer, me))
            pl.when(away)(lambda: outgoing(step, slot, peer).start())
            if step == 0:
                pl.when(jnp.logical_not(away))(lambda: kept(slot).start())

    def arrive(step):
        for column in range(8):
            source = (source_group, r + step, column)
            away = jnp.logical_not(same_place(source, me))

            @pl.when(away)
            def _():
                pltpu.make_async_remote_copy(
                    src_ref=colour_ref.at[0],
                    dst_ref=out_ref.at[step + 1, column],
                    send_sem=send_sem.at[0, 0],
                    recv_sem=recv_sem.at[step + 1, column],
                    device_id=source,
                    device_id_type=MESH,
                ).wait_recv()

    def finish(step):
        for slot, peer in targets(step):
            away = jnp.logical_not(same_place(peer, me))
            pl.when(away)(lambda: outgoing(step, slot, peer).wait_send())
            if step == 0:
                pl.when(jnp.logical_not(away))(lambda: kept(slot).wait())

    on_rows(start)
    pl.when(perceives)(lambda: on_rows(arrive))
    on_rows(finish)


def pixel_kernel(strip_ref, out_ref, send_sem, recv_sem, own_sem):
    g, r, c = position()
    me = (g, r, c)
    barrier = pltpu.get_barrier_semaphore()
    perceives = g < 3
    frame = 8 * g + c
    home = frame // 6
    place = lax.rem(frame, 6)
    before = perceives & (place == 0) & (home > 0)
    after = perceives & (place == 5) & (home < 3)

    def on_rows(do):
        for step in (-1, 0, 1):
            pl.when((r + step >= 0) & (r + step < 8))(functools.partial(do, step))

    def sources(do):
        for slot in range(8):
            source_frame = 6 * g - 1 + slot
            inside = (source_frame >= 0) & (source_frame < 24)

            def each(step, slot=slot, source_frame=source_frame):
                source = (source_frame // 8, r + step, lax.rem(source_frame, 8))
                pl.when(jnp.logical_not(same_place(source, me)))(
                    functools.partial(do, step, slot, source)
                )

            pl.when(inside)(functools.partial(on_rows, each))

    def greet(step, slot, source):
        pl.semaphore_signal(barrier, inc=1, device_id=source, device_id_type=MESH)

    def targets(do):
        for kind, (group, needed) in enumerate(
            ((home, perceives), (home - 1, before), (home + 1, after))
        ):

            def each(step, kind=kind, group=group):
                for column in range(8):
                    peer = (group, r + step, column)
                    do(kind, step, column, peer, jnp.logical_not(same_place(peer, me)))

            pl.when(needed)(functools.partial(on_rows, each))

    sources(greet)
    groups = jnp.where(perceives, 1, 0) + jnp.where(before, 1, 0) + jnp.where(after, 1, 0)
    to_itself = perceives & (home == g) | before & (home == g + 1) | after & (home == g - 1)
    awaited = 8 * row_count(r) * groups - jnp.where(to_itself, 1, 0)
    pl.when(perceives)(lambda: pl.semaphore_wait(barrier, awaited))

    def outgoing(kind, step, column, peer):
        return pltpu.make_async_remote_copy(
            src_ref=strip_ref,
            dst_ref=out_ref.at[frame - 6 * peer[0] + 1, 1 - step],
            send_sem=send_sem.at[kind, step + 1, column],
            recv_sem=recv_sem.at[frame - 6 * peer[0] + 1, 1 - step],
            device_id=peer,
            device_id_type=MESH,
        )

    def kept():
        return pltpu.make_async_copy(strip_ref, out_ref.at[frame - 6 * g + 1, 1], own_sem)

    def start(kind, step, column, peer, away):
        pl.when(away)(lambda: outgoing(kind, step, column, peer).start())
        if step == 0:
            pl.when(jnp.logical_not(away))(lambda: kept().start())

    def finish(kind, step, column, peer, away):
        pl.when(away)(lambda: outgoing(kind, step, column, peer).wait_send())
        if step == 0:
            pl.when(jnp.logical_not(away))(lambda: kept().wait())

    def arrive(step, slot, source):
        pltpu.make_async_remote_copy(
            src_ref=strip_ref,
            dst_ref=out_ref.at[slot, step + 1],
            send_sem=send_sem.at[0, 0, 0],
            recv_sem=recv_sem.at[slot, step + 1],
            device_id=source,
            device_id_type=MESH,
        ).wait_recv()

    targets(start)
    sources(arrive)
    targets(finish)


def in_vmem(count):
    return [pl.BlockSpec(memory_space=pltpu.VMEM)] * count


def b16(*shape):
    return jax.ShapeDtypeStruct(shape, jnp.bfloat16)


def exchange(kernel, ident, outs, sems, *operands):
    outs = tuple(outs)
    return pl.pallas_call(
        kernel,
        out_shape=outs,
        in_specs=in_vmem(len(operands)),
        out_specs=tuple(in_vmem(len(outs))),
        scratch_shapes=[pltpu.SemaphoreType.DMA(shape) for shape in sems],
        compiler_params=pltpu.CompilerParams(
            collective_id=ident, has_side_effects=True, vmem_limit_bytes=24 * 2**20
        ),
    )(*operands)


def transposed_dot(one, other):
    return lax.dot_general(one, other, (((0,), (0,)), ((), ())), preferred_element_type=jnp.float32)


def side_by_side(value):
    cols = value.shape[0]
    at = lax.broadcasted_iota(jnp.int32, value.shape, 0)
    before = jnp.where(at == 0, 0.0, pltpu.roll(value, 1, 0))
    after = jnp.where(at == cols - 1, 0.0, pltpu.roll(value, cols - 1, 0))
    return jnp.concatenate([before, value, after], axis=1).astype(jnp.bfloat16)


def three_rows(ref, row, count):
    parts = [ref[pl.ds(row + step, count)].reshape(-1, ref.shape[-1]) for step in range(3)]
    return jnp.concatenate(parts, axis=1)


def dot32(one, other):
    return jnp.dot(one, other, preferred_element_type=jnp.float32)


def gelu_both(preact, slope_too):
    square = preact * preact
    inner_tanh = jnp.tanh(gelu_scale * preact * (1.0 + gelu_cubic * square))
    half = 0.5 * (1.0 + inner_tanh)
    value = preact * half
    if not slope_too:
        return value, None
    bend = (0.5 * gelu_scale) * (1.0 + 3.0 * gelu_cubic * square)
    return value, half + preact * (1.0 - inner_tanh * inner_tanh) * bend


def perceptual_kernel(
    planes_ref, w1_ref, w2_ref, w3_ref, w3_back_ref, w2_back_ref, w1_back_ref, out_ref,
    taps, act1, slope1, pooled, delta3, diff2, slope2, delta2, delta1, tmp, pixels,
):
    row0 = lax.axis_index("row") * 8 - 8
    lane = lax.broadcasted_iota(jnp.int32, (192, 128), 1)
    planes = planes_ref[...].reshape(192, 128)
    before = jnp.where(lane == 0, 0.0, pltpu.roll(planes, 1, 1))
    after = jnp.where(lane == 127, 0.0, pltpu.roll(planes, 127, 1))
    taps[:, 0:8] = before.reshape(24, 8, 128)
    taps[:, 8:16] = planes.reshape(24, 8, 128)
    taps[:, 16:24] = after.reshape(24, 8, 128)

    def shown(row):
        return (row0 + row >= 0) & (row0 + row < 64)

    def kept(row, value):
        return jnp.where(shown(row), value, 0.0)

    def first_rows(low, high, slope_too):
        @pl.loop(low, high)
        def _(i):
            cells = taps[pl.ds(i, 3)].reshape(72, 128).astype(jnp.bfloat16)
            value, slope = gelu_both(transposed_dot(cells, w1_ref[...]), slope_too)
            act1[i] = side_by_side(kept(i + 1, value))
            if slope_too:
                slope1[i - 6] = slope

    first_rows(0, 6, False)
    first_rows(6, 16, True)
    first_rows(16, 22, False)

    def second_rows(low, high, slope_too):
        @pl.loop(low, high)
        def _(p):
            plane = dot32(three_rows(act1, 2 * p, 2), w2_ref[...])
            value, slope = gelu_both(plane, slope_too)
            value = kept(2 * p + 2, value)
            if slope_too:
                difference = 0.25 * (value - pltpu.roll(value, 64, 1))
                diff2[pl.ds(2 * p - 4, 2)] = difference.reshape(2, 128, 128)
                slope2[pl.ds(2 * p - 4, 2)] = slope.reshape(2, 128, 128)
            tmp[...] = value[:128] + value[128:]
            mean = 0.25 * (tmp[pl.ds(0, 64, 2)] + tmp[pl.ds(1, 64, 2)])
            pooled[p] = side_by_side(mean)

    second_rows(0, 2, False)
    second_rows(2, 8, True)
    second_rows(8, 10, False)

    @pl.loop(0, 4)
    def _(half):
        j = 2 * half
        plane = dot32(three_rows(pooled, j, 2), w3_ref[...])
        value, slope = gelu_both(plane[:, :128], True)
        guide, _ = gelu_both(plane[:, 128:], False)
        delta = 0.5 * (value - guide) * slope
        delta3[j] = side_by_side(kept(2 * j + 4, delta[:64]))
        delta3[j + 1] = side_by_side(kept(2 * j + 6, delta[64:]))

    @pl.loop(0, 6)
    def _(m):
        grad = 0.25 * dot32(three_rows(delta3, m, 1), w3_back_ref[...])
        tmp[pl.ds(0, 64, 2)] = grad
        tmp[pl.ds(1, 64, 2)] = grad
        spread = tmp[...]
        for k in range(2):
            delta = (spread + diff2[2 * m + k]) * slope2[2 * m + k]
            delta2[2 * m + k] = side_by_side(kept(2 * m + 6, delta))

    @pl.loop(0, 5)
    def _(half):
        n = 2 * half
        grad = dot32(three_rows(delta2, n, 2), w2_back_ref[...])
        for k in range(2):
            delta = grad[128 * k : 128 * (k + 1)] * slope1[n + k]
            delta1[n + k] = side_by_side(kept(n + k + 7, delta))

    @pl.loop(0, 8)
    def _(q):
        grad = lax.dot_general(
            w1_back_ref[...],
            three_rows(delta1, q, 1),
            (((1,), (1,)), ((), ())),
            preferred_element_type=jnp.float32,
        )
        own = planes_ref[q + 8]
        direct = (1.0 / 6.0) * (own - pltpu.roll(own, 5, 0))
        pixels[pl.ds(pl.multiple_of(q * 8, 8), 8)] = grad + direct

    rows = [pixels[pl.ds(k, 8, 8)] for k in range(3)] + [jnp.zeros((8, 128), jnp.float32)]
    out_ref[...] = jnp.concatenate(rows, axis=0).astype(jnp.bfloat16)


def two_blocks(weight):
    _, i, o = weight.shape
    return jnp.pad(weight, ((0, 0), (0, i), (0, o))) + jnp.pad(weight, ((0, 0), (i, 0), (o, 0)))


def perceptual_weights(vgg_first, vgg_second, vgg_third):
    first = vgg_first.reshape(9, 3, 64)
    w1 = jnp.pad(two_blocks(first), ((0, 0), (0, 2), (0, 0))).reshape(72, 128)
    second = vgg_second.reshape(9, 64, 64)
    third = vgg_third.reshape(9, 64, 128)
    w2 = two_blocks(second).reshape(1152, 128)
    w3 = two_blocks(third).reshape(1152, 256)
    w3_back = jnp.pad(jnp.transpose(third[::-1], (0, 2, 1)), ((0, 0), (0, 0), (0, 64))).reshape(1152, 128)
    w2_back = jnp.pad(jnp.transpose(second[::-1], (0, 2, 1)), ((0, 0), (0, 64), (0, 64))).reshape(1152, 128)
    w1_back = jnp.pad(jnp.transpose(first[::-1], (1, 0, 2)), ((0, 5), (0, 0), (0, 64))).reshape(8, 1152)
    return w1, w2, w3, w3_back, w2_back, w1_back


def perceptual_strip(planes, weights):
    f32, half = jnp.float32, jnp.bfloat16
    return pl.pallas_call(
        perceptual_kernel,
        out_shape=b16(32, 128),
        in_specs=in_vmem(7),
        out_specs=in_vmem(1)[0],
        scratch_shapes=[
            pltpu.VMEM((24, 24, 128), f32),
            pltpu.VMEM((22, 128, 384), half),
            pltpu.VMEM((10, 128, 128), f32),
            pltpu.VMEM((10, 64, 384), half),
            pltpu.VMEM((8, 64, 384), half),
            pltpu.VMEM((12, 128, 128), f32),
            pltpu.VMEM((12, 128, 128), f32),
            pltpu.VMEM((12, 128, 384), half),
            pltpu.VMEM((10, 128, 384), half),
            pltpu.VMEM((128, 128), f32),
            pltpu.VMEM((64, 128), f32),
        ],
        compiler_params=pltpu.CompilerParams(vmem_limit_bytes=40 * 2**20),
    )(planes, *weights)


def taps_in_lanes(weight_ref, out_ref):
    for q in range(9):
        for k in range(3):
            tap = 3 * q + k
            out_ref[128 * q : 128 * (q + 1), 128 * k : 128 * (k + 1)] = weight_ref[
                128 * tap : 128 * (tap + 1), :
            ]


def turned_taps(weight_ref, out_ref):
    for q in range(9):
        for k in range(3):
            tap = 26 - 3 * q - k
            block = weight_ref[128 * tap : 128 * (tap + 1), :].astype(jnp.float32)
            out_ref[128 * q : 128 * (q + 1), 128 * k : 128 * (k + 1)] = block.T.astype(jnp.bfloat16)


def conv_frame(source, frame, rows, taps_ref):
    parts = [
        source[frame + dt, pl.ds(dr, rows)].reshape(rows * 32, 128) for dt in range(3) for dr in range(3)
    ]
    sums = dot32(jnp.concatenate(parts, axis=1), taps_ref[...])
    total = pltpu.roll(sums[:, :128], 1, 0) + sums[:, 128:256]
    total += pltpu.roll(sums[:, 256:], rows * 32 - 1, 0)
    return total.reshape(rows, 32, 128)


def silu_parts(preact):
    gate = 1.0 / (1.0 + jnp.exp(-preact))
    return preact * gate, gate * (1.0 + preact * (1.0 - gate))


def forward_kernel(
    cells_ref, first_ref, second_ref, rgb_ref, hidden_out, slope1_out, slope2_out, colour_out, taps1, taps2
):
    g, r, c = position()
    taps_in_lanes(first_ref, taps1)
    taps_in_lanes(second_ref, taps2)
    row = lax.broadcasted_iota(jnp.int32, (12, 32, 128), 0) + (8 * r - 2)
    col = lax.broadcasted_iota(jnp.int32, (12, 32, 128), 1) + (16 * c - 8)
    shown = (row >= 0) & (row < 64) & (col >= 0) & (col < 128)

    @pl.loop(0, 10)
    def _(f):
        value, slope = silu_parts(conv_frame(cells_ref, f, 12, taps1))
        frame = 6 * g - 2 + f
        value = jnp.where(shown, value, 0.0) * jnp.where((frame >= 0) & (frame < 24), 1.0, 0.0)
        hidden_out[f] = value.astype(jnp.bfloat16)
        slope1_out[f] = slope[2:10, 8:24].reshape(128, 128)

    @pl.loop(0, 8)
    def _(f):
        value, slope = silu_parts(conv_frame(hidden_out, f, 10, taps2))
        slope2_out[f] = slope
        own = value[1:9, 8:24].reshape(128, 128).astype(jnp.bfloat16)
        colour = lax.dot_general(
            rgb_ref[...], own, (((1,), (1,)), ((), ())), preferred_element_type=jnp.float32
        )
        colour_out[f] = colour.astype(jnp.bfloat16)


def columns_in_lanes(source, frame0, row0, out_ref):
    @pl.loop(0, 8)
    def _(f):
        value = source[f + frame0, pl.ds(row0, 10)].reshape(320, 128).astype(jnp.float32)
        parts = [pltpu.roll(value, 1, 0), value, pltpu.roll(value, 319, 0)]
        for k, part in enumerate(parts):
            own = part.reshape(10, 32, 128)[:, 8:24]
            out_ref[f, :, :, 128 * k : 128 * (k + 1)] = own.astype(jnp.bfloat16)


def weight_terms(columns, delta, terms, out_ref):
    @pl.loop(0, 9)
    def _(q):
        cells = columns[pl.ds(q // 3, 6), pl.ds(lax.rem(q, 3), 8)].reshape(768, 384)
        terms[pl.ds(pl.multiple_of(384 * q, 384), 384)] = transposed_dot(cells, delta[...])

    terms[pl.ds(3456, 8)] = jnp.zeros((8, 128), jnp.float32)

    @pl.loop(0, 128)
    def _(p):
        out_ref[0, p] = terms[pl.ds(27 * p, 16)].astype(jnp.bfloat16)
        out_ref[1, p] = terms[pl.ds(27 * p + 13, 16)].astype(jnp.bfloat16)


def backward_kernel(
    pixel_ref, cells_ref, hidden_ref, slope1_ref, slope2_ref, second_ref, rgb_ref, first_out, second_out,
    taps, columns, field, delta, terms,
):
    turned_taps(second_ref, taps)

    @pl.loop(0, 8)
    def _(f):
        hidden_grad = transposed_dot(pixel_ref[f], rgb_ref[...])
        value = hidden_grad.reshape(10, 32, 128) * slope2_ref[f]
        field[f] = value.astype(jnp.bfloat16)

        @pl.when((f >= 1) & (f < 7))
        def _():
            own = value[1:9, 8:24].reshape(128, 128).astype(jnp.bfloat16)
            delta[pl.ds(pl.multiple_of(128 * (f - 1), 128), 128)] = own

    columns_in_lanes(hidden_ref, 1, 1, columns)
    weight_terms(columns, delta, terms, second_out)

    @pl.loop(0, 6)
    def _(f):
        back = conv_frame(field, f, 8, taps)[:, 8:24].reshape(128, 128)
        value = (back * slope1_ref[f + 2]).astype(jnp.bfloat16)
        delta[pl.ds(pl.multiple_of(128 * f, 128), 128)] = value

    columns_in_lanes(cells_ref, 2, 2, columns)
    weight_terms(columns, delta, terms, first_out)


def f32_shape(*shape):
    return jax.ShapeDtypeStruct(shape, jnp.float32)


def plain_call(kernel, outs, scratch, *operands):
    return pl.pallas_call(
        kernel,
        out_shape=tuple(outs),
        in_specs=in_vmem(len(operands)),
        out_specs=tuple(in_vmem(len(outs))),
        scratch_shapes=scratch,
        compiler_params=pltpu.CompilerParams(vmem_limit_bytes=48 * 2**20),
    )(*operands)


def inside(start, count, limit):
    positions = start + jnp.arange(count)
    return (positions >= 0) & (positions < limit)


def cell_mask(frame0, frames, row0, rows, col0, cols):
    keep_frames = inside(frame0, frames, 24)
    keep_rows = inside(row0, rows, 64)
    keep_cols = inside(col0, cols, 128)
    return (keep_frames[:, None, None] & keep_rows[None, :, None] & keep_cols[None, None, :])[
        ..., None
    ]


def local(dec_input, target, conv_first, conv_second, rgb_weight, vgg_first, vgg_second, vgg_third):
    g, r, c = position()
    channels = dec_input.shape[-1]
    frame0, row0, col0 = 6 * g, 8 * r, 16 * c
    video = jnp.pad(dec_input.reshape(24, 8, 16, channels), ((3, 3), (0, 0), (0, 0), (0, 0)))
    own = lax.dynamic_slice_in_dim(video, frame0, 12, axis=0)

    def columns(part):
        return jnp.transpose(part, (1, 0, 2, 3)).reshape(8, 48, channels)

    guide_own = lax.dynamic_index_in_dim(target, jnp.minimum(g, 2), 1, keepdims=False)
    guide_own = guide_own.reshape(24, 128)
    top, bottom, left, right, corners, guide_near = exchange(
        halo_kernel,
        2,
        (
            b16(12, 3, 16, channels), b16(12, 3, 16, channels), b16(8, 48, channels),
            b16(8, 48, channels), b16(4, 3, 48, channels), b16(2, 32, 128),
        ),
        ((10,), (10,)),
        own,
        columns(own[:, :, :4]),
        columns(own[:, :, 12:]),
        jnp.pad(guide_own, ((0, 8), (0, 0))),
    )

    def strip(part):
        return jnp.transpose(part.reshape(-1, 12, 4, channels), (1, 0, 2, 3))

    gap = jnp.zeros((12, 14, 4, channels), jnp.bfloat16)
    cells = jnp.concatenate(
        [
            gap,
            jnp.concatenate([strip(corners[0]), strip(left), strip(corners[2])], axis=1),
            jnp.concatenate([top, own, bottom], axis=1),
            jnp.concatenate([strip(corners[1]), strip(right), strip(corners[3])], axis=1),
            gap,
        ],
        axis=2,
    )
    cells = jnp.where(
        inside(row0 - 3, 14, 64)[None, :, None, None] & inside(col0 - 8, 32, 128)[None, None, :, None],
        cells,
        jnp.zeros_like(cells),
    )
    half = jnp.bfloat16
    rgb = jnp.pad(rgb_weight, ((0, 13), (0, 0)))
    hidden, slope1, slope2, colour = plain_call(
        forward_kernel,
        (b16(10, 12, 32, 128), f32_shape(10, 128, 128), f32_shape(8, 10, 32, 128), b16(8, 16, 128)),
        [pltpu.VMEM((1152, 384), half), pltpu.VMEM((1152, 384), half)],
        cells, conv_first, conv_second, rgb,
    )
    colour_near = exchange(
        colour_kernel,
        3,
        (b16(3, 8, 16, 128),),
        ((3, 6), (3, 8), ()),
        colour,
    )[0]
    images = jnp.transpose(colour_near[:, :, :3].reshape(3, 8, 3, 8, 16), (0, 3, 2, 1, 4))
    guides = jnp.stack(
        [guide_near[0, :24].reshape(3, 8, 128), guide_own.reshape(3, 8, 128), guide_near[1, :24].reshape(3, 8, 128)]
    )
    guides = jnp.transpose(guides, (0, 2, 1, 3))
    planes = jnp.concatenate([images.reshape(24, 3, 128), guides.reshape(24, 3, 128)], axis=1)
    planes = jnp.where(inside(row0 - 8, 24, 64)[:, None, None], planes, jnp.zeros_like(planes))
    planes = jnp.pad(planes.astype(jnp.float32), ((0, 0), (0, 2), (0, 0)))
    strip_out = perceptual_strip(planes, perceptual_weights(vgg_first, vgg_second, vgg_third))
    returned = exchange(
        pixel_kernel,
        4,
        (b16(8, 3, 32, 128),),
        ((3, 3, 8), (8, 3), ()),
        strip_out,
    )[0]
    rows_near = jnp.transpose(returned[:, :, :24].reshape(8, 3, 3, 8, 128), (2, 0, 1, 3, 4))
    rows_near = rows_near.reshape(3, 8, 24, 128)[:, :, 7:17]
    rows_near = jnp.pad(rows_near, ((0, 0), (0, 0), (0, 0), (8, 8)))
    pixels = lax.dynamic_slice_in_dim(rows_near, col0, 32, axis=3)
    pixel_keep = cell_mask(frame0 - 1, 8, row0 - 1, 10, col0 - 8, 32)
    pixels = jnp.where(pixel_keep[None, ..., 0], pixels, jnp.zeros_like(pixels))
    pixels = jnp.pad(jnp.transpose(pixels, (1, 0, 2, 3)).reshape(8, 3, 320), ((0, 0), (0, 13), (0, 0)))
    first_terms, second_terms = plain_call(
        backward_kernel,
        (b16(2, 128, 16, 128), b16(2, 128, 16, 128)),
        [
            pltpu.VMEM((1152, 384), half),
            pltpu.VMEM((8, 10, 16, 384), half),
            pltpu.VMEM((8, 10, 32, 128), half),
            pltpu.VMEM((768, 128), half),
            pltpu.VMEM((3464, 128), jnp.float32),
        ],
        pixels, cells, hidden, slope1, slope2, conv_second, rgb,
    )
    return scattered_sums(first_terms, second_terms)


def solution(mesh):
    in_specs = (
        P(None, None, "row", "col", None),
        P(None, None, "col", "row", None),
        P(),
        P(),
        P(),
        P(),
        P(),
        P(),
    )
    out_specs = (P(("grp", "row", "col")), P(("grp", "row", "col")))
    return jax.shard_map(local, mesh=mesh, in_specs=in_specs, out_specs=out_specs, check_vma=False)
```

profile of v0, /device:TPU:32, one launch (start us, length us, event | category | flops | bytes accessed | tf_op | source)
XLA Modules:
  0.0 132.5 jit_solution(8274953779528527336)
XLA Ops:
  0.6 0.0 copy-start.7
  0.6 1.2 fusion.3
  1.9 0.0 copy-done.7
  2.0 0.1 pad_dynamic-slice_fusion.2.own_ref
  2.1 0.7 dynamic-slice_bitcast_fusion.1
  2.8 11.1 %shard_map.95 = (bf16[12,3,16,128]{3,2,1,0:T(8,128)(2,1)S(1)}, bf16[12,3,16,128]{3,2,1,0:T(8,128)(2,1)S(1)}, bf16[8,48,128]{2,1,0:T(8,128)(2,1)S(1)}, bf16[8,48,...) custom-call(bf16[12,8,16,128]{3,2,1,0:T(8,128)(2,1)S(1)} %pad_dynamic-slice_fusion.2.own_, ...), custom_call_target="tpu_custom_call" | custom-call | tf_op jit(solution)/shard_map/pallas_call | solution.py:402
  13.9 0.1 pad_maximum_fusion.2
  14.1 0.1 pad_maximum_fusion
  14.2 0.1 pad_maximum_fusion.1
  14.4 1.0 concatenate.18
  15.4 0.1 broadcast_and_fusion.1
  15.5 0.0 copy-start.12
  15.5 0.0 copy-start.1
  15.5 0.0 copy-start.4
  15.5 0.2 broadcast_select_fusion.cells_ref
  15.7 0.5 copy-done.12
  16.2 0.0 copy-start
  16.2 0.5 copy-done.1
  16.7 0.3 copy-done.4
  17.0 0.0 copy-start.9
  17.0 13.3 %shard_map.96 = (bf16[10,12,32,128]{3,2,1,0:T(8,128)(2,1)S(1)}, f32[10,128,128]{2,1,0:T(8,128)S(1)}, f32[8,10,32,128]{3,2,1,0:T(8,128)S(1)}, bf16[8,16,128]{2,1,0:T(8,128)(2,1)S(1)}) custom-call(bf16[12,14,32,128]{3,2,1,0:T(8,128)(2,1)S(1)} %broadcast_select_fusion.cells_ref, bf16[3456,128]{1,0:T(8,128)(2,1)S(1)} %copy-done.4, ...), custom_call_target="tpu_custom_call" | custom-call | tf_op jit(solution)/shard_map/pallas_call | solution.py:702
  30.3 0.0 copy-done
  30.3 0.0 copy-start.2
  30.3 1.1 copy-done.2
  31.4 0.0 copy-start.5
  31.4 0.8 copy-done.5
  32.2 12.1 %shard_map.97 = bf16[3,8,16,128]{3,2,1,0:T(8,128)(2,1)S(1)} custom-call(bf16[8,16,128]{2,1,0:T(8,128)(2,1)S(1)} %get-tuple-element.19.colour_ref), custom_call_target="tpu_custom_call" | custom-call | tf_op jit(solution)/shard_map/pallas_call | solution.py:402
  44.3 0.0 copy-start.10
  44.3 0.1 reshape.195
  44.5 0.2 reshape.213
  44.7 0.1 maximum_select_fusion
  44.8 0.0 copy-done.9
  44.8 0.3 copy.36
  45.1 0.0 copy-start.11
  45.1 0.1 pad.77
  45.2 0.0 copy-done.10
  45.2 0.1 copy.35
  45.4 0.0 copy-start.8
  45.4 0.6 copy-done.8
  46.0 0.2 copy.47
  46.2 0.1 pad.78.clone
  46.3 1.1 pad_add_fusion.1
  47.4 0.0 copy-done.11
  47.4 0.1 pad_add_fusion.2
  47.6 15.3 %shard_map.98.strip_ref = bf16[32,128]{1,0:T(8,128)(2,1)S(1)} custom-call(f32[24,8,128]{2,1,0:T(8,128)S(1)} %pad_convert_fusion.planes_ref, bf16[72,128]{1,0:T(8,128)(2,1)S(1)} %pad_bitcast_fusion.1.w1_ref, bf16[1152,128]{1,0:T(8,128)(2,1)S(1)} %bitcast.84, bf16[1152,256]{1,0:T(8,128)(2,1)S(1)} %bitcast.82, bf16[1152,128]{1,0:T(8,128)(2,1)S(1)} %bitcast.85, ...), custom_call_target="tpu_custom_call" | custom-call | tf_op jit(solution)/shard_map/pallas_call | solution.py:560
  62.9 0.0 copy-start.6
  62.9 19.1 %shard_map.99 = bf16[8,3,32,128]{3,2,1,0:T(8,128)(2,1)S(1)} custom-call(bf16[32,128]{1,0:T(8,128)(2,1)S(1)} %shard_map.98.strip_ref), custom_call_target="tpu_custom_call" | custom-call | tf_op jit(solution)/shard_map/pallas_call | solution.py:402
  82.2 0.1 broadcast_and_fusion.2
  82.2 0.1 broadcast_and_fusion
  82.3 0.1 fusion.1
  82.5 0.1 reshape.209
  82.6 0.0 copy-done.6
  82.6 0.0 copy-start.3
  82.6 1.3 copy-done.3
  83.9 15.2 %shard_map.100 = (bf16[2,128,16,128]{3,2,1,0:T(8,128)(2,1)S(1)}, bf16[2,128,16,128]{3,2,1,0:T(8,128)(2,1)S(1)}) custom-call(bf16[8,16,320]{2,1,0:T(8,128)(2,1)S(1)} %pad.81.pixel_ref, bf16[12,14,32,128]{3,2,1,0:T(8,128)(2,1)} %copy-done, bf16[10,12,32,128]{3,2,1,0:T(8,128)(2,1)S(1)} %get-tuple-element.21.hidden_ref, f32[10,128,128]{2,1,0:T(8,128)S(1)} %copy-done.6, ...), custom_call_target="tpu_custom_call" | custom-call | tf_op jit(solution)/shard_map/pallas_call | solution.py:702
  99.2 32.6 %shard_map.101 = f32[2,16,128]{2,1,0:T(8,128)S(1)} custom-call(bf16[2,8,4,4,16,128]{5,4,3,2,1,0:T(8,128)(2,1)S(1)} %bitcast.86, bf16[2,8,4,4,16,128]{5,4,3,2,1,0:T(8,128)(2,1)S(1)} %bitcast.87), custom_call_target="tpu_custom_call" | custom-call | tf_op jit(solution)/shard_map/pallas_call | solution.py:116
  131.8 0.7 dynamic-slice_reduce_fusion
  (37 shorter events, 0.6 us)
Async XLA Ops:
  0.6 1.3 copy-start.7
  15.5 0.7 copy-start.12
  15.5 1.2 copy-start.1
  15.5 1.4 %copy-start.4 = (bf16[3456,128]{1,0:T(8,128)(2,1)S(1)}, bf16[3456,128]{1,0:T(8,128)(2,1)}, u32[]{:S(2)}) copy-start(bf16[3456,128]{1,0:T(8,128)(2,1)} %first_ref.1) | copy-start | bytes 2654212
  16.2 14.1 %copy-start = (bf16[12,14,32,128]{3,2,1,0:T(8,128)(2,1)}, bf16[12,14,32,128]{3,2,1,0:T(8,128)(2,1)S(1)}, u32[]{:S(2)}) copy-start(bf16[12,14,32,128]{3,2,1,0:T(8,128)(2,1)S(1)} %broadcast_select_fusion.cells_ref) | copy-start | bytes 4128772
  17.0 27.9 %copy-start.9 = (bf16[576,128]{1,0:T(8,128)(2,1)S(1)}, bf16[576,128]{1,0:T(8,128)(2,1)}, u32[]{:S(2)}) copy-start(bf16[576,128]{1,0:T(8,128)(2,1)} %param.15) | copy-start | bytes 442372
  30.3 1.1 copy-start.2
  31.4 0.8 copy-start.5
  44.3 0.9 copy-start.10
  45.1 2.3 %copy-start.11 = (bf16[27,64]{1,0:T(8,128)(2,1)S(1)}, bf16[27,64]{1,0:T(8,128)(2,1)}, u32[]{:S(2)}) copy-start(bf16[27,64]{1,0:T(8,128)(2,1)} %param.13) | copy-start | bytes 10372
  45.4 0.7 copy-start.8
  62.9 19.7 %copy-start.6 = (f32[10,128,128]{2,1,0:T(8,128)S(1)}, f32[10,128,128]{2,1,0:T(8,128)}, u32[]{:S(2)}) copy-start(f32[10,128,128]{2,1,0:T(8,128)} %copy-done.5) | copy-start | bytes 1966084
  82.6 1.3 copy-start.3
where the time goes:
time: 134 us; the launch traced here: 133 us
  Pallas kernels  119 us (89%)
  local copies, waits for them, and re-layouts  10.4 us (8%)
  other arithmetic  2.26 us (2%)
    pallas_call x3, Pallas kernels, exchange(): pl.pallas_call(kernel, out_shape=outs, in_specs=in_vmem(len(operands)), o...  42.3 us
    pallas_call x1, Pallas kernels, scattered_sums(): pl.pallas_call(reduce_kernel, out_shape=jax.ShapeDtypeStruct((2, 16, 128)...  32.6 us
    pallas_call x2, Pallas kernels, plain_call(): pl.pallas_call(kernel, out_shape=tuple(outs), in_specs=in_vmem(len(operan...  28.5 us
    pallas_call x1, Pallas kernels, perceptual_strip(): pl.pallas_call(perceptual_kernel, out_shape=b16(32, 128), in_specs=in_vme...  15.3 us
    unnamed x30, local copies, waits for them, and re-layouts  5.43 us

commit v1 on v0

v1 whole, which is shorter than its diff:
```python
import functools

import jax
import jax.numpy as jnp
from jax import lax
from jax.experimental import pallas as pl
from jax.experimental.pallas import tpu as pltpu
from jax.sharding import PartitionSpec as P

MESH = pl.DeviceIdType.MESH

gelu_scale = 0.7978845608028654
gelu_cubic = 0.044715


def position():
    return lax.axis_index("grp"), lax.axis_index("row"), lax.axis_index("col")


def same_place(one, other):
    return (one[0] == other[0]) & (one[1] == other[1]) & (one[2] == other[2])


def row_count(r):
    return 1 + jnp.where(r > 0, 1, 0) + jnp.where(r < 7, 1, 0)


def remote(src, dst, sems, slot, peer):
    return pltpu.make_async_remote_copy(
        src_ref=src,
        dst_ref=dst,
        send_sem=sems[0].at[slot],
        recv_sem=sems[1].at[slot],
        device_id=peer,
        device_id_type=MESH,
    )


def halo_kernel(
    own_ref, left_ref, right_ref, guide_ref,
    top_out, bottom_out, left_out, right_out, corner_out, guide_out, send_sem, recv_sem,
):
    g, r, c = position()
    sems = (send_sem, recv_sem)
    west, east = (g, r, lax.rem(c + 7, 8)), (g, r, lax.rem(c + 1, 8))
    has_up, has_down = r > 0, r < 7
    barrier = pltpu.get_barrier_semaphore()

    def greet(row_index):
        for step in (7, 0, 1):
            peer = (g, row_index, lax.rem(c + step, 8))
            pl.semaphore_signal(barrier, inc=1, device_id=peer, device_id_type=MESH)

    for peer in (west, east):
        pl.semaphore_signal(barrier, inc=1, device_id=peer, device_id_type=MESH)
    pl.when(has_up)(lambda: greet(r - 1))
    pl.when(has_down)(lambda: greet(r + 1))
    pl.semaphore_wait(barrier, 3 * row_count(r) - 1)
    sideways = [
        remote(left_ref, right_out, sems, 0, west),
        remote(right_ref, left_out, sems, 1, east),
    ]

    def to_row(row_index, rows, strip_out, corners, guide_slot, first_slot):
        west_peer = (g, row_index, west[2])
        east_peer = (g, row_index, east[2])
        here = (g, row_index, c)
        return [
            remote(own_ref.at[:, rows], strip_out, sems, first_slot, here),
            remote(guide_ref, guide_out.at[guide_slot], sems, first_slot + 1, here),
            remote(left_ref.at[rows], corner_out.at[corners + 1], sems, first_slot + 2, west_peer),
            remote(right_ref.at[rows], corner_out.at[corners], sems, first_slot + 3, east_peer),
        ]

    upward = to_row(r - 1, pl.ds(0, 3), bottom_out, 2, 1, 2)
    downward = to_row(r + 1, pl.ds(5, 3), top_out, 0, 0, 6)

    def start(copies):
        for copy in copies:
            copy.start()

    def sent(copies):
        for copy in copies:
            copy.wait_send()

    def landed(copies):
        for copy in copies:
            copy.wait_recv()

    pl.when(has_up)(lambda: start(upward))
    pl.when(has_down)(lambda: start(downward))
    start(sideways)
    landed(sideways)
    pl.when(has_down)(lambda: landed(upward))
    pl.when(has_up)(lambda: landed(downward))
    sent(sideways)
    pl.when(has_up)(lambda: sent(upward))
    pl.when(has_down)(lambda: sent(downward))


def in_vmem(count):
    return [pl.BlockSpec(memory_space=pltpu.VMEM)] * count


def b16(*shape):
    return jax.ShapeDtypeStruct(shape, jnp.bfloat16)


def exchange(kernel, ident, outs, sems, *operands):
    outs = tuple(outs)
    return pl.pallas_call(
        kernel,
        out_shape=outs,
        in_specs=in_vmem(len(operands)),
        out_specs=tuple(in_vmem(len(outs))),
        scratch_shapes=[pltpu.SemaphoreType.DMA(shape) for shape in sems],
        compiler_params=pltpu.CompilerParams(
            collective_id=ident, has_side_effects=True, vmem_limit_bytes=24 * 2**20
        ),
    )(*operands)


def transposed_dot(one, other):
    return lax.dot_general(one, other, (((0,), (0,)), ((), ())), preferred_element_type=jnp.float32)


def side_by_side(value):
    cols = value.shape[0]
    at = lax.broadcasted_iota(jnp.int32, value.shape, 0)
    before = jnp.where(at == 0, 0.0, pltpu.roll(value, 1, 0))
    after = jnp.where(at == cols - 1, 0.0, pltpu.roll(value, cols - 1, 0))
    return jnp.concatenate([before, value, after], axis=1).astype(jnp.bfloat16)


def three_rows(ref, row, count):
    parts = [ref[pl.ds(row + step, count)].reshape(-1, ref.shape[-1]) for step in range(3)]
    return jnp.concatenate(parts, axis=1)


def dot32(one, other):
    return jnp.dot(one, other, preferred_element_type=jnp.float32)


def gelu_both(preact, slope_too):
    square = preact * preact
    inner_tanh = jnp.tanh(gelu_scale * preact * (1.0 + gelu_cubic * square))
    half = 0.5 * (1.0 + inner_tanh)
    value = preact * half
    if not slope_too:
        return value, None
    bend = (0.5 * gelu_scale) * (1.0 + 3.0 * gelu_cubic * square)
    return value, half + preact * (1.0 - inner_tanh * inner_tanh) * bend


def perceptual_kernel(
    planes_ref, w1_ref, w2_ref, w3_ref, w3_back_ref, w2_back_ref, w1_back_ref, out_ref,
    taps, act1, slope1, pooled, delta3, diff2, slope2, delta2, delta1, tmp, pixels, strip, send_sem, recv_sem, own_sem,
):
    g, r, c = position()
    me = (g, r, c)
    barrier = pltpu.get_barrier_semaphore()
    perceives = g < 3
    own_frame = 8 * g + c
    home = own_frame // 6
    place = lax.rem(own_frame, 6)
    ahead = perceives & (place == 0) & (home > 0)
    behind = perceives & (place == 5) & (home < 3)

    def sources(do):
        for slot in range(8):
            source_frame = 6 * g - 1 + slot

            def each(step, slot=slot, source_frame=source_frame):
                source = (source_frame // 8, r + step, lax.rem(source_frame, 8))
                pl.when(jnp.logical_not(same_place(source, me)))(
                    functools.partial(do, step, slot, source)
                )

            pl.when((source_frame >= 0) & (source_frame < 24))(functools.partial(on_rows, r, each))

    def greet(step, slot, source):
        pl.semaphore_signal(barrier, inc=1, device_id=source, device_id_type=MESH)

    sources(greet)
    row0 = 8 * r - 8
    lane = lax.broadcasted_iota(jnp.int32, (192, 128), 1)
    planes = planes_ref[...].reshape(192, 128)
    before = jnp.where(lane == 0, 0.0, pltpu.roll(planes, 1, 1))
    after = jnp.where(lane == 127, 0.0, pltpu.roll(planes, 127, 1))
    taps[:, 0:8] = before.reshape(24, 8, 128)
    taps[:, 8:16] = planes.reshape(24, 8, 128)
    taps[:, 16:24] = after.reshape(24, 8, 128)

    def shown(row):
        return (row0 + row >= 0) & (row0 + row < 64)

    def kept(row, value):
        return jnp.where(shown(row), value, 0.0)

    def first_rows(low, high, slope_too):
        @pl.loop(low, high)
        def _(i):
            cells = taps[pl.ds(i, 3)].reshape(72, 128).astype(jnp.bfloat16)
            value, slope = gelu_both(transposed_dot(cells, w1_ref[...]), slope_too)
            act1[i] = side_by_side(kept(i + 1, value))
            if slope_too:
                slope1[i - 6] = slope

    first_rows(0, 6, False)
    first_rows(6, 16, True)
    first_rows(16, 22, False)

    def second_rows(low, high, slope_too):
        @pl.loop(low, high)
        def _(p):
            plane = dot32(three_rows(act1, 2 * p, 2), w2_ref[...])
            value, slope = gelu_both(plane, slope_too)
            value = kept(2 * p + 2, value)
            if slope_too:
                difference = 0.25 * (value - pltpu.roll(value, 64, 1))
                diff2[pl.ds(2 * p - 4, 2)] = difference.reshape(2, 128, 128)
                slope2[pl.ds(2 * p - 4, 2)] = slope.reshape(2, 128, 128)
            tmp[...] = value[:128] + value[128:]
            mean = 0.25 * (tmp[pl.ds(0, 64, 2)] + tmp[pl.ds(1, 64, 2)])
            pooled[p] = side_by_side(mean)

    second_rows(0, 2, False)
    second_rows(2, 8, True)
    second_rows(8, 10, False)

    @pl.loop(0, 4)
    def _(half):
        j = 2 * half
        plane = dot32(three_rows(pooled, j, 2), w3_ref[...])
        value, slope = gelu_both(plane[:, :128], True)
        guide, _ = gelu_both(plane[:, 128:], False)
        delta = 0.5 * (value - guide) * slope
        delta3[j] = side_by_side(kept(2 * j + 4, delta[:64]))
        delta3[j + 1] = side_by_side(kept(2 * j + 6, delta[64:]))

    @pl.loop(0, 6)
    def _(m):
        grad = 0.25 * dot32(three_rows(delta3, m, 1), w3_back_ref[...])
        tmp[pl.ds(0, 64, 2)] = grad
        tmp[pl.ds(1, 64, 2)] = grad
        spread = tmp[...]
        for k in range(2):
            delta = (spread + diff2[2 * m + k]) * slope2[2 * m + k]
            delta2[2 * m + k] = side_by_side(kept(2 * m + 6, delta))

    @pl.loop(0, 5)
    def _(half):
        n = 2 * half
        grad = dot32(three_rows(delta2, n, 2), w2_back_ref[...])
        for k in range(2):
            delta = grad[128 * k : 128 * (k + 1)] * slope1[n + k]
            delta1[n + k] = side_by_side(kept(n + k + 7, delta))

    @pl.loop(0, 8)
    def _(q):
        grad = lax.dot_general(
            w1_back_ref[...],
            three_rows(delta1, q, 1),
            (((1,), (1,)), ((), ())),
            preferred_element_type=jnp.float32,
        )
        own = planes_ref[q + 8]
        direct = (1.0 / 6.0) * (own - pltpu.roll(own, 5, 0))
        pixels[pl.ds(pl.multiple_of(q * 8, 8), 8)] = grad + direct

    rows = [pixels[pl.ds(k, 8, 8)] for k in range(3)] + [jnp.zeros((8, 128), jnp.float32)]
    strip[...] = jnp.concatenate(rows, axis=0).astype(jnp.bfloat16)

    groups = jnp.where(perceives, 1, 0) + jnp.where(ahead, 1, 0) + jnp.where(behind, 1, 0)
    to_itself = perceives & (home == g) | ahead & (home == g + 1) | behind & (home == g - 1)
    awaited = 8 * row_count(r) * groups - jnp.where(to_itself, 1, 0)
    pl.when(perceives)(lambda: pl.semaphore_wait(barrier, awaited))

    def targets(do):
        for kind, (group, needed) in enumerate(((home, perceives), (home - 1, ahead), (home + 1, behind))):

            def each(step, kind=kind, group=group):
                for column in range(8):
                    peer = (group, r + step, column)
                    do(kind, step, column, peer, jnp.logical_not(same_place(peer, me)))

            pl.when(needed)(functools.partial(on_rows, r, each))

    def outgoing(kind, step, column, peer):
        place_there = own_frame - 6 * peer[0] + 1
        return pltpu.make_async_remote_copy(
            src_ref=strip,
            dst_ref=out_ref.at[place_there, 1 - step],
            send_sem=send_sem.at[kind, step + 1, column],
            recv_sem=recv_sem.at[place_there, 1 - step],
            device_id=peer,
            device_id_type=MESH,
        )

    def kept():
        return pltpu.make_async_copy(strip, out_ref.at[own_frame - 6 * g + 1, 1], own_sem)

    def start(kind, step, column, peer, away):
        pl.when(away)(lambda: outgoing(kind, step, column, peer).start())
        if step == 0:
            pl.when(jnp.logical_not(away))(lambda: kept().start())

    def finish(kind, step, column, peer, away):
        pl.when(away)(lambda: outgoing(kind, step, column, peer).wait_send())
        if step == 0:
            pl.when(jnp.logical_not(away))(lambda: kept().wait())

    def arrive(step, slot, source):
        pltpu.make_async_remote_copy(
            src_ref=strip,
            dst_ref=out_ref.at[slot, step + 1],
            send_sem=send_sem.at[0, 0, 0],
            recv_sem=recv_sem.at[slot, step + 1],
            device_id=source,
            device_id_type=MESH,
        ).wait_recv()

    targets(start)
    sources(arrive)
    targets(finish)


def two_blocks(weight):
    _, i, o = weight.shape
    return jnp.pad(weight, ((0, 0), (0, i), (0, o))) + jnp.pad(weight, ((0, 0), (i, 0), (o, 0)))


def perceptual_weights(vgg_first, vgg_second, vgg_third):
    first = vgg_first.reshape(9, 3, 64)
    w1 = jnp.pad(two_blocks(first), ((0, 0), (0, 2), (0, 0))).reshape(72, 128)
    second = vgg_second.reshape(9, 64, 64)
    third = vgg_third.reshape(9, 64, 128)
    w2 = two_blocks(second).reshape(1152, 128)
    w3 = two_blocks(third).reshape(1152, 256)
    w3_back = jnp.pad(jnp.transpose(third[::-1], (0, 2, 1)), ((0, 0), (0, 0), (0, 64))).reshape(1152, 128)
    w2_back = jnp.pad(jnp.transpose(second[::-1], (0, 2, 1)), ((0, 0), (0, 64), (0, 64))).reshape(1152, 128)
    w1_back = jnp.pad(jnp.transpose(first[::-1], (1, 0, 2)), ((0, 5), (0, 0), (0, 64))).reshape(8, 1152)
    return w1, w2, w3, w3_back, w2_back, w1_back


def perceptual_strip(planes, weights):
    f32, half = jnp.float32, jnp.bfloat16
    return pl.pallas_call(
        perceptual_kernel,
        out_shape=b16(8, 3, 32, 128),
        in_specs=in_vmem(7),
        out_specs=in_vmem(1)[0],
        scratch_shapes=[
            pltpu.VMEM((24, 24, 128), f32),
            pltpu.VMEM((22, 128, 384), half),
            pltpu.VMEM((10, 128, 128), f32),
            pltpu.VMEM((10, 64, 384), half),
            pltpu.VMEM((8, 64, 384), half),
            pltpu.VMEM((12, 128, 128), f32),
            pltpu.VMEM((12, 128, 128), f32),
            pltpu.VMEM((12, 128, 384), half),
            pltpu.VMEM((10, 128, 384), half),
            pltpu.VMEM((128, 128), f32),
            pltpu.VMEM((64, 128), f32),
            pltpu.VMEM((32, 128), half),
            pltpu.SemaphoreType.DMA((3, 3, 8)),
            pltpu.SemaphoreType.DMA((8, 3)),
            pltpu.SemaphoreType.DMA(()),
        ],
        compiler_params=pltpu.CompilerParams(
            collective_id=4, has_side_effects=True, vmem_limit_bytes=40 * 2**20
        ),
    )(planes, *weights)


def taps_in_lanes(weight_ref, out_ref):
    for q in range(9):
        for k in range(3):
            tap = 3 * q + k
            out_ref[128 * q : 128 * (q + 1), 128 * k : 128 * (k + 1)] = weight_ref[
                128 * tap : 128 * (tap + 1), :
            ]


def turned_taps(weight_ref, out_ref):
    for q in range(9):
        for k in range(3):
            tap = 26 - 3 * q - k
            block = weight_ref[128 * tap : 128 * (tap + 1), :].astype(jnp.float32)
            out_ref[128 * q : 128 * (q + 1), 128 * k : 128 * (k + 1)] = block.T.astype(jnp.bfloat16)


def conv_frame(source, frame, rows, taps_ref):
    parts = [
        source[frame + dt, pl.ds(dr, rows)].reshape(rows * 32, 128) for dt in range(3) for dr in range(3)
    ]
    sums = dot32(jnp.concatenate(parts, axis=1), taps_ref[...])
    total = pltpu.roll(sums[:, :128], 1, 0) + sums[:, 128:256]
    total += pltpu.roll(sums[:, 256:], rows * 32 - 1, 0)
    return total.reshape(rows, 32, 128)


def silu_parts(preact):
    gate = 1.0 / (1.0 + jnp.exp(-preact))
    return preact * gate, gate * (1.0 + preact * (1.0 - gate))


def on_rows(r, do):
    for step in (-1, 0, 1):
        pl.when((r + step >= 0) & (r + step < 8))(functools.partial(do, step))


def forward_kernel(
    cells_ref, first_ref, second_ref, rgb_ref, hidden_out, slope1_out, slope2_out, near_out,
    taps1, taps2, colours, send_sem, recv_sem, own_sem,
):
    g, r, c = position()
    me = (g, r, c)
    barrier = pltpu.get_barrier_semaphore()
    perceives = g < 3
    source_group = (8 * g + c) // 6

    def sources(do):
        def each(step):
            for column in range(8):
                source = (source_group, r + step, column)
                pl.when(jnp.logical_not(same_place(source, me)))(
                    functools.partial(do, step, column, source)
                )

        pl.when(perceives)(lambda: on_rows(r, each))

    def greet(step, column, source):
        pl.semaphore_signal(barrier, inc=1, device_id=source, device_id_type=MESH)

    sources(greet)

    taps_in_lanes(first_ref, taps1)
    taps_in_lanes(second_ref, taps2)
    row = lax.broadcasted_iota(jnp.int32, (12, 32, 128), 0) + (8 * r - 2)
    col = lax.broadcasted_iota(jnp.int32, (12, 32, 128), 1) + (16 * c - 8)
    shown = (row >= 0) & (row < 64) & (col >= 0) & (col < 128)

    @pl.loop(0, 10)
    def _(f):
        value, slope = silu_parts(conv_frame(cells_ref, f, 12, taps1))
        frame = 6 * g - 2 + f
        value = jnp.where(shown, value, 0.0) * jnp.where((frame >= 0) & (frame < 24), 1.0, 0.0)
        hidden_out[f] = value.astype(jnp.bfloat16)
        slope1_out[f] = slope[2:10, 8:24].reshape(128, 128)

    to_itself = jnp.where(perceives & (2 * g + c < 6), 1, 0)
    pl.semaphore_wait(barrier, 6 * row_count(r) - to_itself)

    def target(step, slot):
        frame = 6 * g + slot
        return (frame // 8, r + step, lax.rem(frame, 8))

    def outgoing(step, slot):
        return pltpu.make_async_remote_copy(
            src_ref=colours.at[slot],
            dst_ref=near_out.at[1 - step, c],
            send_sem=send_sem.at[step + 1, slot],
            recv_sem=recv_sem.at[1 - step, c],
            device_id=target(step, slot),
            device_id_type=MESH,
        )

    def kept(slot):
        return pltpu.make_async_copy(colours.at[slot], near_out.at[1, c], own_sem)

    def start(slot, step):
        away = jnp.logical_not(same_place(target(step, slot), me))
        pl.when(away)(lambda: outgoing(step, slot).start())
        if step == 0:
            pl.when(jnp.logical_not(away))(lambda: kept(slot).start())

    def finish(slot, step):
        away = jnp.logical_not(same_place(target(step, slot), me))
        pl.when(away)(lambda: outgoing(step, slot).wait_send())
        if step == 0:
            pl.when(jnp.logical_not(away))(lambda: kept(slot).wait())

    def arrive(step, column, source):
        pltpu.make_async_remote_copy(
            src_ref=colours.at[0],
            dst_ref=near_out.at[step + 1, column],
            send_sem=send_sem.at[0, 0],
            recv_sem=recv_sem.at[step + 1, column],
            device_id=source,
            device_id_type=MESH,
        ).wait_recv()

    @pl.loop(0, 6)
    def _(slot):
        value, slope = silu_parts(conv_frame(hidden_out, slot + 1, 10, taps2))
        slope2_out[slot + 1] = slope
        own = value[1:9, 8:24].reshape(128, 128).astype(jnp.bfloat16)
        colour = lax.dot_general(
            rgb_ref[...], own, (((1,), (1,)), ((), ())), preferred_element_type=jnp.float32
        )
        colours[slot] = colour.astype(jnp.bfloat16)
        on_rows(r, functools.partial(start, slot))

    @pl.loop(0, 2)
    def _(end):
        slope2_out[7 * end] = silu_parts(conv_frame(hidden_out, 7 * end, 10, taps2))[1]

    sources(arrive)

    @pl.loop(0, 6)
    def _(slot):
        on_rows(r, functools.partial(finish, slot))


def columns_in_lanes(source, frame0, row0, out_ref):
    @pl.loop(0, 8)
    def _(f):
        value = source[f + frame0, pl.ds(row0, 10)].reshape(320, 128).astype(jnp.float32)
        parts = [pltpu.roll(value, 1, 0), value, pltpu.roll(value, 319, 0)]
        for k, part in enumerate(parts):
            own = part.reshape(10, 32, 128)[:, 8:24]
            out_ref[f, :, :, 128 * k : 128 * (k + 1)] = own.astype(jnp.bfloat16)


def weight_terms(columns, delta, terms):
    @pl.loop(0, 9)
    def _(q):
        cells = columns[pl.ds(q // 3, 6), pl.ds(lax.rem(q, 3), 8)].reshape(768, 384)
        terms[pl.ds(pl.multiple_of(384 * q, 384), 384)] = transposed_dot(cells, delta[...])


def by_chip(terms, out_ref, which):
    @pl.loop(0, 8)
    def _(z):
        for chip in range(16):
            start = 432 * z + 27 * chip
            out_ref[which, 0, z, chip // 4, chip % 4] = terms[pl.ds(start, 16)].astype(jnp.bfloat16)
            out_ref[which, 1, z, chip // 4, chip % 4] = terms[pl.ds(start + 13, 16)].astype(jnp.bfloat16)


def backward_kernel(
    pixel_ref, cells_ref, hidden_ref, slope1_ref, slope2_ref, second_ref, rgb_ref, out_ref,
    taps, columns, field, delta, terms,
    sending, core_in, held, x_in, y_in, mid_x, mid_y, yy_in, xx_in, last, z_in, send_sem, recv_sem,
):
    g, r, c = position()
    zh, x, y, core = r // 4, lax.rem(r, 4), c // 2, lax.rem(c, 2)
    z = g * 2 + zh
    other = 1 - core

    def at_x(step):
        return (g, zh * 4 + lax.rem(x + step, 4), c)

    def at_y(step):
        return (g, r, lax.rem(y + step, 4) * 2 + core)

    def at_z(step):
        to = lax.rem(z + step, 8)
        return (to // 2, lax.rem(to, 2) * 4 + x, c)

    partner = (g, r, y * 2 + other)
    barrier = pltpu.get_barrier_semaphore()
    everyone = [partner] + [at_x(s) for s in (1, 2, 3)] + [at_y(s) for s in (1, 2, 3)]
    everyone += [at_z(s) for s in range(1, 8)]
    for peer in everyone:
        pl.semaphore_signal(barrier, inc=1, device_id=peer, device_id_type=MESH)

    def send(src, dst, which, slot, peer):
        copy = pltpu.make_async_remote_copy(
            src_ref=src,
            dst_ref=dst,
            send_sem=send_sem.at[which, slot],
            recv_sem=recv_sem.at[which, slot],
            device_id=peer,
            device_id_type=MESH,
        )
        copy.start()
        return copy

    f32, half = jnp.float32, jnp.bfloat16

    def summed(own, received):
        total = own.astype(f32)
        for k in range(3):
            total += received[k].astype(f32)
        return total.astype(half)

    def to_partner(which):
        return send(sending.at[which, other], core_in.at[which], which, 0, partner)

    def first_step(which, copy):
        copy.wait()

        @pl.loop(0, 8)
        def _(k):
            pair = sending[which, core, k].astype(f32) + core_in[which, k].astype(f32)
            held[which, k] = pair.astype(half)

        low, high = held.at[which, pl.ds(0, 4)], held.at[which, pl.ds(4, 4)]
        copies = []
        for s in (1, 2, 3):
            copies.append(send(low.at[:, lax.rem(x + s, 4)], x_in.at[which, s - 1], which, s, at_x(s)))
            copies.append(send(high.at[:, :, lax.rem(y + s, 4)], y_in.at[which, s - 1], which, 3 + s, at_y(s)))
        return copies

    def second_step(which, copies):
        for copy in copies:
            copy.wait()
        mid_x[which] = summed(held[which, 0:4, x], [x_in[which, k] for k in range(3)])
        mid_y[which] = summed(held[which, 4:8, :, y], [y_in[which, k] for k in range(3)])
        after = []
        for s in (1, 2, 3):
            after.append(send(mid_x.at[which, :, lax.rem(y + s, 4)], yy_in.at[which, s - 1], which, 6 + s, at_y(s)))
            after.append(send(mid_y.at[which, :, lax.rem(x + s, 4)], xx_in.at[which, s - 1], which, 9 + s, at_x(s)))
        return after

    def third_step(which, copies):
        for copy in copies:
            copy.wait()
        last[which, 0:4] = summed(mid_x[which, :, y], [yy_in[which, k] for k in range(3)])
        last[which, 4:8] = summed(mid_y[which, :, x], [xx_in[which, k] for k in range(3)])
        return [
            send(last.at[which, lax.rem(z + s, 8)], z_in.at[which, s - 1], which, 12 + s, at_z(s))
            for s in range(1, 8)
        ]

    def result(which, copies):
        for copy in copies:
            copy.wait()
        total = last[which, z].astype(f32)
        for k in range(7):
            total += z_in[which, k].astype(f32)
        out_ref[which] = total

    turned_taps(second_ref, taps)

    @pl.loop(0, 8)
    def _(f):
        hidden_grad = transposed_dot(pixel_ref[f], rgb_ref[...])
        value = hidden_grad.reshape(10, 32, 128) * slope2_ref[f]
        field[f] = value.astype(half)

    @pl.loop(0, 6)
    def _(f):
        own = field[f + 1, 1:9].astype(f32)[:, 8:24].reshape(128, 128).astype(half)
        delta[pl.ds(pl.multiple_of(128 * f, 128), 128)] = own

    columns_in_lanes(hidden_ref, 1, 1, columns)
    terms[pl.ds(3456, 8)] = jnp.zeros((8, 128), f32)
    weight_terms(columns, delta, terms)
    by_chip(terms, sending, 1)
    pl.semaphore_wait(barrier, len(everyone))
    swap_second = to_partner(1)

    @pl.loop(0, 6)
    def _(f):
        back = conv_frame(field, f, 8, taps)[:, 8:24].reshape(128, 128)
        value = (back * slope1_ref[f + 2]).astype(half)
        delta[pl.ds(pl.multiple_of(128 * f, 128), 128)] = value

    moves_second = first_step(1, swap_second)
    columns_in_lanes(cells_ref, 2, 2, columns)
    weight_terms(columns, delta, terms)
    moves_second = second_step(1, moves_second)
    by_chip(terms, sending, 0)
    swap_first = to_partner(0)
    moves_second = third_step(1, moves_second)
    moves_first = first_step(0, swap_first)
    result(1, moves_second)
    moves_first = second_step(0, moves_first)
    moves_first = third_step(0, moves_first)
    result(0, moves_first)


def f32_shape(*shape):
    return jax.ShapeDtypeStruct(shape, jnp.float32)


def talking_call(kernel, ident, outs, scratch, *operands):
    return pl.pallas_call(
        kernel,
        out_shape=tuple(outs),
        in_specs=in_vmem(len(operands)),
        out_specs=tuple(in_vmem(len(outs))),
        scratch_shapes=scratch,
        compiler_params=pltpu.CompilerParams(
            collective_id=ident, has_side_effects=True, vmem_limit_bytes=48 * 2**20
        ),
    )(*operands)


def inside(start, count, limit):
    positions = start + jnp.arange(count)
    return (positions >= 0) & (positions < limit)


def cell_mask(frame0, frames, row0, rows, col0, cols):
    keep_frames = inside(frame0, frames, 24)
    keep_rows = inside(row0, rows, 64)
    keep_cols = inside(col0, cols, 128)
    return (keep_frames[:, None, None] & keep_rows[None, :, None] & keep_cols[None, None, :])[
        ..., None
    ]


def local(dec_input, target, conv_first, conv_second, rgb_weight, vgg_first, vgg_second, vgg_third):
    g, r, c = position()
    channels = dec_input.shape[-1]
    frame0, row0, col0 = 6 * g, 8 * r, 16 * c
    video = jnp.pad(dec_input.reshape(24, 8, 16, channels), ((3, 3), (0, 0), (0, 0), (0, 0)))
    own = lax.dynamic_slice_in_dim(video, frame0, 12, axis=0)

    def columns(part):
        return jnp.transpose(part, (1, 0, 2, 3)).reshape(8, 48, channels)

    guide_own = lax.dynamic_index_in_dim(target, jnp.minimum(g, 2), 1, keepdims=False)
    guide_own = guide_own.reshape(24, 128)
    top, bottom, left, right, corners, guide_near = exchange(
        halo_kernel,
        2,
        (
            b16(12, 3, 16, channels), b16(12, 3, 16, channels), b16(8, 48, channels),
            b16(8, 48, channels), b16(4, 3, 48, channels), b16(2, 32, 128),
        ),
        ((10,), (10,)),
        own,
        columns(own[:, :, :4]),
        columns(own[:, :, 12:]),
        jnp.pad(guide_own, ((0, 8), (0, 0))),
    )

    def strip(part):
        return jnp.transpose(part.reshape(-1, 12, 4, channels), (1, 0, 2, 3))

    gap = jnp.zeros((12, 14, 4, channels), jnp.bfloat16)
    cells = jnp.concatenate(
        [
            gap,
            jnp.concatenate([strip(corners[0]), strip(left), strip(corners[2])], axis=1),
            jnp.concatenate([top, own, bottom], axis=1),
            jnp.concatenate([strip(corners[1]), strip(right), strip(corners[3])], axis=1),
            gap,
        ],
        axis=2,
    )
    cells = jnp.where(
        inside(row0 - 3, 14, 64)[None, :, None, None] & inside(col0 - 8, 32, 128)[None, None, :, None],
        cells,
        jnp.zeros_like(cells),
    )
    half = jnp.bfloat16
    rgb = jnp.pad(rgb_weight, ((0, 13), (0, 0)))
    dma = pltpu.SemaphoreType.DMA
    hidden, slope1, slope2, colour_near = talking_call(
        forward_kernel,
        3,
        (b16(10, 12, 32, 128), f32_shape(10, 128, 128), f32_shape(8, 10, 32, 128), b16(3, 8, 16, 128)),
        [
            pltpu.VMEM((1152, 384), half), pltpu.VMEM((1152, 384), half), pltpu.VMEM((6, 16, 128), half),
            dma((3, 6)), dma((3, 8)), dma(()),
        ],
        cells, conv_first, conv_second, rgb,
    )
    images = jnp.transpose(colour_near[:, :, :3].reshape(3, 8, 3, 8, 16), (0, 3, 2, 1, 4))
    guides = jnp.stack(
        [guide_near[0, :24].reshape(3, 8, 128), guide_own.reshape(3, 8, 128), guide_near[1, :24].reshape(3, 8, 128)]
    )
    guides = jnp.transpose(guides, (0, 2, 1, 3))
    planes = jnp.concatenate([images.reshape(24, 3, 128), guides.reshape(24, 3, 128)], axis=1)
    planes = jnp.where(inside(row0 - 8, 24, 64)[:, None, None], planes, jnp.zeros_like(planes))
    planes = jnp.pad(planes.astype(jnp.float32), ((0, 0), (0, 2), (0, 0)))
    returned = perceptual_strip(planes, perceptual_weights(vgg_first, vgg_second, vgg_third))
    rows_near = jnp.transpose(returned[:, :, :24].reshape(8, 3, 3, 8, 128), (2, 0, 1, 3, 4))
    rows_near = rows_near.reshape(3, 8, 24, 128)[:, :, 7:17]
    rows_near = jnp.pad(rows_near, ((0, 0), (0, 0), (0, 0), (8, 8)))
    pixels = lax.dynamic_slice_in_dim(rows_near, col0, 32, axis=3)
    pixel_keep = cell_mask(frame0 - 1, 8, row0 - 1, 10, col0 - 8, 32)
    pixels = jnp.where(pixel_keep[None, ..., 0], pixels, jnp.zeros_like(pixels))
    pixels = jnp.pad(jnp.transpose(pixels, (1, 0, 2, 3)).reshape(8, 3, 320), ((0, 0), (0, 13), (0, 0)))
    sums = talking_call(
        backward_kernel,
        1,
        (f32_shape(2, 16, 128),),
        [
            pltpu.VMEM((1152, 384), half),
            pltpu.VMEM((8, 10, 16, 384), half),
            pltpu.VMEM((8, 10, 32, 128), half),
            pltpu.VMEM((768, 128), half),
            pltpu.VMEM((3464, 128), jnp.float32),
            pltpu.VMEM((2, 2, 8, 4, 4, 16, 128), half),
            pltpu.VMEM((2, 8, 4, 4, 16, 128), half),
            pltpu.VMEM((2, 8, 4, 4, 16, 128), half),
            pltpu.VMEM((2, 3, 4, 4, 16, 128), half),
            pltpu.VMEM((2, 3, 4, 4, 16, 128), half),
            pltpu.VMEM((2, 4, 4, 16, 128), half),
            pltpu.VMEM((2, 4, 4, 16, 128), half),
            pltpu.VMEM((2, 3, 4, 16, 128), half),
            pltpu.VMEM((2, 3, 4, 16, 128), half),
            pltpu.VMEM((2, 8, 16, 128), half),
            pltpu.VMEM((2, 7, 16, 128), half),
            dma((2, 20)),
            dma((2, 20)),
        ],
        pixels, cells, hidden, slope1, slope2, conv_second, rgb,
    )[0]
    flat = sums[:, :14].reshape(2, 14 * 128)
    own_sums = lax.dynamic_slice_in_dim(flat, lax.rem(c, 2) * 64, 1728, axis=1)
    return own_sums[0], own_sums[1]


def solution(mesh):
    in_specs = (
        P(None, None, "row", "col", None),
        P(None, None, "col", "row", None),
        P(),
        P(),
        P(),
        P(),
        P(),
        P(),
    )
    out_specs = (P(("grp", "row", "col")), P(("grp", "row", "col")))
    return jax.shard_map(local, mesh=mesh, in_specs=in_specs, out_specs=out_specs, check_vma=False)
```

time: 134 us -> 125 us (0.933)
  Pallas kernels: 119 us -> 99.8 us
  local copies, waits for them, and re-layouts: 10.4 us -> 17.1 us
  other arithmetic: 2.26 us -> 6.2 us
    pallas_call x3 -> x1, Pallas kernels: 42.3 us -> 11.1 us  [exchange(): pl.pallas_call(kernel, out_shape=outs, in_specs=in_vmem(len(operands)), o...]
    pallas_call x4 -> x3, Pallas kernels: 76.5 us -> 88.8 us  [the longest x2 61.4 us: talking_call(): pl.pallas_call(kernel, out_shape=tuple(outs), in_specs=in_vmem(len(operan...]
    concatenate x1, local copies, waits for them, and re-layouts: 0.96 us -> 5.04 us  [local(): jnp.concatenate([gap, jnp.concatenate([strip(corners[0]), strip(left), st...]
    unnamed x30 -> x34, local copies, waits for them, and re-layouts: 5.43 us -> 7.37 us
    add x3, other arithmetic: 1.23 us -> 2.95 us  [two_blocks(): jnp.pad(weight, ((0, 0), (0, i), (0, o)))]
    select_n x1, other arithmetic: 0.19 us -> 1.65 us  [local(): jnp.where(inside(row0 - 3, 14, 64)[None, :, None, None] & inside(col0 - 8...]
where the time goes in v1:
time: 125 us; the launch traced here: 124 us
  Pallas kernels  99.8 us (80%)
  local copies, waits for them, and re-layouts  17.1 us (14%)
  other arithmetic  6.2 us (5%)
    pallas_call x2, Pallas kernels, talking_call(): pl.pallas_call(kernel, out_shape=tuple(outs), in_specs=in_vmem(len(operan...  61.4 us
    pallas_call x1, Pallas kernels, perceptual_strip(): pl.pallas_call(perceptual_kernel, out_shape=b16(8, 3, 32, 128), in_specs=...  27.4 us
    pallas_call x1, Pallas kernels, exchange(): pl.pallas_call(kernel, out_shape=outs, in_specs=in_vmem(len(operands)), o...  11.1 us
    unnamed x34, local copies, waits for them, and re-layouts  7.37 us
    concatenate x1, local copies, waits for them, and re-layouts, local(): jnp.concatenate([gap, jnp.concatenate([strip(corners[0]), strip(left), st...  5.04 us
    add x3, other arithmetic, two_blocks(): jnp.pad(weight, ((0, 0), (0, i), (0, o)))  2.95 us

profile of v1, /device:TPU:32, one launch (start us, length us, event | category | flops | bytes accessed | tf_op | source)
XLA Modules:
  0.0 124.3 jit_solution(6869374744627988839)
XLA Ops:
  0.6 0.0 copy-start.9
  0.6 1.2 fusion.3
  1.9 0.0 copy-done.9
  2.0 0.1 pad_dynamic-slice_fusion.2.own_ref
  2.1 0.7 dynamic-slice_bitcast_fusion.1
  2.8 11.1 %shard_map.95 = (bf16[12,3,16,128]{3,2,1,0:T(8,128)(2,1)S(1)}, bf16[12,3,16,128]{3,2,1,0:T(8,128)(2,1)S(1)}, bf16[8,48,128]{2,1,0:T(8,128)(2,1)S(1)}, bf16[8,48,...) custom-call(bf16[12,8,16,128]{3,2,1,0:T(8,128)(2,1)S(1)} %pad_dynamic-slice_fusion.2.own_, ...), custom_call_target="tpu_custom_call" | custom-call | tf_op jit(solution)/shard_map/pallas_call | solution.py:111
  13.9 0.1 pad_maximum_fusion.2
  14.1 0.1 pad_maximum_fusion
  14.2 0.1 pad_maximum_fusion.1
  14.4 5.0 %concatenate.18 = bf16[12,14,32,128]{3,2,1,0:T(8,128)(2,1)} concatenate(bf16[12,14,4,128]{3,2,1,0:T(4,128)(2,1)S(1)} %broadcast_in_dim.45, bf16[12,14,4,128]{3,2,1,0:T(4,128)(2,1)S(1)} %pad_maximum_fusion.1, bf16[12,14,16,128]{3,2,1,0:T(8,128)(2,1)S(1)} %pad_maximum_fusion, bf16[12,14,4,128]{3,2,1,0:T(4,128)(2,1)S(1)} %pad_maximum_fusion.2, ...), dimensions={2} | concatenate | bytes 2752512 | tf_op jit(solution)/shard_map/concatenate | solution.py:737
  19.5 0.0 copy-start.13
  19.5 0.1 broadcast_and_fusion.1
  19.6 0.0 copy-start.14
  19.6 0.0 copy-start
  19.6 0.0 copy-start.6
  19.6 1.7 %broadcast_select_fusion.cells_ref = bf16[12,14,32,128]{3,2,1,0:T(8,128)(2,1)S(1)} fusion(bf16[12,14,32,128]{3,2,1,0:T(8,128)(2,1)} %concatenate.18, pred[14,32]{1,0:T(8,128)(4,1)S(1)} %broadcast_and_fusion.1), kind=kLoop, calls=%fused_computation | loop fusion | flops 688128 | bytes 2752960 | tf_op jit(solution)/shard_map/jit(_where)/select_n | solution.py:747
  21.2 0.0 copy-done.13
  21.2 0.0 copy-done.14
  21.3 0.0 copy-done
  21.3 0.2 copy-done.6
  21.4 0.0 copy-start.11
  21.4 14.5 %shard_map.96 = (bf16[10,12,32,128]{3,2,1,0:T(8,128)(2,1)S(1)}, f32[10,128,128]{2,1,0:T(8,128)S(1)}, f32[8,10,32,128]{3,2,1,0:T(8,128)S(1)}, bf16[3,8,16,128]{3,2,1,0:T(8,128)(2,1)S(1)}) custom-call(bf16[12,14,32,128]{3,2,1,0:T(8,128)(2,1)S(1)} %broadcast_select_fusion.cells_ref, bf16[3456,128]{1,0:T(8,128)(2,1)S(1)} %copy-done.6, ...), custom_call_target="tpu_custom_call" | custom-call | tf_op jit(solution)/shard_map/pallas_call | solution.py:681
  35.9 0.0 copy-start.1
  35.9 1.1 copy-done.1
  37.0 0.0 copy-start.4
  37.0 0.9 copy-done.4
  37.9 0.0 copy-start.7
  37.9 0.8 copy-done.7
  38.8 0.0 copy-start.12
  38.8 0.1 reshape.189
  39.0 0.2 reshape.205
  39.2 0.1 maximum_select_fusion
  39.3 0.0 copy-done.11
  39.3 0.3 copy.36
  39.6 0.1 pad.77
  39.7 0.0 copy-done.12
  39.7 0.1 copy.35
  39.9 0.0 copy-start.10
  39.9 0.6 copy-done.10
  40.5 0.2 copy.47
  40.7 0.1 pad.78.clone
  40.8 1.0 pad_add_fusion
  41.8 1.8 %pad_add_fusion.1 = bf16[9,128,128]{2,1,0:T(8,128)(2,1)} fusion(bf16[9,64,64]{2,1,0:T(8,128)(2,1)} %bitcast.89), kind=kLoop, calls=%fused_computation.7 | loop fusion | flops 589824 | bytes 368640 | tf_op jit(solution)/shard_map/add | solution.py:330
  43.6 0.7 reshape.192
  44.3 0.1 pad_add_fusion.2
  44.5 0.0 copy-start.3
  44.5 1.0 copy-done.3
  45.4 27.4 %shard_map.97 = bf16[8,3,32,128]{3,2,1,0:T(8,128)(2,1)S(1)} custom-call(f32[24,8,128]{2,1,0:T(8,128)S(1)} %pad_convert_fusion.planes_ref, bf16[72,128]{1,0:T(8,128)(2,1)S(1)} %pad_bitcast_fusion.1.w1_ref, bf16[1152,128]{1,0:T(8,128)(2,1)S(1)} %bitcast.83, bf16[1152,256]{1,0:T(8,128)(2,1)S(1)} %bitcast.80, bf16[1152,128]{1,0:T(8,128)(2,1)S(1)} %bitcast.81, ...), custom_call_target="tpu_custom_call" | custom-call | tf_op jit(solution)/shard_map/pallas_call | solution.py:348
  72.9 0.0 copy-start.5
  73.0 0.1 broadcast_and_fusion.2
  73.1 0.8 broadcast_and_fusion
  73.9 0.1 fusion.1
  74.0 0.1 reshape.203
  74.2 0.0 copy-done.5
  74.2 0.0 copy-start.2
  74.2 1.3 %copy-done.2 = f32[8,10,32,128]{3,2,1,0:T(8,128)S(1)} copy-done((f32[8,10,32,128]{3,2,1,0:T(8,128)S(1)}, f32[8,10,32,128]{3,2,1,0:T(8,128)}, u32[]{:S(2)}) %copy-start.2) | copy-done | bytes 1310744
  75.5 0.0 copy-start.8
  75.5 1.1 copy-done.8
  76.6 46.9 %shard_map.98 = f32[2,16,128]{2,1,0:T(8,128)S(1)} custom-call(bf16[8,16,320]{2,1,0:T(8,128)(2,1)S(1)} %pad.81.pixel_ref, bf16[12,14,32,128]{3,2,1,0:T(8,128)(2,1)S(1)} %broadcast_select_fusion.cells_ref, bf16[10,12,32,128]{3,2,1,0:T(8,128)(2,1)S(1)} %copy-done.5, f32[10,128,128]{2,1,0:T(8,128)S(1)} %copy-done.8, f32[8,10,32,128]{3,2,1,0:T(8,128)S(1)} %copy-done.2, ...), custom_call_target="tpu_custom_call" | custom-call | tf_op jit(solution)/shard_map/pallas_call | solution.py:681
  123.6 0.7 dynamic-slice_reduce_fusion
  (35 shorter events, 0.5 us)
Async XLA Ops:
  0.6 1.3 %copy-start.9 = (bf16[3,8,8,16,128]{4,3,2,1,0:T(8,128)(2,1)S(1)}, bf16[3,8,8,16,128]{4,3,2,1,0:T(8,128)(2,1)}, u32[]{:S(2)}) copy-start(bf16[3,8,8,16,128]{4,3,2,1,0:T(8,128)(2,1)} %param.8) | copy-start | bytes 2359300
  19.5 1.8 %copy-start.13 = (pred[32]{0:T(512)(128)(4,1)}, pred[32]{0:T(512)(128)(4,1)S(1)}, u32[]{:S(2)}) copy-start(pred[32]{0:T(512)(128)(4,1)S(1)} %compare_and_fusion.2) | copy-start | bytes 100
  19.6 1.7 %copy-start.14 = (bf16[3,128]{1,0:T(4,128)(2,1)S(1)}, bf16[3,128]{1,0:T(4,128)(2,1)}, u32[]{:S(2)}) copy-start(bf16[3,128]{1,0:T(4,128)(2,1)} %param.12) | copy-start | bytes 2308
  19.6 1.7 %copy-start = (bf16[3456,128]{1,0:T(8,128)(2,1)S(1)}, bf16[3456,128]{1,0:T(8,128)(2,1)}, u32[]{:S(2)}) copy-start(bf16[3456,128]{1,0:T(8,128)(2,1)} %second_ref.3) | copy-start | bytes 2654212
  19.6 1.9 %copy-start.6 = (bf16[3456,128]{1,0:T(8,128)(2,1)S(1)}, bf16[3456,128]{1,0:T(8,128)(2,1)}, u32[]{:S(2)}) copy-start(bf16[3456,128]{1,0:T(8,128)(2,1)} %first_ref.1) | copy-start | bytes 2654212
  21.4 17.9 %copy-start.11 = (bf16[576,128]{1,0:T(8,128)(2,1)S(1)}, bf16[576,128]{1,0:T(8,128)(2,1)}, u32[]{:S(2)}) copy-start(bf16[576,128]{1,0:T(8,128)(2,1)} %param.15) | copy-start | bytes 442372
  35.9 1.1 copy-start.1
  37.0 0.9 copy-start.4
  37.9 0.8 copy-start.7
  38.8 0.9 copy-start.12
  39.9 0.7 copy-start.10
  44.5 1.0 copy-start.3
  72.9 1.3 %copy-start.5 = (bf16[10,12,32,128]{3,2,1,0:T(8,128)(2,1)S(1)}, bf16[10,12,32,128]{3,2,1,0:T(8,128)(2,1)}, u32[]{:S(2)}) copy-start(bf16[10,12,32,128]{3,2,1,0:T(8,128)(2,1)} %copy-done.4) | copy-start | bytes 2949124
  74.2 1.3 %copy-start.2 = (f32[8,10,32,128]{3,2,1,0:T(8,128)S(1)}, f32[8,10,32,128]{3,2,1,0:T(8,128)}, u32[]{:S(2)}) copy-start(f32[8,10,32,128]{3,2,1,0:T(8,128)} %copy-done.1) | copy-start | bytes 3932164
  75.5 1.1 copy-start.8

commit v2 on v1

--- a/solution.py
+++ b/solution.py
@@ -25,99 +25,12 @@
     return 1 + jnp.where(r > 0, 1, 0) + jnp.where(r < 7, 1, 0)
 
 
-def remote(src, dst, sems, slot, peer):
-    return pltpu.make_async_remote_copy(
-        src_ref=src,
-        dst_ref=dst,
-        send_sem=sems[0].at[slot],
-        recv_sem=sems[1].at[slot],
-        device_id=peer,
-        device_id_type=MESH,
-    )
-
-
-def halo_kernel(
-    own_ref, left_ref, right_ref, guide_ref,
-    top_out, bottom_out, left_out, right_out, corner_out, guide_out, send_sem, recv_sem,
-):
-    g, r, c = position()
-    sems = (send_sem, recv_sem)
-    west, east = (g, r, lax.rem(c + 7, 8)), (g, r, lax.rem(c + 1, 8))
-    has_up, has_down = r > 0, r < 7
-    barrier = pltpu.get_barrier_semaphore()
-
-    def greet(row_index):
-        for step in (7, 0, 1):
-            peer = (g, row_index, lax.rem(c + step, 8))
-            pl.semaphore_signal(barrier, inc=1, device_id=peer, device_id_type=MESH)
-
-    for peer in (west, east):
-        pl.semaphore_signal(barrier, inc=1, device_id=peer, device_id_type=MESH)
-    pl.when(has_up)(lambda: greet(r - 1))
-    pl.when(has_down)(lambda: greet(r + 1))
-    pl.semaphore_wait(barrier, 3 * row_count(r) - 1)
-    sideways = [
-        remote(left_ref, right_out, sems, 0, west),
-        remote(right_ref, left_out, sems, 1, east),
-    ]
-
-    def to_row(row_index, rows, strip_out, corners, guide_slot, first_slot):
-        west_peer = (g, row_index, west[2])
-        east_peer = (g, row_index, east[2])
-        here = (g, row_index, c)
-        return [
-            remote(own_ref.at[:, rows], strip_out, sems, first_slot, here),
-            remote(guide_ref, guide_out.at[guide_slot], sems, first_slot + 1, here),
-            remote(left_ref.at[rows], corner_out.at[corners + 1], sems, first_slot + 2, west_peer),
-            remote(right_ref.at[rows], corner_out.at[corners], sems, first_slot + 3, east_peer),
-        ]
-
-    upward = to_row(r - 1, pl.ds(0, 3), bottom_out, 2, 1, 2)
-    downward = to_row(r + 1, pl.ds(5, 3), top_out, 0, 0, 6)
-
-    def start(copies):
-        for copy in copies:
-            copy.start()
-
-    def sent(copies):
-        for copy in copies:
-            copy.wait_send()
-
-    def landed(copies):
-        for copy in copies:
-            copy.wait_recv()
-
-    pl.when(has_up)(lambda: start(upward))
-    pl.when(has_down)(lambda: start(downward))
-    start(sideways)
-    landed(sideways)
-    pl.when(has_down)(lambda: landed(upward))
-    pl.when(has_up)(lambda: landed(downward))
-    sent(sideways)
-    pl.when(has_up)(lambda: sent(upward))
-    pl.when(has_down)(lambda: sent(downward))
-
-
 def in_vmem(count):
     return [pl.BlockSpec(memory_space=pltpu.VMEM)] * count
 
 
 def b16(*shape):
     return jax.ShapeDtypeStruct(shape, jnp.bfloat16)
-
-
-def exchange(kernel, ident, outs, sems, *operands):
-    outs = tuple(outs)
-    return pl.pallas_call(
-        kernel,
-        out_shape=outs,
-        in_specs=in_vmem(len(operands)),
-        out_specs=tuple(in_vmem(len(outs))),
-        scratch_shapes=[pltpu.SemaphoreType.DMA(shape) for shape in sems],
-        compiler_params=pltpu.CompilerParams(
-            collective_id=ident, has_side_effects=True, vmem_limit_bytes=24 * 2**20
-        ),
-    )(*operands)
 
 
 def transposed_dot(one, other):
@@ -330,20 +243,14 @@
     return jnp.pad(weight, ((0, 0), (0, i), (0, o))) + jnp.pad(weight, ((0, 0), (i, 0), (o, 0)))
 
 
-def perceptual_weights(vgg_first, vgg_second, vgg_third):
+def first_weights(vgg_first):
     first = vgg_first.reshape(9, 3, 64)
     w1 = jnp.pad(two_blocks(first), ((0, 0), (0, 2), (0, 0))).reshape(72, 128)
-    second = vgg_second.reshape(9, 64, 64)
-    third = vgg_third.reshape(9, 64, 128)
-    w2 = two_blocks(second).reshape(1152, 128)
-    w3 = two_blocks(third).reshape(1152, 256)
-    w3_back = jnp.pad(jnp.transpose(third[::-1], (0, 2, 1)), ((0, 0), (0, 0), (0, 64))).reshape(1152, 128)
-    w2_back = jnp.pad(jnp.transpose(second[::-1], (0, 2, 1)), ((0, 0), (0, 64), (0, 64))).reshape(1152, 128)
     w1_back = jnp.pad(jnp.transpose(first[::-1], (1, 0, 2)), ((0, 5), (0, 0), (0, 64))).reshape(8, 1152)
-    return w1, w2, w3, w3_back, w2_back, w1_back
-
-
-def perceptual_strip(planes, weights):
+    return w1, w1_back
+
+
+def perceptual_strip(planes, first, others):
     f32, half = jnp.float32, jnp.bfloat16
     return pl.pallas_call(
         perceptual_kernel,
@@ -368,9 +275,9 @@
             pltpu.SemaphoreType.DMA(()),
         ],
         compiler_params=pltpu.CompilerParams(
-            collective_id=4, has_side_effects=True, vmem_limit_bytes=40 * 2**20
+            collective_id=4, has_side_effects=True, vmem_limit_bytes=24 * 2**20
         ),
-    )(planes, *weights)
+    )(planes, first[0], *others, first[1])
 
 
 def taps_in_lanes(weight_ref, out_ref):
@@ -390,14 +297,18 @@
             out_ref[128 * q : 128 * (q + 1), 128 * k : 128 * (k + 1)] = block.T.astype(jnp.bfloat16)
 
 
-def conv_frame(source, frame, rows, taps_ref):
-    parts = [
-        source[frame + dt, pl.ds(dr, rows)].reshape(rows * 32, 128) for dt in range(3) for dr in range(3)
-    ]
+def conv_rows(source, frame, starts, count, taps_ref):
+    size = len(starts) * count * 32
+
+    def near(dt, dr):
+        rows = [source[frame + dt, pl.ds(start + dr, count)].reshape(count * 32, 128) for start in starts]
+        return rows[0] if len(rows) == 1 else jnp.concatenate(rows, axis=0)
+
+    parts = [near(dt, dr) for dt in range(3) for dr in range(3)]
     sums = dot32(jnp.concatenate(parts, axis=1), taps_ref[...])
     total = pltpu.roll(sums[:, :128], 1, 0) + sums[:, 128:256]
-    total += pltpu.roll(sums[:, 256:], rows * 32 - 1, 0)
-    return total.reshape(rows, 32, 128)
+    total += pltpu.roll(sums[:, 256:], size - 1, 0)
+    return total.reshape(len(starts) * count, 32, 128)
 
 
 def silu_parts(preact):
@@ -410,15 +321,38 @@
         pl.when((r + step >= 0) & (r + step < 8))(functools.partial(do, step))
 
 
+def lay_out_perceptual(second_ref, third_ref, w2_out, w3_out, w3_back_out, w2_back_out):
+    f32, half = jnp.float32, jnp.bfloat16
+    for t in range(9):
+        block = second_ref[64 * t : 64 * (t + 1), :].astype(f32)
+        wide = third_ref[64 * t : 64 * (t + 1), :].astype(f32)
+        none, low, high = jnp.zeros((64, 64), f32), 128 * t, 128 * (8 - t)
+        w2_out[low : low + 64] = jnp.concatenate([block, none], axis=1).astype(half)
+        w2_out[low + 64 : low + 128] = jnp.concatenate([none, block], axis=1).astype(half)
+        w3_out[low : low + 64, :128] = wide.astype(half)
+        w3_out[low : low + 64, 128:] = jnp.zeros((64, 128), half)
+        w3_out[low + 64 : low + 128, :128] = jnp.zeros((64, 128), half)
+        w3_out[low + 64 : low + 128, 128:] = wide.astype(half)
+        w2_back_out[high : high + 64] = jnp.concatenate([block.T, none], axis=1).astype(half)
+        w2_back_out[high + 64 : high + 128] = jnp.zeros((64, 128), half)
+        turned = jnp.concatenate([wide.T, jnp.zeros((128, 64), f32)], axis=1)
+        w3_back_out[high : high + 128] = turned.astype(half)
+
+
 def forward_kernel(
-    cells_ref, first_ref, second_ref, rgb_ref, hidden_out, slope1_out, slope2_out, near_out,
+    video_ref, target_ref, first_ref, second_ref, rgb_ref, vgg_second_ref, vgg_third_ref,
+    cells, hidden_out, slope1_out, slope2_out, near_out, guide_out, w2_out, w3_out, w3_back_out, w2_back_out,
+    tile, left_send, right_send, top_in, bottom_in, left_in, right_in, corner_in, halo_send, halo_recv,
     taps1, taps2, colours, send_sem, recv_sem, own_sem,
 ):
     g, r, c = position()
     me = (g, r, c)
+    f32, half = jnp.float32, jnp.bfloat16
     barrier = pltpu.get_barrier_semaphore()
     perceives = g < 3
     source_group = (8 * g + c) // 6
+    west, east = lax.rem(c + 7, 8), lax.rem(c + 1, 8)
+    has_up, has_down = r > 0, r < 7
 
     def sources(do):
         def each(step):
@@ -430,27 +364,135 @@
 
         pl.when(perceives)(lambda: on_rows(r, each))
 
-    def greet(step, column, source):
-        pl.semaphore_signal(barrier, inc=1, device_id=source, device_id_type=MESH)
-
-    sources(greet)
+    def signal(peer):
+        pl.semaphore_signal(barrier, inc=1, device_id=peer, device_id_type=MESH)
+
+    signal((g, r, west))
+    signal((g, r, east))
+
+    @pl.when(has_up)
+    def _():
+        for column in (west, c, east):
+            signal((g, r - 1, column))
+
+    @pl.when(has_down)
+    def _():
+        for column in (west, c, east):
+            signal((g, r + 1, column))
+
+    sources(lambda step, column, source: signal(source))
+
+    for f in range(12):
+        frame = 6 * g - 3 + f
+        real = (frame >= 0) & (frame < 24)
+        value = video_ref[jnp.minimum(jnp.maximum(frame, 0), 23)]
+        tile[f] = jnp.where(real, value, jnp.zeros_like(value))
+    for row in range(8):
+        near = [tile[f, row].astype(f32) for f in range(12)]
+        left_send[row] = jnp.concatenate([v[0:4] for v in near], axis=0).astype(half)
+        right_send[row] = jnp.concatenate([v[12:16] for v in near], axis=0).astype(half)
+    block = jnp.minimum(g, 2)
+    planes = [target_ref[k, block, 0].astype(f32) for k in range(3)] + [jnp.zeros((8, 128), f32)]
+    guide_out[1] = jnp.concatenate(planes, axis=0).astype(half)
+
+    to_itself = jnp.where(perceives & (2 * g + c < 6), 1, 0)
+    pl.semaphore_wait(barrier, 9 * row_count(r) - 1 - to_itself)
+
+    def remote(src, dst, slot, peer):
+        return pltpu.make_async_remote_copy(
+            src_ref=src,
+            dst_ref=dst,
+            send_sem=halo_send.at[slot],
+            recv_sem=halo_recv.at[slot],
+            device_id=peer,
+            device_id_type=MESH,
+        )
+
+    sideways = [remote(left_send, right_in, 0, (g, r, west)), remote(right_send, left_in, 1, (g, r, east))]
+
+    def to_row(row_index, rows, strip_in, corners, guide_slot, first_slot):
+        rows = pl.ds(rows, 3)
+        return [
+            remote(tile.at[:, rows], strip_in, first_slot, (g, row_index, c)),
+            remote(left_send.at[rows], corner_in.at[corners + 1], first_slot + 1, (g, row_index, west)),
+            remote(right_send.at[rows], corner_in.at[corners], first_slot + 2, (g, row_index, east)),
+            remote(guide_out.at[1], guide_out.at[guide_slot], first_slot + 3, (g, row_index, c)),
+        ]
+
+    upward = to_row(r - 1, 0, bottom_in, 2, 2, 2)
+    downward = to_row(r + 1, 5, top_in, 0, 0, 6)
+
+    def start(copies):
+        for copy in copies:
+            copy.start()
+
+    def sent(copies):
+        for copy in copies:
+            copy.wait_send()
+
+    def landed(copies):
+        for copy in copies:
+            copy.wait_recv()
+
+    pl.when(has_up)(lambda: start(upward))
+    pl.when(has_down)(lambda: start(downward))
+    start(sideways)
 
     taps_in_lanes(first_ref, taps1)
     taps_in_lanes(second_ref, taps2)
-    row = lax.broadcasted_iota(jnp.int32, (12, 32, 128), 0) + (8 * r - 2)
-    col = lax.broadcasted_iota(jnp.int32, (12, 32, 128), 1) + (16 * c - 8)
-    shown = (row >= 0) & (row < 64) & (col >= 0) & (col < 128)
+
+    def assemble(first_row, count, real, own, left, right):
+        col = lax.broadcasted_iota(jnp.int32, (count, 32, 128), 1) + (16 * c - 8)
+        shown = (col >= 0) & (col < 128) & real
+        for quad in range(3):
+            before = left[:, 16 * quad : 16 * (quad + 1)].astype(f32)
+            after = right[:, 16 * quad : 16 * (quad + 1)].astype(f32)
+            for k in range(4):
+                f, eight = 4 * quad + k, slice(8 * (k // 2), 8 * (k // 2) + 8)
+                one = before[:, eight].reshape(8 * count, 128)
+                two = after[:, eight].reshape(8 * count, 128)
+                if k % 2 == 0:
+                    one = pltpu.roll(one, 4, 0)
+                else:
+                    two = pltpu.roll(two, 8 * count - 4, 0)
+                sides = [one.reshape(count, 8, 128), own(f).astype(f32), two.reshape(count, 8, 128)]
+                value = jnp.where(shown, jnp.concatenate(sides, axis=1), 0.0)
+                cells[f, first_row : first_row + count] = value.astype(half)
+
+    row = lax.broadcasted_iota(jnp.int32, (6, 32, 128), 0)
+    col = lax.broadcasted_iota(jnp.int32, (6, 32, 128), 1) + (16 * c - 8)
+    in_cols = (col >= 0) & (col < 128)
+
+    def in_frames(f):
+        frame = 6 * g - 2 + f
+        return jnp.where((frame >= 0) & (frame < 24), 1.0, 0.0)
+
+    landed(sideways)
+    assemble(3, 8, True, lambda f: tile[f], left_in[...], right_in[...])
 
     @pl.loop(0, 10)
     def _(f):
-        value, slope = silu_parts(conv_frame(cells_ref, f, 12, taps1))
-        frame = 6 * g - 2 + f
-        value = jnp.where(shown, value, 0.0) * jnp.where((frame >= 0) & (frame < 24), 1.0, 0.0)
-        hidden_out[f] = value.astype(jnp.bfloat16)
-        slope1_out[f] = slope[2:10, 8:24].reshape(128, 128)
-
-    to_itself = jnp.where(perceives & (2 * g + c < 6), 1, 0)
-    pl.semaphore_wait(barrier, 6 * row_count(r) - to_itself)
+        value, slope = silu_parts(conv_rows(cells, f, (3,), 6, taps1))
+        value = jnp.where(in_cols, value, 0.0) * in_frames(f)
+        hidden_out[f, 3:9] = value.astype(half)
+        slope1_out[f, 16:112] = slope[:, 8:24].reshape(96, 128)
+
+    lay_out_perceptual(vgg_second_ref, vgg_third_ref, w2_out, w3_out, w3_back_out, w2_back_out)
+    pl.when(has_up)(lambda: landed(downward))
+    pl.when(has_down)(lambda: landed(upward))
+    assemble(0, 3, has_up, lambda f: top_in[f], corner_in[0], corner_in[1])
+    assemble(11, 3, has_down, lambda f: bottom_in[f], corner_in[2], corner_in[3])
+    image_row = jnp.where(row < 3, row, row + 6) + (8 * r - 2)
+    in_image = in_cols & (image_row >= 0) & (image_row < 64)
+
+    @pl.loop(0, 10)
+    def _(f):
+        value, slope = silu_parts(conv_rows(cells, f, (0, 9), 3, taps1))
+        value = (jnp.where(in_image, value, 0.0) * in_frames(f)).astype(half)
+        hidden_out[f, 0:3] = value[0:3]
+        hidden_out[f, 9:12] = value[3:6]
+        slope1_out[f, 0:16] = slope[2, 8:24]
+        slope1_out[f, 112:128] = slope[3, 8:24]
 
     def target(step, slot):
         frame = 6 * g + slot
@@ -469,7 +511,7 @@
     def kept(slot):
         return pltpu.make_async_copy(colours.at[slot], near_out.at[1, c], own_sem)
 
-    def start(slot, step):
+    def start_colour(slot, step):
         away = jnp.logical_not(same_place(target(step, slot), me))
         pl.when(away)(lambda: outgoing(step, slot).start())
         if step == 0:
@@ -493,24 +535,28 @@
 
     @pl.loop(0, 6)
     def _(slot):
-        value, slope = silu_parts(conv_frame(hidden_out, slot + 1, 10, taps2))
+        value, slope = silu_parts(conv_rows(hidden_out, slot + 1, (0,), 10, taps2))
         slope2_out[slot + 1] = slope
         own = value[1:9, 8:24].reshape(128, 128).astype(jnp.bfloat16)
         colour = lax.dot_general(
             rgb_ref[...], own, (((1,), (1,)), ((), ())), preferred_element_type=jnp.float32
         )
         colours[slot] = colour.astype(jnp.bfloat16)
-        on_rows(r, functools.partial(start, slot))
+        on_rows(r, functools.partial(start_colour, slot))
 
     @pl.loop(0, 2)
     def _(end):
-        slope2_out[7 * end] = silu_parts(conv_frame(hidden_out, 7 * end, 10, taps2))[1]
+        slope2_out[7 * end] = silu_parts(conv_rows(hidden_out, 7 * end, (0,), 10, taps2))[1]
 
     sources(arrive)
 
     @pl.loop(0, 6)
     def _(slot):
         on_rows(r, functools.partial(finish, slot))
+
+    sent(sideways)
+    pl.when(has_up)(lambda: sent(upward))
+    pl.when(has_down)(lambda: sent(downward))
 
 
 def columns_in_lanes(source, frame0, row0, out_ref):
@@ -655,7 +701,7 @@
 
     @pl.loop(0, 6)
     def _(f):
-        back = conv_frame(field, f, 8, taps)[:, 8:24].reshape(128, 128)
+        back = conv_rows(field, f, (0,), 8, taps)[:, 8:24].reshape(128, 128)
         value = (back * slope1_ref[f + 2]).astype(half)
         delta[pl.ds(pl.multiple_of(128 * f, 128), 128)] = value
 
@@ -677,7 +723,7 @@
     return jax.ShapeDtypeStruct(shape, jnp.float32)
 
 
-def talking_call(kernel, ident, outs, scratch, *operands):
+def talking_call(kernel, ident, mebibytes, outs, scratch, *operands):
     return pl.pallas_call(
         kernel,
         out_shape=tuple(outs),
@@ -685,7 +731,7 @@
         out_specs=tuple(in_vmem(len(outs))),
         scratch_shapes=scratch,
         compiler_params=pltpu.CompilerParams(
-            collective_id=ident, has_side_effects=True, vmem_limit_bytes=48 * 2**20
+            collective_id=ident, has_side_effects=True, vmem_limit_bytes=mebibytes * 2**20
         ),
     )(*operands)
 
@@ -693,94 +739,52 @@
 def inside(start, count, limit):
     positions = start + jnp.arange(count)
     return (positions >= 0) & (positions < limit)
-
-
-def cell_mask(frame0, frames, row0, rows, col0, cols):
-    keep_frames = inside(frame0, frames, 24)
-    keep_rows = inside(row0, rows, 64)
-    keep_cols = inside(col0, cols, 128)
-    return (keep_frames[:, None, None] & keep_rows[None, :, None] & keep_cols[None, None, :])[
-        ..., None
-    ]
 
 
 def local(dec_input, target, conv_first, conv_second, rgb_weight, vgg_first, vgg_second, vgg_third):
     g, r, c = position()
     channels = dec_input.shape[-1]
     frame0, row0, col0 = 6 * g, 8 * r, 16 * c
-    video = jnp.pad(dec_input.reshape(24, 8, 16, channels), ((3, 3), (0, 0), (0, 0), (0, 0)))
-    own = lax.dynamic_slice_in_dim(video, frame0, 12, axis=0)
-
-    def columns(part):
-        return jnp.transpose(part, (1, 0, 2, 3)).reshape(8, 48, channels)
-
-    guide_own = lax.dynamic_index_in_dim(target, jnp.minimum(g, 2), 1, keepdims=False)
-    guide_own = guide_own.reshape(24, 128)
-    top, bottom, left, right, corners, guide_near = exchange(
-        halo_kernel,
-        2,
-        (
-            b16(12, 3, 16, channels), b16(12, 3, 16, channels), b16(8, 48, channels),
-            b16(8, 48, channels), b16(4, 3, 48, channels), b16(2, 32, 128),
-        ),
-        ((10,), (10,)),
-        own,
-        columns(own[:, :, :4]),
-        columns(own[:, :, 12:]),
-        jnp.pad(guide_own, ((0, 8), (0, 0))),
-    )
-
-    def strip(part):
-        return jnp.transpose(part.reshape(-1, 12, 4, channels), (1, 0, 2, 3))
-
-    gap = jnp.zeros((12, 14, 4, channels), jnp.bfloat16)
-    cells = jnp.concatenate(
-        [
-            gap,
-            jnp.concatenate([strip(corners[0]), strip(left), strip(corners[2])], axis=1),
-            jnp.concatenate([top, own, bottom], axis=1),
-            jnp.concatenate([strip(corners[1]), strip(right), strip(corners[3])], axis=1),
-            gap,
-        ],
-        axis=2,
-    )
-    cells = jnp.where(
-        inside(row0 - 3, 14, 64)[None, :, None, None] & inside(col0 - 8, 32, 128)[None, None, :, None],
-        cells,
-        jnp.zeros_like(cells),
-    )
-    half = jnp.bfloat16
+    half, f32, dma, vmem = jnp.bfloat16, jnp.float32, pltpu.SemaphoreType.DMA, pltpu.VMEM
     rgb = jnp.pad(rgb_weight, ((0, 13), (0, 0)))
-    dma = pltpu.SemaphoreType.DMA
-    hidden, slope1, slope2, colour_near = talking_call(
+    cells, hidden, slope1, slope2, colour_near, guide_near, w2, w3, w3_back, w2_back = talking_call(
         forward_kernel,
         3,
-        (b16(10, 12, 32, 128), f32_shape(10, 128, 128), f32_shape(8, 10, 32, 128), b16(3, 8, 16, 128)),
+        24,
+        (
+            b16(12, 14, 32, 128), b16(10, 12, 32, 128), f32_shape(10, 128, 128), f32_shape(8, 10, 32, 128),
+            b16(3, 8, 16, 128), b16(3, 32, 128),
+            b16(1152, 128), b16(1152, 256), b16(1152, 128), b16(1152, 128),
+        ),
         [
-            pltpu.VMEM((1152, 384), half), pltpu.VMEM((1152, 384), half), pltpu.VMEM((6, 16, 128), half),
+            vmem((12, 8, 16, 128), half), vmem((8, 48, 128), half), vmem((8, 48, 128), half),
+            vmem((12, 3, 16, 128), half), vmem((12, 3, 16, 128), half),
+            vmem((8, 48, 128), half), vmem((8, 48, 128), half), vmem((4, 3, 48, 128), half),
+            dma((10,)), dma((10,)),
+            vmem((1152, 384), half), vmem((1152, 384), half), vmem((6, 16, 128), half),
             dma((3, 6)), dma((3, 8)), dma(()),
         ],
-        cells, conv_first, conv_second, rgb,
+        dec_input.reshape(24, 8, 16, channels), target, conv_first, conv_second, rgb, vgg_second, vgg_third,
     )
     images = jnp.transpose(colour_near[:, :, :3].reshape(3, 8, 3, 8, 16), (0, 3, 2, 1, 4))
-    guides = jnp.stack(
-        [guide_near[0, :24].reshape(3, 8, 128), guide_own.reshape(3, 8, 128), guide_near[1, :24].reshape(3, 8, 128)]
-    )
-    guides = jnp.transpose(guides, (0, 2, 1, 3))
+    guides = jnp.transpose(guide_near[:, :24].reshape(3, 3, 8, 128), (0, 2, 1, 3))
     planes = jnp.concatenate([images.reshape(24, 3, 128), guides.reshape(24, 3, 128)], axis=1)
     planes = jnp.where(inside(row0 - 8, 24, 64)[:, None, None], planes, jnp.zeros_like(planes))
     planes = jnp.pad(planes.astype(jnp.float32), ((0, 0), (0, 2), (0, 0)))
-    returned = perceptual_strip(planes, perceptual_weights(vgg_first, vgg_second, vgg_third))
+    returned = perceptual_strip(planes, first_weights(vgg_first), (w2, w3, w3_back, w2_back))
     rows_near = jnp.transpose(returned[:, :, :24].reshape(8, 3, 3, 8, 128), (2, 0, 1, 3, 4))
     rows_near = rows_near.reshape(3, 8, 24, 128)[:, :, 7:17]
     rows_near = jnp.pad(rows_near, ((0, 0), (0, 0), (0, 0), (8, 8)))
     pixels = lax.dynamic_slice_in_dim(rows_near, col0, 32, axis=3)
-    pixel_keep = cell_mask(frame0 - 1, 8, row0 - 1, 10, col0 - 8, 32)
-    pixels = jnp.where(pixel_keep[None, ..., 0], pixels, jnp.zeros_like(pixels))
+    keep_frames = inside(frame0 - 1, 8, 24)[None, :, None, None]
+    keep_rows = inside(row0 - 1, 10, 64)[None, None, :, None]
+    keep_cols = inside(col0 - 8, 32, 128)[None, None, None, :]
+    pixels = jnp.where(keep_frames & keep_rows & keep_cols, pixels, jnp.zeros_like(pixels))
     pixels = jnp.pad(jnp.transpose(pixels, (1, 0, 2, 3)).reshape(8, 3, 320), ((0, 0), (0, 13), (0, 0)))
     sums = talking_call(
         backward_kernel,
         1,
+        30,
         (f32_shape(2, 16, 128),),
         [
             pltpu.VMEM((1152, 384), half),

time: 125 us -> 117 us (0.936)
  other arithmetic: 6.2 us -> 0.5 us
  Pallas kernels: 99.8 us -> 96.6 us
  local copies, waits for them, and re-layouts: 17.1 us -> 18.7 us
    pallas_call x1 -> x0, Pallas kernels: 11.1 us -> none  [exchange(): pl.pallas_call(kernel, out_shape=outs, in_specs=in_vmem(len(operands)), o...]
    unnamed x34 -> x41, local copies, waits for them, and re-layouts: 7.37 us -> 16.7 us
    pallas_call x2, Pallas kernels: 61.4 us -> 69.6 us  [talking_call(): pl.pallas_call(kernel, out_shape=tuple(outs), in_specs=in_vmem(len(operan...]
    concatenate x1 -> x0, local copies, waits for them, and re-layouts: 5.04 us -> none  [local(): jnp.concatenate([gap, jnp.concatenate([strip(corners[0]), strip(left), st...]
    add x3 -> x1, other arithmetic: 2.95 us -> 0.08 us  [two_blocks(): jnp.pad(weight, ((0, 0), (0, i), (0, o)))]
    select_n x1 -> x0, other arithmetic: 1.65 us -> none  [local(): jnp.where(inside(row0 - 3, 14, 64)[None, :, None, None] & inside(col0 - 8...]
    transpose x9 -> x1, local copies, waits for them, and re-layouts: 1.34 us -> 0.01 us  [first_weights(): jnp.transpose(first[::-1], (1, 0, 2))]
where the time goes in v2:
time: 117 us
  Pallas kernels  96.6 us (83%)
  local copies, waits for them, and re-layouts  18.7 us (16%)
    pallas_call x2, Pallas kernels, talking_call(): pl.pallas_call(kernel, out_shape=tuple(outs), in_specs=in_vmem(len(operan...  69.6 us
    pallas_call x1, Pallas kernels, perceptual_strip(): pl.pallas_call(perceptual_kernel, out_shape=b16(8, 3, 32, 128), in_specs=...  27 us
    unnamed x41, local copies, waits for them, and re-layouts  16.7 us

profile of v2, /device:TPU:32, one launch (start us, length us, event | category | flops | bytes accessed | tf_op | source)
XLA Modules:
  0.0 116.7 jit_solution(4502216721155755809)
XLA Ops:
  0.6 0.7 pad.34.rgb_ref
  1.3 1.0 copy.14.vgg_second_ref
  2.3 0.0 copy-start
  2.4 1.2 copy-done
  3.5 0.0 copy-start.4
  3.5 1.2 copy-done.4
  4.7 0.0 copy-start.5
  4.7 1.1 copy-done.5
  5.8 0.0 copy-start.16
  5.8 0.9 copy-done.16
  6.7 0.0 copy-start.17
  6.7 0.7 copy-done.17
  7.5 0.0 copy-start.18
  7.5 23.4 %shard_map.95 = (bf16[12,14,32,128]{3,2,1,0:T(8,128)(2,1)S(1)}, bf16[10,12,32,128]{3,2,1,0:T(8,128)(2,1)S(1)}, f32[10,128,128]{2,1,0:T(8,128)S(1)}, f32[8,10,32,...) custom-call(bf16[24,8,16,128]{3,2,1,0:T(8,128)(2,1)S(1)} %bitcast.35, ...), custom_call_target="tpu_custom_call" | custom-call | tf_op jit(solution)/shard_map/pallas_call | solution.py:727
  30.8 0.0 copy-start.2
  30.8 1.1 copy-done.2
  31.9 0.0 copy-start.6
  31.9 0.8 copy-done.6
  32.7 0.0 copy-start.8
  32.7 0.8 copy-done.8
  33.6 0.0 copy-start.10
  33.6 0.7 copy-done.10
  34.3 0.0 copy-start.12
  34.3 0.7 copy-done.12
  35.0 0.0 copy-start.14
  35.0 0.1 reshape.111
  35.2 0.2 reshape.122
  35.4 0.1 maximum_select_fusion
  35.6 0.0 copy-done.18
  35.6 0.1 pad_add_fusion
  35.7 0.0 copy-done.14
  35.7 0.0 copy-start.9
  35.8 1.1 copy-done.9
  36.8 0.0 copy-start.11
  36.8 1.0 copy-done.11
  37.8 0.0 copy-start.13
  37.8 1.0 copy-done.13
  38.7 0.0 copy-start.15
  38.7 1.0 copy-done.15
  39.7 0.0 copy-start.1
  39.7 27.0 %shard_map.96 = bf16[8,3,32,128]{3,2,1,0:T(8,128)(2,1)S(1)} custom-call(f32[24,8,128]{2,1,0:T(8,128)S(1)} %pad_convert_fusion.planes_ref, bf16[72,128]{1,0:T(8,128)(2,1)S(1)} %pad_bitcast_fusion.1.w1_ref, bf16[1152,128]{1,0:T(8,128)(2,1)S(1)} %copy-done.11, bf16[1152,256]{1,0:T(8,128)(2,1)S(1)} %copy-done.9, bf16[1152,128]{1,0:T(8,128)(2,1)S(1)} %copy-done.13, ...), custom_call_target="tpu_custom_call" | custom-call | tf_op jit(solution)/shard_map/pallas_call | solution.py:255
  66.8 0.1 broadcast_and_fusion.1
  66.9 0.1 broadcast_and_fusion
  67.0 0.1 fusion.1
  67.1 0.1 reshape.120
  67.3 0.0 copy-done.1
  67.3 0.0 copy-start.3
  67.3 1.3 %copy-done.3 = f32[8,10,32,128]{3,2,1,0:T(8,128)S(1)} copy-done((f32[8,10,32,128]{3,2,1,0:T(8,128)S(1)}, f32[8,10,32,128]{3,2,1,0:T(8,128)}, u32[]{:S(2)}) %copy-start.3) | copy-done | bytes 1310744
  68.6 0.0 copy-start.7
  68.6 1.1 copy-done.7
  69.7 46.2 %shard_map.97 = f32[2,16,128]{2,1,0:T(8,128)S(1)} custom-call(bf16[8,16,320]{2,1,0:T(8,128)(2,1)S(1)} %pad.42.pixel_ref, bf16[12,14,32,128]{3,2,1,0:T(8,128)(2,1)S(1)} %get-tuple-element.18.cells_ref, bf16[10,12,32,128]{3,2,1,0:T(8,128)(2,1)S(1)} %get-tuple-element.19.hidden_ref, f32[10,128,128]{2,1,0:T(8,128)S(1)} %copy-done.7, ...), custom_call_target="tpu_custom_call" | custom-call | tf_op jit(solution)/shard_map/pallas_call | solution.py:727
  116.0 0.7 dynamic-slice_reduce_fusion
  (20 shorter events, 0.2 us)
Async XLA Ops:
  2.3 1.2 %copy-start = (bf16[3456,128]{1,0:T(8,128)(2,1)S(1)}, bf16[3456,128]{1,0:T(8,128)(2,1)}, u32[]{:S(2)}) copy-start(bf16[3456,128]{1,0:T(8,128)(2,1)} %second_ref.3) | copy-start | bytes 2654212
  3.5 1.2 %copy-start.4 = (bf16[3456,128]{1,0:T(8,128)(2,1)S(1)}, bf16[3456,128]{1,0:T(8,128)(2,1)}, u32[]{:S(2)}) copy-start(bf16[3456,128]{1,0:T(8,128)(2,1)} %first_ref.1) | copy-start | bytes 2654212
  4.7 1.1 copy-start.5
  5.8 0.9 copy-start.16
  6.7 0.7 copy-start.17
  7.5 28.1 %copy-start.18 = (bf16[27,64]{1,0:T(8,128)(2,1)S(1)}, bf16[27,64]{1,0:T(8,128)(2,1)}, u32[]{:S(2)}) copy-start(bf16[27,64]{1,0:T(8,128)(2,1)} %param.13) | copy-start | bytes 10372
  30.8 1.1 copy-start.2
  31.9 0.8 copy-start.6
  32.7 0.8 copy-start.8
  33.6 0.7 copy-start.10
  34.3 0.7 copy-start.12
  35.0 0.7 copy-start.14
  35.7 1.1 copy-start.9
  36.8 1.0 copy-start.11
  37.8 1.0 copy-start.13
  38.7 1.0 copy-start.15
  39.7 27.6 %copy-start.1 = (bf16[3456,128]{1,0:T(8,128)(2,1)S(1)}, bf16[3456,128]{1,0:T(8,128)(2,1)}, u32[]{:S(2)}) copy-start(bf16[3456,128]{1,0:T(8,128)(2,1)} %second_ref.3) | copy-start | bytes 2654212
  67.3 1.3 %copy-start.3 = (f32[8,10,32,128]{3,2,1,0:T(8,128)S(1)}, f32[8,10,32,128]{3,2,1,0:T(8,128)}, u32[]{:S(2)}) copy-start(f32[8,10,32,128]{3,2,1,0:T(8,128)} %copy-done.2) | copy-start | bytes 3932164
  68.6 1.1 copy-start.7

commit v3 on v2

--- a/solution.py
+++ b/solution.py
@@ -66,8 +66,9 @@
 
 
 def perceptual_kernel(
-    planes_ref, w1_ref, w2_ref, w3_ref, w3_back_ref, w2_back_ref, w1_back_ref, out_ref,
-    taps, act1, slope1, pooled, delta3, diff2, slope2, delta2, delta1, tmp, pixels, strip, send_sem, recv_sem, own_sem,
+    planes_ref, w1_ref, vgg_second_ref, vgg_third_ref, w1_back_ref, out_ref,
+    taps, act1, slope1, pooled, delta3, diff2, slope2, delta2, delta1, tmp, pixels, strip,
+    w2_ref, w3_ref, w3_back_ref, w2_back_ref, send_sem, recv_sem, own_sem,
 ):
     g, r, c = position()
     me = (g, r, c)
@@ -95,6 +96,7 @@
         pl.semaphore_signal(barrier, inc=1, device_id=source, device_id_type=MESH)
 
     sources(greet)
+    lay_out_perceptual(vgg_second_ref, vgg_third_ref, w2_ref, w3_ref, w3_back_ref, w2_back_ref)
     row0 = 8 * r - 8
     lane = lax.broadcasted_iota(jnp.int32, (192, 128), 1)
     planes = planes_ref[...].reshape(192, 128)
@@ -181,8 +183,12 @@
         direct = (1.0 / 6.0) * (own - pltpu.roll(own, 5, 0))
         pixels[pl.ds(pl.multiple_of(q * 8, 8), 8)] = grad + direct
 
-    rows = [pixels[pl.ds(k, 8, 8)] for k in range(3)] + [jnp.zeros((8, 128), jnp.float32)]
-    strip[...] = jnp.concatenate(rows, axis=0).astype(jnp.bfloat16)
+    colour_rows = [pixels[pl.ds(k, 8, 8)] for k in range(3)]
+    third = lax.broadcasted_iota(jnp.int32, (8, 128), 1) // 32
+    for column in range(8):
+        turned = [pltpu.roll(v, (32 * k + 8 - 16 * column) % 128, 1) for k, v in enumerate(colour_rows)]
+        part = jnp.where(third == 0, turned[0], jnp.where(third == 1, turned[1], turned[2]))
+        strip[column] = jnp.concatenate([part, jnp.zeros((8, 128), jnp.float32)], axis=0).astype(jnp.bfloat16)
 
     groups = jnp.where(perceives, 1, 0) + jnp.where(ahead, 1, 0) + jnp.where(behind, 1, 0)
     to_itself = perceives & (home == g) | ahead & (home == g + 1) | behind & (home == g - 1)
@@ -202,7 +208,7 @@
     def outgoing(kind, step, column, peer):
         place_there = own_frame - 6 * peer[0] + 1
         return pltpu.make_async_remote_copy(
-            src_ref=strip,
+            src_ref=strip.at[column],
             dst_ref=out_ref.at[place_there, 1 - step],
             send_sem=send_sem.at[kind, step + 1, column],
             recv_sem=recv_sem.at[place_there, 1 - step],
@@ -211,7 +217,7 @@
         )
 
     def kept():
-        return pltpu.make_async_copy(strip, out_ref.at[own_frame - 6 * g + 1, 1], own_sem)
+        return pltpu.make_async_copy(strip.at[c], out_ref.at[own_frame - 6 * g + 1, 1], own_sem)
 
     def start(kind, step, column, peer, away):
         pl.when(away)(lambda: outgoing(kind, step, column, peer).start())
@@ -225,7 +231,7 @@
 
     def arrive(step, slot, source):
         pltpu.make_async_remote_copy(
-            src_ref=strip,
+            src_ref=strip.at[0],
             dst_ref=out_ref.at[slot, step + 1],
             send_sem=send_sem.at[0, 0, 0],
             recv_sem=recv_sem.at[slot, step + 1],
@@ -254,8 +260,8 @@
     f32, half = jnp.float32, jnp.bfloat16
     return pl.pallas_call(
         perceptual_kernel,
-        out_shape=b16(8, 3, 32, 128),
-        in_specs=in_vmem(7),
+        out_shape=b16(8, 3, 16, 128),
+        in_specs=in_vmem(5),
         out_specs=in_vmem(1)[0],
         scratch_shapes=[
             pltpu.VMEM((24, 24, 128), f32),
@@ -269,7 +275,11 @@
             pltpu.VMEM((10, 128, 384), half),
             pltpu.VMEM((128, 128), f32),
             pltpu.VMEM((64, 128), f32),
-            pltpu.VMEM((32, 128), half),
+            pltpu.VMEM((8, 16, 128), half),
+            pltpu.VMEM((1152, 128), half),
+            pltpu.VMEM((1152, 256), half),
+            pltpu.VMEM((1152, 128), half),
+            pltpu.VMEM((1152, 128), half),
             pltpu.SemaphoreType.DMA((3, 3, 8)),
             pltpu.SemaphoreType.DMA((8, 3)),
             pltpu.SemaphoreType.DMA(()),
@@ -340,11 +350,20 @@
 
 
 def forward_kernel(
-    video_ref, target_ref, first_ref, second_ref, rgb_ref, vgg_second_ref, vgg_third_ref,
-    cells, hidden_out, slope1_out, slope2_out, near_out, guide_out, w2_out, w3_out, w3_back_out, w2_back_out,
-    tile, left_send, right_send, top_in, bottom_in, left_in, right_in, corner_in, halo_send, halo_recv,
+    video_hbm, target_ref, first_hbm, second_hbm, rgb_ref,
+    cells_hbm, hidden_hbm, slope1_hbm, slope2_hbm, near_out, guide_out,
+    video, first_ref, second_ref, rgb16, cells, hidden_out, slope1_out, slope2_out, load_sem, store_sem,
+    tile, left_send, right_send, edge_tile, edge_left, edge_right, guide_send,
+    top_in, bottom_in, left_in, right_in, corner_in, halo_send, halo_recv,
     taps1, taps2, colours, send_sem, recv_sem, own_sem,
 ):
+    loads = [
+        pltpu.make_async_copy(video_hbm, video, load_sem.at[0]),
+        pltpu.make_async_copy(first_hbm, first_ref, load_sem.at[1]),
+        pltpu.make_async_copy(second_hbm, second_ref, load_sem.at[2]),
+    ]
+    for load in loads:
+        load.start()
     g, r, c = position()
     me = (g, r, c)
     f32, half = jnp.float32, jnp.bfloat16
@@ -353,6 +372,7 @@
     source_group = (8 * g + c) // 6
     west, east = lax.rem(c + 7, 8), lax.rem(c + 1, 8)
     has_up, has_down = r > 0, r < 7
+    group_up, group_down = jnp.where(r == 4, 3 - g, g), jnp.where(r == 3, 3 - g, g)
 
     def sources(do):
         def each(step):
@@ -373,27 +393,51 @@
     @pl.when(has_up)
     def _():
         for column in (west, c, east):
-            signal((g, r - 1, column))
+            signal((group_up, r - 1, column))
 
     @pl.when(has_down)
     def _():
         for column in (west, c, east):
-            signal((g, r + 1, column))
+            signal((group_down, r + 1, column))
 
     sources(lambda step, column, source: signal(source))
 
+    def guide_of(group):
+        block = jnp.minimum(group, 2)
+        rows = [target_ref[k, block, 0].astype(f32) for k in range(3)] + [jnp.zeros((8, 128), f32)]
+        return jnp.concatenate(rows, axis=0).astype(half)
+
+    guide_out[1] = guide_of(g)
+    guide_send[0] = guide_of(group_up)
+    guide_send[1] = guide_of(group_down)
+    rgb16[...] = jnp.zeros((16, 128), f32)
+    rgb16[0:3] = rgb_ref[...].astype(f32)
+    loads[0].wait()
+
+    def frames_of(group, rows):
+        values = []
+        for f in range(12):
+            frame = 6 * group - 3 + f
+            value = video[jnp.minimum(jnp.maximum(frame, 0), 23), rows]
+            values.append(jnp.where((frame >= 0) & (frame < 24), value, jnp.zeros_like(value)))
+        return values
+
+    def sides(values, row):
+        near = [value[row].astype(f32) for value in values]
+        west_side = jnp.concatenate([v[0:4] for v in near], axis=0).astype(half)
+        return west_side, jnp.concatenate([v[12:16] for v in near], axis=0).astype(half)
+
+    for edge, (group, rows) in enumerate(((group_up, slice(0, 3)), (group_down, slice(5, 8)))):
+        values = frames_of(group, rows)
+        for f in range(12):
+            edge_tile[edge, f] = values[f]
+        for row in range(3):
+            edge_left[edge, row], edge_right[edge, row] = sides(values, row)
+    values = frames_of(g, slice(0, 8))
     for f in range(12):
-        frame = 6 * g - 3 + f
-        real = (frame >= 0) & (frame < 24)
-        value = video_ref[jnp.minimum(jnp.maximum(frame, 0), 23)]
-        tile[f] = jnp.where(real, value, jnp.zeros_like(value))
+        tile[f] = values[f]
     for row in range(8):
-        near = [tile[f, row].astype(f32) for f in range(12)]
-        left_send[row] = jnp.concatenate([v[0:4] for v in near], axis=0).astype(half)
-        right_send[row] = jnp.concatenate([v[12:16] for v in near], axis=0).astype(half)
-    block = jnp.minimum(g, 2)
-    planes = [target_ref[k, block, 0].astype(f32) for k in range(3)] + [jnp.zeros((8, 128), f32)]
-    guide_out[1] = jnp.concatenate(planes, axis=0).astype(half)
+        left_send[row], right_send[row] = sides(values, row)
 
     to_itself = jnp.where(perceives & (2 * g + c < 6), 1, 0)
     pl.semaphore_wait(barrier, 9 * row_count(r) - 1 - to_itself)
@@ -410,17 +454,16 @@
 
     sideways = [remote(left_send, right_in, 0, (g, r, west)), remote(right_send, left_in, 1, (g, r, east))]
 
-    def to_row(row_index, rows, strip_in, corners, guide_slot, first_slot):
-        rows = pl.ds(rows, 3)
+    def to_row(edge, group, row_index, strip_in, corners, guide_slot, first_slot):
         return [
-            remote(tile.at[:, rows], strip_in, first_slot, (g, row_index, c)),
-            remote(left_send.at[rows], corner_in.at[corners + 1], first_slot + 1, (g, row_index, west)),
-            remote(right_send.at[rows], corner_in.at[corners], first_slot + 2, (g, row_index, east)),
-            remote(guide_out.at[1], guide_out.at[guide_slot], first_slot + 3, (g, row_index, c)),
+            remote(edge_tile.at[edge], strip_in, first_slot, (group, row_index, c)),
+            remote(edge_left.at[edge], corner_in.at[corners + 1], first_slot + 1, (group, row_index, west)),
+            remote(edge_right.at[edge], corner_in.at[corners], first_slot + 2, (group, row_index, east)),
+            remote(guide_send.at[edge], guide_out.at[guide_slot], first_slot + 3, (group, row_index, c)),
         ]
 
-    upward = to_row(r - 1, 0, bottom_in, 2, 2, 2)
-    downward = to_row(r + 1, 5, top_in, 0, 0, 6)
+    upward = to_row(0, group_up, r - 1, bottom_in, 2, 2, 2)
+    downward = to_row(1, group_down, r + 1, top_in, 0, 0, 6)
 
     def start(copies):
         for copy in copies:
@@ -438,7 +481,9 @@
     pl.when(has_down)(lambda: start(downward))
     start(sideways)
 
+    loads[1].wait()
     taps_in_lanes(first_ref, taps1)
+    loads[2].wait()
     taps_in_lanes(second_ref, taps2)
 
     def assemble(first_row, count, real, own, left, right):
@@ -477,7 +522,6 @@
         hidden_out[f, 3:9] = value.astype(half)
         slope1_out[f, 16:112] = slope[:, 8:24].reshape(96, 128)
 
-    lay_out_perceptual(vgg_second_ref, vgg_third_ref, w2_out, w3_out, w3_back_out, w2_back_out)
     pl.when(has_up)(lambda: landed(downward))
     pl.when(has_down)(lambda: landed(upward))
     assemble(0, 3, has_up, lambda f: top_in[f], corner_in[0], corner_in[1])
@@ -493,6 +537,14 @@
         hidden_out[f, 9:12] = value[3:6]
         slope1_out[f, 0:16] = slope[2, 8:24]
         slope1_out[f, 112:128] = slope[3, 8:24]
+
+    stores = [
+        pltpu.make_async_copy(cells.at[pl.ds(2, 8), pl.ds(2, 10)], cells_hbm, store_sem.at[0]),
+        pltpu.make_async_copy(hidden_out.at[pl.ds(1, 8), pl.ds(1, 10)], hidden_hbm, store_sem.at[1]),
+        pltpu.make_async_copy(slope1_out.at[pl.ds(2, 6)], slope1_hbm, store_sem.at[2]),
+        pltpu.make_async_copy(slope2_out, slope2_hbm, store_sem.at[3]),
+    ]
+    start(stores[:3])
 
     def target(step, slot):
         frame = 6 * g + slot
@@ -539,7 +591,7 @@
         slope2_out[slot + 1] = slope
         own = value[1:9, 8:24].reshape(128, 128).astype(jnp.bfloat16)
         colour = lax.dot_general(
-            rgb_ref[...], own, (((1,), (1,)), ((), ())), preferred_element_type=jnp.float32
+            rgb16[...].astype(half), own, (((1,), (1,)), ((), ())), preferred_element_type=jnp.float32
         )
         colours[slot] = colour.astype(jnp.bfloat16)
         on_rows(r, functools.partial(start_colour, slot))
@@ -548,11 +600,15 @@
     def _(end):
         slope2_out[7 * end] = silu_parts(conv_rows(hidden_out, 7 * end, (0,), 10, taps2))[1]
 
+    stores[3].start()
     sources(arrive)
 
     @pl.loop(0, 6)
     def _(slot):
         on_rows(r, functools.partial(finish, slot))
+
+    for store in stores:
+        store.wait()
 
     sent(sideways)
     pl.when(has_up)(lambda: sent(upward))
@@ -586,11 +642,23 @@
 
 
 def backward_kernel(
-    pixel_ref, cells_ref, hidden_ref, slope1_ref, slope2_ref, second_ref, rgb_ref, out_ref,
+    pixel_ref, cells_hbm, hidden_hbm, slope1_hbm, slope2_hbm, second_hbm, rgb_ref, out_ref,
+    cells_ref, hidden_ref, slope1_ref, slope2_ref, second_ref, rgb16, load_sem,
     taps, columns, field, delta, terms,
     sending, core_in, held, x_in, y_in, mid_x, mid_y, yy_in, xx_in, last, z_in, send_sem, recv_sem,
 ):
     g, r, c = position()
+    loads = [
+        pltpu.make_async_copy(src, dst, load_sem.at[k])
+        for k, (src, dst) in enumerate(
+            (
+                (second_hbm, second_ref), (slope2_hbm, slope2_ref), (hidden_hbm, hidden_ref),
+                (slope1_hbm, slope1_ref), (cells_hbm, cells_ref),
+            )
+        )
+    ]
+    for load in loads:
+        load.start()
     zh, x, y, core = r // 4, lax.rem(r, 4), c // 2, lax.rem(c, 2)
     z = g * 2 + zh
     other = 1 - core
@@ -679,11 +747,15 @@
             total += z_in[which, k].astype(f32)
         out_ref[which] = total
 
+    rgb16[...] = jnp.zeros((16, 128), f32)
+    rgb16[0:3] = rgb_ref[...].astype(f32)
+    loads[0].wait()
     turned_taps(second_ref, taps)
+    loads[1].wait()
 
     @pl.loop(0, 8)
     def _(f):
-        hidden_grad = transposed_dot(pixel_ref[f], rgb_ref[...])
+        hidden_grad = transposed_dot(pixel_ref[f], rgb16[...].astype(half))
         value = hidden_grad.reshape(10, 32, 128) * slope2_ref[f]
         field[f] = value.astype(half)
 
@@ -692,21 +764,24 @@
         own = field[f + 1, 1:9].astype(f32)[:, 8:24].reshape(128, 128).astype(half)
         delta[pl.ds(pl.multiple_of(128 * f, 128), 128)] = own
 
-    columns_in_lanes(hidden_ref, 1, 1, columns)
+    loads[2].wait()
+    columns_in_lanes(hidden_ref, 0, 0, columns)
     terms[pl.ds(3456, 8)] = jnp.zeros((8, 128), f32)
     weight_terms(columns, delta, terms)
     by_chip(terms, sending, 1)
     pl.semaphore_wait(barrier, len(everyone))
     swap_second = to_partner(1)
+    loads[3].wait()
 
     @pl.loop(0, 6)
     def _(f):
         back = conv_rows(field, f, (0,), 8, taps)[:, 8:24].reshape(128, 128)
-        value = (back * slope1_ref[f + 2]).astype(half)
+        value = (back * slope1_ref[f]).astype(half)
         delta[pl.ds(pl.multiple_of(128 * f, 128), 128)] = value
 
     moves_second = first_step(1, swap_second)
-    columns_in_lanes(cells_ref, 2, 2, columns)
+    loads[4].wait()
+    columns_in_lanes(cells_ref, 0, 0, columns)
     weight_terms(columns, delta, terms)
     moves_second = second_step(1, moves_second)
     by_chip(terms, sending, 0)
@@ -723,12 +798,16 @@
     return jax.ShapeDtypeStruct(shape, jnp.float32)
 
 
-def talking_call(kernel, ident, mebibytes, outs, scratch, *operands):
+def places(text):
+    return [pl.BlockSpec(memory_space=pltpu.VMEM if letter == "v" else pl.ANY) for letter in text]
+
+
+def talking_call(kernel, ident, mebibytes, in_places, out_places, outs, scratch, *operands):
     return pl.pallas_call(
         kernel,
         out_shape=tuple(outs),
-        in_specs=in_vmem(len(operands)),
-        out_specs=tuple(in_vmem(len(outs))),
+        in_specs=places(in_places),
+        out_specs=tuple(places(out_places)),
         scratch_shapes=scratch,
         compiler_params=pltpu.CompilerParams(
             collective_id=ident, has_side_effects=True, vmem_limit_bytes=mebibytes * 2**20
@@ -746,47 +825,54 @@
     channels = dec_input.shape[-1]
     frame0, row0, col0 = 6 * g, 8 * r, 16 * c
     half, f32, dma, vmem = jnp.bfloat16, jnp.float32, pltpu.SemaphoreType.DMA, pltpu.VMEM
-    rgb = jnp.pad(rgb_weight, ((0, 13), (0, 0)))
-    cells, hidden, slope1, slope2, colour_near, guide_near, w2, w3, w3_back, w2_back = talking_call(
+    cells, hidden, slope1, slope2, colour_near, guide_near = talking_call(
         forward_kernel,
         3,
-        24,
+        28,
+        "hvhhv",
+        "hhhhvv",
         (
-            b16(12, 14, 32, 128), b16(10, 12, 32, 128), f32_shape(10, 128, 128), f32_shape(8, 10, 32, 128),
+            b16(8, 10, 32, 128), b16(8, 10, 32, 128), f32_shape(6, 128, 128), f32_shape(8, 10, 32, 128),
             b16(3, 8, 16, 128), b16(3, 32, 128),
-            b16(1152, 128), b16(1152, 256), b16(1152, 128), b16(1152, 128),
         ),
         [
+            vmem((24, 8, 16, 128), half), vmem((3456, 128), half), vmem((3456, 128), half), vmem((16, 128), f32),
+            vmem((12, 14, 32, 128), half), vmem((10, 12, 32, 128), half),
+            vmem((10, 128, 128), f32), vmem((8, 10, 32, 128), f32), dma((3,)), dma((4,)),
             vmem((12, 8, 16, 128), half), vmem((8, 48, 128), half), vmem((8, 48, 128), half),
+            vmem((2, 12, 3, 16, 128), half), vmem((2, 3, 48, 128), half), vmem((2, 3, 48, 128), half),
+            vmem((2, 32, 128), half),
             vmem((12, 3, 16, 128), half), vmem((12, 3, 16, 128), half),
             vmem((8, 48, 128), half), vmem((8, 48, 128), half), vmem((4, 3, 48, 128), half),
             dma((10,)), dma((10,)),
             vmem((1152, 384), half), vmem((1152, 384), half), vmem((6, 16, 128), half),
             dma((3, 6)), dma((3, 8)), dma(()),
         ],
-        dec_input.reshape(24, 8, 16, channels), target, conv_first, conv_second, rgb, vgg_second, vgg_third,
+        dec_input.reshape(24, 8, 16, channels), target, conv_first, conv_second, rgb_weight,
     )
     images = jnp.transpose(colour_near[:, :, :3].reshape(3, 8, 3, 8, 16), (0, 3, 2, 1, 4))
     guides = jnp.transpose(guide_near[:, :24].reshape(3, 3, 8, 128), (0, 2, 1, 3))
     planes = jnp.concatenate([images.reshape(24, 3, 128), guides.reshape(24, 3, 128)], axis=1)
     planes = jnp.where(inside(row0 - 8, 24, 64)[:, None, None], planes, jnp.zeros_like(planes))
     planes = jnp.pad(planes.astype(jnp.float32), ((0, 0), (0, 2), (0, 0)))
-    returned = perceptual_strip(planes, first_weights(vgg_first), (w2, w3, w3_back, w2_back))
-    rows_near = jnp.transpose(returned[:, :, :24].reshape(8, 3, 3, 8, 128), (2, 0, 1, 3, 4))
-    rows_near = rows_near.reshape(3, 8, 24, 128)[:, :, 7:17]
-    rows_near = jnp.pad(rows_near, ((0, 0), (0, 0), (0, 0), (8, 8)))
-    pixels = lax.dynamic_slice_in_dim(rows_near, col0, 32, axis=3)
-    keep_frames = inside(frame0 - 1, 8, 24)[None, :, None, None]
+    returned = perceptual_strip(planes, first_weights(vgg_first), (vgg_second, vgg_third))
+    pixels = returned[:, :, :8, :96].reshape(8, 3, 8, 3, 32)
+    pixels = jnp.transpose(pixels, (0, 3, 1, 2, 4)).reshape(8, 3, 24, 32)[:, :, 7:17]
+    keep_frames = inside(frame0 - 1, 8, 24)[:, None, None, None]
     keep_rows = inside(row0 - 1, 10, 64)[None, None, :, None]
     keep_cols = inside(col0 - 8, 32, 128)[None, None, None, :]
     pixels = jnp.where(keep_frames & keep_rows & keep_cols, pixels, jnp.zeros_like(pixels))
-    pixels = jnp.pad(jnp.transpose(pixels, (1, 0, 2, 3)).reshape(8, 3, 320), ((0, 0), (0, 13), (0, 0)))
+    pixels = jnp.pad(pixels.reshape(8, 3, 320), ((0, 0), (0, 13), (0, 0)))
     sums = talking_call(
         backward_kernel,
         1,
-        30,
+        34,
+        "vhhhhhv",
+        "v",
         (f32_shape(2, 16, 128),),
         [
+            vmem((8, 10, 32, 128), half), vmem((8, 10, 32, 128), half), vmem((6, 128, 128), f32),
+            vmem((8, 10, 32, 128), f32), vmem((3456, 128), half), vmem((16, 128), f32), dma((5,)),
             pltpu.VMEM((1152, 384), half),
             pltpu.VMEM((8, 10, 16, 384), half),
             pltpu.VMEM((8, 10, 32, 128), half),
@@ -806,7 +892,7 @@
             dma((2, 20)),
             dma((2, 20)),
         ],
-        pixels, cells, hidden, slope1, slope2, conv_second, rgb,
+        pixels, cells, hidden, slope1, slope2, conv_second, rgb_weight,
     )[0]
     flat = sums[:, :14].reshape(2, 14 * 128)
     own_sums = lax.dynamic_slice_in_dim(flat, lax.rem(c, 2) * 64, 1728, axis=1)

time: 117 us -> 122 us (1.043)
  other arithmetic: 0.5 us -> 3.29 us
  local copies, waits for them, and re-layouts: 18.7 us -> 20.7 us
    unnamed x41 -> x29, local copies, waits for them, and re-layouts: 16.7 us -> 11 us
    reshape x2, local copies, waits for them, and re-layouts: 0.18 us -> 3.34 us  [local(): images.reshape(24, 3, 128)]
    reshape x3, local copies, waits for them, and re-layouts: 0.16 us -> 2.61 us  [the longest x1 1.59 us: local(): pixels = returned[:, :, :8, :96].reshape(8, 3, 8, 3, 32)]
    slice x1 -> x2, local copies, waits for them, and re-layouts: 0.03 us -> 2.16 us  [the longest x1 1.54 us: local(): jnp.transpose(pixels, (0, 3, 1, 2, 4)).reshape(8, 3, 24, 32)[:, :, 7:17]]
    select_n x0 -> x1, other arithmetic: none -> 1.54 us  [local(): jnp.where(keep_frames & keep_rows & keep_cols, pixels, jnp.zeros_like(pix...]
where the time goes in v3:
time: 122 us
  Pallas kernels  96.9 us (79%)
  local copies, waits for them, and re-layouts  20.7 us (17%)
  other arithmetic  3.29 us (3%)
    pallas_call x2, Pallas kernels, talking_call(): pl.pallas_call(kernel, out_shape=tuple(outs), in_specs=places(in_places),...  69.5 us
    pallas_call x1, Pallas kernels, perceptual_strip(): pl.pallas_call(perceptual_kernel, out_shape=b16(8, 3, 16, 128), in_specs=...  27.4 us
    unnamed x29, local copies, waits for them, and re-layouts  11 us
    reshape x2, local copies, waits for them, and re-layouts, local(): images.reshape(24, 3, 128)  3.34 us

profile of v3, /device:TPU:32, one launch (start us, length us, event | category | flops | bytes accessed | tf_op | source)
XLA Modules:
  0.0 121.7 jit_solution(582516538733470228)
XLA Ops:
  0.6 0.0 copy-start
  0.6 1.2 copy-done
  1.8 0.0 copy-start.2
  1.8 1.2 copy-done.2
  3.0 0.0 copy-start.3
  3.0 1.1 copy-done.3
  4.1 0.0 copy-start.9
  4.1 0.7 copy-done.9
  4.8 0.0 copy-start.10
  4.8 0.7 copy-done.10
  5.5 0.0 copy-start.12
  5.5 24.0 %shard_map.95 = (bf16[8,10,32,128]{3,2,1,0:T(8,128)(2,1)S(1)}, bf16[8,10,32,128]{3,2,1,0:T(8,128)(2,1)S(1)}, f32[6,128,128]{2,1,0:T(8,128)S(1)}, f32[8,10,32,128...) custom-call(bf16[24,8,16,128]{3,2,1,0:T(8,128)(2,1)S(1)} %bitcast.31, ...), custom_call_target="tpu_custom_call" | custom-call | tf_op jit(solution)/shard_map/pallas_call | solution.py:806
  29.6 0.0 copy-start.5
  29.6 0.7 copy-done.5
  30.4 0.8 reshape.108
  31.1 0.0 copy-start.1
  31.1 0.0 copy-start.11
  31.1 1.7 %copy.21 = bf16[3,8,3,8,16]{4,3,2,1,0:T(8,128)(2,1)} copy(bf16[3,8,3,8,16]{4,1,3,2,0:T(8,128)(2,1)} %bitcast.32) | data formatting | bytes 36864 | tf_op jit(solution)/shard_map/reshape | solution.py:855
  32.8 1.7 %reshape.119 = bf16[24,3,128]{2,1,0:T(4,128)(2,1)} reshape(bf16[3,8,3,8,16]{4,3,2,1,0:T(8,128)(2,1)} %copy.21) | data formatting | bytes 36864 | tf_op jit(solution)/shard_map/reshape | solution.py:855
  34.5 0.8 maximum_select_fusion
  35.3 0.7 pad_convert_fusion.planes_ref
  36.0 0.0 copy-done.12
  36.0 0.1 pad_add_fusion
  36.1 1.7 %copy.18.vgg_second_ref = bf16[576,64]{1,0:T(8,128)(2,1)} copy(bf16[576,64]{0,1:T(8,128)(2,1)} %param.14) | data formatting | bytes 147456 | tf_op args[6]
  37.8 0.0 copy-start.4
  37.8 0.9 copy-done.4
  38.7 0.0 copy-start.7
  38.7 0.9 copy-done.7
  39.6 0.0 copy-start.8
  39.6 0.9 copy-done.8
  40.5 27.4 %shard_map.96 = bf16[8,3,16,128]{3,2,1,0:T(8,128)(2,1)S(1)} custom-call(f32[24,8,128]{2,1,0:T(8,128)S(1)} %copy-done.7, bf16[72,128]{1,0:T(8,128)(2,1)S(1)} %pad_bitcast_fusion.1.w1_ref, bf16[576,64]{1,0:T(8,128)(2,1)S(1)} %copy-done.4, bf16[576,128]{1,0:T(8,128)(2,1)S(1)} %copy-done.8, bf16[8,1152]{1,0:T(8,128)(2,1)S(1)} %pad_bitcast_fusion.w1_back_ref), custom_call_target="tpu_custom_call" | custom-call | tf_op jit(solution)/shard_map/pallas_call | solution.py:261
  67.9 0.6 slice.23
  68.5 1.6 %reshape.115 = bf16[8,3,8,3,32]{4,3,2,1,0:T(4,128)(2,1)} reshape(bf16[8,3,8,96]{3,2,1,0:T(8,128)(2,1)} %slice.23) | data formatting | bytes 73728 | tf_op jit(solution)/shard_map/reshape | solution.py:859
  70.1 1.5 %slice.28 = bf16[8,3,10,32]{3,1,2,0:T(4,128)(2,1)} slice(bf16[8,3,24,32]{3,1,2,0:T(4,128)(2,1)} %bitcast.33), slice={[0:8], [0:3], [7:17], [0:32]} | slice | bytes 30720 | tf_op jit(solution)/shard_map/slice | solution.py:860
  71.7 0.1 broadcast_and_fusion.1
  71.8 0.1 broadcast_and_fusion
  71.9 1.5 %copy_select_fusion = bf16[8,3,10,32]{3,2,0,1:T(8,128)(2,1)} fusion(bf16[8,3,10,32]{3,1,2,0:T(4,128)(2,1)} %slice.28, pred[8,10,32]{2,1,0:T(8,128)(4,1)S(1)} %broadcast_and_fusion), kind=kLoop, calls=%fused_computation | loop fusion | flops 7680 | bytes 33280 | tf_op jit(solution)/shard_map/jit(_where)/select_n | solution.py:864
  73.4 1.0 reshape.117
  74.5 0.0 copy-done.1
  74.5 0.0 copy-done.11
  74.5 0.0 copy-start.6
  74.5 1.0 copy-done.6
  75.5 45.4 %shard_map.97 = f32[2,16,128]{2,1,0:T(8,128)S(1)} custom-call(bf16[8,16,320]{2,1,0:T(8,128)(2,1)S(1)} %pad.32.pixel_ref, bf16[8,10,32,128]{3,2,1,0:T(8,128)(2,1)S(1)} %get-tuple-element.10.cells_hbm, bf16[8,10,32,128]{3,2,1,0:T(8,128)(2,1)S(1)} %get-tuple-element.11.hidden_hbm, f32[6,128,128]{2,1,0:T(8,128)S(1)} %copy-done.6, ...), custom_call_target="tpu_custom_call" | custom-call | tf_op jit(solution)/shard_map/pallas_call | solution.py:806
  121.0 0.7 dynamic-slice_reduce_fusion
  (16 shorter events, 0.1 us)
Async XLA Ops:
  0.6 1.2 copy-start
  1.8 1.2 copy-start.2
  3.0 1.1 copy-start.3
  4.1 0.7 copy-start.9
  4.8 0.7 copy-start.10
  5.5 30.5 %copy-start.12 = (bf16[27,64]{1,0:T(8,128)(2,1)S(1)}, bf16[27,64]{1,0:T(8,128)(2,1)}, u32[]{:S(2)}) copy-start(bf16[27,64]{1,0:T(8,128)(2,1)} %param.13) | copy-start | bytes 10372
  29.6 0.7 copy-start.5
  31.1 43.3 %copy-start.1 = (bf16[3456,128]{1,0:T(8,128)(2,1)S(1)}, bf16[3456,128]{1,0:T(8,128)(2,1)}, u32[]{:S(2)}) copy-start(bf16[3456,128]{1,0:T(8,128)(2,1)} %second_hbm.3) | copy-start | bytes 2654212
  31.1 43.3 %copy-start.11 = (bf16[3,128]{1,0:T(4,128)(2,1)S(1)}, bf16[3,128]{1,0:T(4,128)(2,1)}, u32[]{:S(2)}) copy-start(bf16[3,128]{1,0:T(4,128)(2,1)} %rgb_ref.3) | copy-start | bytes 2308
  37.8 0.9 copy-start.4
  38.7 0.9 copy-start.7
  39.6 0.9 copy-start.8
  74.5 1.0 copy-start.6

commit v4 on v3

--- a/solution.py
+++ b/solution.py
@@ -66,7 +66,8 @@
 
 
 def perceptual_kernel(
-    planes_ref, w1_ref, vgg_second_ref, vgg_third_ref, w1_back_ref, out_ref,
+    near_ref, guide_ref, w1_ref, vgg_second_ref, vgg_third_ref, w1_back_ref, out_ref,
+    planes_ref, guides,
     taps, act1, slope1, pooled, delta3, diff2, slope2, delta2, delta1, tmp, pixels, strip,
     w2_ref, w3_ref, w3_back_ref, w2_back_ref, send_sem, recv_sem, own_sem,
 ):
@@ -98,6 +99,20 @@
     sources(greet)
     lay_out_perceptual(vgg_second_ref, vgg_third_ref, w2_ref, w3_ref, w3_back_ref, w2_back_ref)
     row0 = 8 * r - 8
+    kind = lax.broadcasted_iota(jnp.int32, (8, 128), 0)
+    block = lax.broadcasted_iota(jnp.int32, (8, 128), 1) // 16
+    for part in range(3):
+        guides[...] = guide_ref[part].astype(jnp.float32)
+        tiles = [near_ref[part, column].astype(jnp.float32)[0:8] for column in range(8)]
+        here = (kind < 3) & (row0 + 8 * part >= 0) & (row0 + 8 * part < 64)
+        seen = (row0 + 8 * part >= 0) & (row0 + 8 * part < 64)
+        for i in range(8):
+            image = jnp.zeros((8, 128), jnp.float32)
+            for column in range(8):
+                turned = pltpu.roll(tiles[column], (16 * column - 16 * i) % 128, 1)
+                image = jnp.where(block == column, turned, image)
+            planes_ref[8 * part + i] = jnp.where(here, image, 0.0)
+            planes_ref[8 * part + i, 3:6] = jnp.where(seen, guides[pl.ds(i, 3, 8)], 0.0)
     lane = lax.broadcasted_iota(jnp.int32, (192, 128), 1)
     planes = planes_ref[...].reshape(192, 128)
     before = jnp.where(lane == 0, 0.0, pltpu.roll(planes, 1, 1))
@@ -256,14 +271,16 @@
     return w1, w1_back
 
 
-def perceptual_strip(planes, first, others):
+def perceptual_strip(near, guides, first, others):
     f32, half = jnp.float32, jnp.bfloat16
     return pl.pallas_call(
         perceptual_kernel,
         out_shape=b16(8, 3, 16, 128),
-        in_specs=in_vmem(5),
+        in_specs=in_vmem(6),
         out_specs=in_vmem(1)[0],
         scratch_shapes=[
+            pltpu.VMEM((24, 8, 128), f32),
+            pltpu.VMEM((32, 128), f32),
             pltpu.VMEM((24, 24, 128), f32),
             pltpu.VMEM((22, 128, 384), half),
             pltpu.VMEM((10, 128, 128), f32),
@@ -287,7 +304,7 @@
         compiler_params=pltpu.CompilerParams(
             collective_id=4, has_side_effects=True, vmem_limit_bytes=24 * 2**20
         ),
-    )(planes, first[0], *others, first[1])
+    )(near, guides, first[0], *others, first[1])
 
 
 def taps_in_lanes(weight_ref, out_ref):
@@ -334,7 +351,8 @@
 def lay_out_perceptual(second_ref, third_ref, w2_out, w3_out, w3_back_out, w2_back_out):
     f32, half = jnp.float32, jnp.bfloat16
     for t in range(9):
-        block = second_ref[64 * t : 64 * (t + 1), :].astype(f32)
+        turned_block = second_ref[:, 64 * t : 64 * (t + 1)].astype(f32)
+        block = turned_block.T
         wide = third_ref[64 * t : 64 * (t + 1), :].astype(f32)
         none, low, high = jnp.zeros((64, 64), f32), 128 * t, 128 * (8 - t)
         w2_out[low : low + 64] = jnp.concatenate([block, none], axis=1).astype(half)
@@ -343,7 +361,7 @@
         w3_out[low : low + 64, 128:] = jnp.zeros((64, 128), half)
         w3_out[low + 64 : low + 128, :128] = jnp.zeros((64, 128), half)
         w3_out[low + 64 : low + 128, 128:] = wide.astype(half)
-        w2_back_out[high : high + 64] = jnp.concatenate([block.T, none], axis=1).astype(half)
+        w2_back_out[high : high + 64] = jnp.concatenate([turned_block, none], axis=1).astype(half)
         w2_back_out[high + 64 : high + 128] = jnp.zeros((64, 128), half)
         turned = jnp.concatenate([wide.T, jnp.zeros((128, 64), f32)], axis=1)
         w3_back_out[high : high + 128] = turned.astype(half)
@@ -753,11 +771,24 @@
     turned_taps(second_ref, taps)
     loads[1].wait()
 
+    lane = lax.broadcasted_iota(jnp.int32, (8, 128), 1)
+    col = lax.rem(lane, 32) + (16 * c - 8)
+    in_cols = (lane < 96) & (col >= 0) & (col < 128)
+
     @pl.loop(0, 8)
     def _(f):
-        hidden_grad = transposed_dot(pixel_ref[f], rgb16[...].astype(half))
-        value = hidden_grad.reshape(10, 32, 128) * slope2_ref[f]
-        field[f] = value.astype(half)
+        frame = 6 * g - 1 + f
+        known = in_cols & (frame >= 0) & (frame < 24)
+        parts = []
+        for part in range(3):
+            seen = known & (r + part - 1 >= 0) & (r + part - 1 < 8)
+            parts.append(jnp.where(seen, pixel_ref[f, part].astype(f32)[0:8], 0.0))
+        turned = jnp.concatenate(parts, axis=0).T
+        for i in range(10):
+            hidden_grad = turned[0:32, i + 7 : i + 8] * rgb16[0:1]
+            for k in (1, 2):
+                hidden_grad += turned[32 * k : 32 * (k + 1), i + 7 : i + 8] * rgb16[k : k + 1]
+            field[f, i] = (hidden_grad * slope2_ref[f, i]).astype(half)
 
     @pl.loop(0, 6)
     def _(f):
@@ -799,7 +830,7 @@
 
 
 def places(text):
-    return [pl.BlockSpec(memory_space=pltpu.VMEM if letter == "v" else pl.ANY) for letter in text]
+    return [pl.BlockSpec(memory_space=pltpu.VMEM if letter == "v" else pltpu.HBM) for letter in text]
 
 
 def talking_call(kernel, ident, mebibytes, in_places, out_places, outs, scratch, *operands):
@@ -815,20 +846,14 @@
     )(*operands)
 
 
-def inside(start, count, limit):
-    positions = start + jnp.arange(count)
-    return (positions >= 0) & (positions < limit)
-
-
 def local(dec_input, target, conv_first, conv_second, rgb_weight, vgg_first, vgg_second, vgg_third):
     g, r, c = position()
     channels = dec_input.shape[-1]
-    frame0, row0, col0 = 6 * g, 8 * r, 16 * c
     half, f32, dma, vmem = jnp.bfloat16, jnp.float32, pltpu.SemaphoreType.DMA, pltpu.VMEM
     cells, hidden, slope1, slope2, colour_near, guide_near = talking_call(
         forward_kernel,
         3,
-        28,
+        58,
         "hvhhv",
         "hhhhvv",
         (
@@ -850,23 +875,13 @@
         ],
         dec_input.reshape(24, 8, 16, channels), target, conv_first, conv_second, rgb_weight,
     )
-    images = jnp.transpose(colour_near[:, :, :3].reshape(3, 8, 3, 8, 16), (0, 3, 2, 1, 4))
-    guides = jnp.transpose(guide_near[:, :24].reshape(3, 3, 8, 128), (0, 2, 1, 3))
-    planes = jnp.concatenate([images.reshape(24, 3, 128), guides.reshape(24, 3, 128)], axis=1)
-    planes = jnp.where(inside(row0 - 8, 24, 64)[:, None, None], planes, jnp.zeros_like(planes))
-    planes = jnp.pad(planes.astype(jnp.float32), ((0, 0), (0, 2), (0, 0)))
-    returned = perceptual_strip(planes, first_weights(vgg_first), (vgg_second, vgg_third))
-    pixels = returned[:, :, :8, :96].reshape(8, 3, 8, 3, 32)
-    pixels = jnp.transpose(pixels, (0, 3, 1, 2, 4)).reshape(8, 3, 24, 32)[:, :, 7:17]
-    keep_frames = inside(frame0 - 1, 8, 24)[:, None, None, None]
-    keep_rows = inside(row0 - 1, 10, 64)[None, None, :, None]
-    keep_cols = inside(col0 - 8, 32, 128)[None, None, None, :]
-    pixels = jnp.where(keep_frames & keep_rows & keep_cols, pixels, jnp.zeros_like(pixels))
-    pixels = jnp.pad(pixels.reshape(8, 3, 320), ((0, 0), (0, 13), (0, 0)))
+    pixels = perceptual_strip(
+        colour_near, guide_near, first_weights(vgg_first), (vgg_second.T, vgg_third)
+    )
     sums = talking_call(
         backward_kernel,
         1,
-        34,
+        58,
         "vhhhhhv",
         "v",
         (f32_shape(2, 16, 128),),

time: 122 us -> 105 us (0.86)
  local copies, waits for them, and re-layouts: 20.7 us -> 3.76 us
  other arithmetic: 3.29 us -> 0.08 us
  Pallas kernels: 96.9 us -> 100 us
    unnamed x29 -> x14, local copies, waits for them, and re-layouts: 11 us -> 3.01 us
    reshape x8 -> x0, local copies, waits for them, and re-layouts: 6.76 us -> none  [the longest x2 3.34 us: local(): images.reshape(24, 3, 128)]
    pallas_call x2, Pallas kernels: 69.5 us -> 72.6 us  [talking_call(): pl.pallas_call(kernel, out_shape=tuple(outs), in_specs=places(in_places),...]
    select_n x2 -> x0, other arithmetic: 2.37 us -> none  [the longest x1 1.54 us: local(): jnp.where(keep_frames & keep_rows & keep_cols, pixels, jnp.zeros_like(pix...]
    slice x4 -> x0, local copies, waits for them, and re-layouts: 2.18 us -> none  [the longest x1 1.54 us: local(): jnp.transpose(pixels, (0, 3, 1, 2, 4)).reshape(8, 3, 24, 32)[:, :, 7:17]]
where the time goes in v4:
time: 105 us
  Pallas kernels  100 us (95%)
  local copies, waits for them, and re-layouts  3.76 us (4%)
    pallas_call x2, Pallas kernels, talking_call(): pl.pallas_call(kernel, out_shape=tuple(outs), in_specs=places(in_places),...  72.6 us
    pallas_call x1, Pallas kernels, perceptual_strip(): pl.pallas_call(perceptual_kernel, out_shape=b16(8, 3, 16, 128), in_specs=...  27.6 us
    unnamed x14, local copies, waits for them, and re-layouts  3.01 us

profile of v4, /device:TPU:32, one launch (start us, length us, event | category | flops | bytes accessed | tf_op | source)
XLA Modules:
  0.0 104.8 jit_solution(5395863952204271008)
XLA Ops:
  0.6 0.0 copy-start.5
  0.6 0.0 copy-start.1
  0.7 0.0 copy-start.3
  0.7 25.1 %shard_map.95 = (bf16[8,10,32,128]{3,2,1,0:T(8,128)(2,1)}, bf16[8,10,32,128]{3,2,1,0:T(8,128)(2,1)}, f32[6,128,128]{2,1,0:T(8,128)}, f32[8,10,32,128]{3,2,1,0:T(...) custom-call(bf16[24,8,16,128]{3,2,1,0:T(8,128)(2,1)} %bitcast.14, ...), custom_call_target="tpu_custom_call" | custom-call | tf_op jit(solution)/shard_map/pallas_call | solution.py:837
  25.8 0.0 copy-done.5
  25.8 0.1 pad_add_fusion
  26.0 0.0 copy-done.1
  26.0 0.0 copy-done.3
  26.0 0.0 copy-start.2
  26.0 0.9 copy-done.2
  26.9 0.0 copy-start.4
  26.9 0.7 copy-done.4
  27.6 27.6 %shard_map.96.pixel_ref = bf16[8,3,16,128]{3,2,1,0:T(8,128)(2,1)S(1)} custom-call(bf16[3,8,16,128]{3,2,1,0:T(8,128)(2,1)S(1)} %copy-done.2, bf16[3,32,128]{2,1,0:T(8,128)(2,1)S(1)} %copy-done.4, bf16[72,128]{1,0:T(8,128)(2,1)S(1)} %pad_bitcast_fusion.1.w1_ref, bf16[64,576]{1,0:T(8,128)(2,1)S(1)} %bitcast.13, bf16[576,128]{1,0:T(8,128)(2,1)S(1)} %copy-done.1, ...), custom_call_target="tpu_custom_call" | custom-call | tf_op jit(solution)/shard_map/pallas_call | solution.py:276
  55.2 0.0 copy-start
  55.3 0.6 copy-done
  55.9 47.4 %shard_map.97 = f32[2,16,128]{2,1,0:T(8,128)} custom-call(bf16[8,3,16,128]{3,2,1,0:T(8,128)(2,1)} %copy-done, bf16[8,10,32,128]{3,2,1,0:T(8,128)(2,1)} %get-tuple-element.10.cells_hbm, bf16[8,10,32,128]{3,2,1,0:T(8,128)(2,1)} %get-tuple-element.11.hidden_hbm, f32[6,128,128]{2,1,0:T(8,128)} %get-tuple-element.12.slope1_hbm, ...), custom_call_target="tpu_custom_call" | custom-call | tf_op jit(solution)/shard_map/pallas_call | solution.py:837
  103.3 0.7 slice_bitcast_fusion
  104.1 0.7 dynamic-slice_reduce_fusion
  (5 shorter events, 0.1 us)
Async XLA Ops:
  0.6 25.2 %copy-start.5 = (bf16[27,64]{1,0:T(8,128)(2,1)S(1)}, bf16[27,64]{1,0:T(8,128)(2,1)}, u32[]{:S(2)}) copy-start(bf16[27,64]{1,0:T(8,128)(2,1)} %param.13) | copy-start | bytes 10372
  0.6 25.3 %copy-start.1 = (bf16[576,128]{1,0:T(8,128)(2,1)S(1)}, bf16[576,128]{1,0:T(8,128)(2,1)}, u32[]{:S(2)}) copy-start(bf16[576,128]{1,0:T(8,128)(2,1)} %vgg_third_ref.1) | copy-start | bytes 442372
  0.7 25.3 %copy-start.3 = (bf16[576,64]{0,1:T(8,128)(2,1)S(1)}, bf16[576,64]{0,1:T(8,128)(2,1)}, u32[]{:S(2)}) copy-start(bf16[576,64]{0,1:T(8,128)(2,1)} %param.14) | copy-start | bytes 221188
  26.0 0.9 copy-start.2
  26.9 0.7 copy-start.4
  55.2 0.6 copy-start

commit v5 on v4

--- a/solution.py
+++ b/solution.py
@@ -371,8 +371,8 @@
     video_hbm, target_ref, first_hbm, second_hbm, rgb_ref,
     cells_hbm, hidden_hbm, slope1_hbm, slope2_hbm, near_out, guide_out,
     video, first_ref, second_ref, rgb16, cells, hidden_out, slope1_out, slope2_out, load_sem, store_sem,
-    tile, left_send, right_send, edge_tile, edge_left, edge_right, guide_send,
-    top_in, bottom_in, left_in, right_in, corner_in, halo_send, halo_recv,
+    tile, left_send, right_send, left_in, right_in, rows_in, to_west, to_east, from_east, from_west,
+    halo_send, halo_recv, edge_send, edge_recv,
     taps1, taps2, colours, send_sem, recv_sem, own_sem,
 ):
     loads = [
@@ -390,7 +390,7 @@
     source_group = (8 * g + c) // 6
     west, east = lax.rem(c + 7, 8), lax.rem(c + 1, 8)
     has_up, has_down = r > 0, r < 7
-    group_up, group_down = jnp.where(r == 4, 3 - g, g), jnp.where(r == 3, 3 - g, g)
+    has_prev, has_next = g > 0, g < 3
 
     def sources(do):
         def each(step):
@@ -408,57 +408,36 @@
     signal((g, r, west))
     signal((g, r, east))
 
-    @pl.when(has_up)
+    pl.when(has_up)(lambda: signal((g, r - 1, c)))
+    pl.when(has_down)(lambda: signal((g, r + 1, c)))
+
+    @pl.when(has_prev)
     def _():
         for column in (west, c, east):
-            signal((group_up, r - 1, column))
-
-    @pl.when(has_down)
+            signal((g - 1, r, column))
+
+    @pl.when(has_next)
     def _():
         for column in (west, c, east):
-            signal((group_down, r + 1, column))
+            signal((g + 1, r, column))
 
     sources(lambda step, column, source: signal(source))
 
-    def guide_of(group):
-        block = jnp.minimum(group, 2)
-        rows = [target_ref[k, block, 0].astype(f32) for k in range(3)] + [jnp.zeros((8, 128), f32)]
-        return jnp.concatenate(rows, axis=0).astype(half)
-
-    guide_out[1] = guide_of(g)
-    guide_send[0] = guide_of(group_up)
-    guide_send[1] = guide_of(group_down)
+    block = jnp.minimum(g, 2)
+    guide = [target_ref[k, block, 0].astype(f32) for k in range(3)] + [jnp.zeros((8, 128), f32)]
+    guide_out[1] = jnp.concatenate(guide, axis=0).astype(half)
     rgb16[...] = jnp.zeros((16, 128), f32)
     rgb16[0:3] = rgb_ref[...].astype(f32)
     loads[0].wait()
 
-    def frames_of(group, rows):
-        values = []
-        for f in range(12):
-            frame = 6 * group - 3 + f
-            value = video[jnp.minimum(jnp.maximum(frame, 0), 23), rows]
-            values.append(jnp.where((frame >= 0) & (frame < 24), value, jnp.zeros_like(value)))
-        return values
-
-    def sides(values, row):
-        near = [value[row].astype(f32) for value in values]
-        west_side = jnp.concatenate([v[0:4] for v in near], axis=0).astype(half)
-        return west_side, jnp.concatenate([v[12:16] for v in near], axis=0).astype(half)
-
-    for edge, (group, rows) in enumerate(((group_up, slice(0, 3)), (group_down, slice(5, 8)))):
-        values = frames_of(group, rows)
-        for f in range(12):
-            edge_tile[edge, f] = values[f]
-        for row in range(3):
-            edge_left[edge, row], edge_right[edge, row] = sides(values, row)
-    values = frames_of(g, slice(0, 8))
     for f in range(12):
-        tile[f] = values[f]
-    for row in range(8):
-        left_send[row], right_send[row] = sides(values, row)
+        frame = 6 * g - 3 + f
+        value = video[jnp.minimum(jnp.maximum(frame, 0), 23)]
+        tile[f] = jnp.where((frame >= 0) & (frame < 24), value, jnp.zeros_like(value))
 
     to_itself = jnp.where(perceives & (2 * g + c < 6), 1, 0)
-    pl.semaphore_wait(barrier, 9 * row_count(r) - 1 - to_itself)
+    groups_near = jnp.where(has_prev, 1, 0) + jnp.where(has_next, 1, 0)
+    pl.semaphore_wait(barrier, 7 * row_count(r) + 1 + 3 * groups_near - to_itself)
 
     def remote(src, dst, slot, peer):
         return pltpu.make_async_remote_copy(
@@ -472,16 +451,68 @@
 
     sideways = [remote(left_send, right_in, 0, (g, r, west)), remote(right_send, left_in, 1, (g, r, east))]
 
-    def to_row(edge, group, row_index, strip_in, corners, guide_slot, first_slot):
+    def to_row(row_index, rows, edge, guide_slot, first_slot):
+        strip = tile.at[pl.ds(3, 6), pl.ds(rows, 3)]
         return [
-            remote(edge_tile.at[edge], strip_in, first_slot, (group, row_index, c)),
-            remote(edge_left.at[edge], corner_in.at[corners + 1], first_slot + 1, (group, row_index, west)),
-            remote(edge_right.at[edge], corner_in.at[corners], first_slot + 2, (group, row_index, east)),
-            remote(guide_send.at[edge], guide_out.at[guide_slot], first_slot + 3, (group, row_index, c)),
+            remote(strip, rows_in.at[edge, pl.ds(3, 6)], first_slot, (g, row_index, c)),
+            remote(guide_out.at[1], guide_out.at[guide_slot], first_slot + 1, (g, row_index, c)),
         ]
 
-    upward = to_row(0, group_up, r - 1, bottom_in, 2, 2, 2)
-    downward = to_row(1, group_down, r + 1, top_in, 0, 0, 6)
+    upward = to_row(r - 1, 0, 1, 2, 2)
+    downward = to_row(r + 1, 5, 0, 0, 4)
+
+    def across(edge):
+        def copy(src, dst, slot, peer):
+            return pltpu.make_async_remote_copy(
+                src_ref=src,
+                dst_ref=dst,
+                send_sem=edge_send.at[edge, slot],
+                recv_sem=edge_recv.at[edge, slot],
+                device_id=peer,
+                device_id_type=MESH,
+            )
+
+        mine, wests, easts = rows_in.at[edge], to_west.at[edge], to_east.at[edge]
+        in_east, in_west, two = from_east.at[edge], from_west.at[edge], pl.ds(1, 2)
+        level = [
+            copy(wests, in_east.at[two], 0, (g, r, west)),
+            copy(easts, in_west.at[two], 1, (g, r, east)),
+        ]
+        onward = [
+            copy(mine.at[pl.ds(6, 3)], mine.at[pl.ds(0, 3)], 2, (g + 1, r, c)),
+            copy(wests.at[1], in_east.at[0], 3, (g + 1, r, west)),
+            copy(easts.at[1], in_west.at[0], 4, (g + 1, r, east)),
+        ]
+        back = [
+            copy(mine.at[pl.ds(3, 3)], mine.at[pl.ds(9, 3)], 5, (g - 1, r, c)),
+            copy(wests.at[0], in_east.at[3], 6, (g - 1, r, west)),
+            copy(easts.at[0], in_west.at[3], 7, (g - 1, r, east)),
+        ]
+        return level, onward, back
+
+    edges = [across(0), across(1)]
+
+    def pass_on(edge):
+        values = [rows_in[edge, 3 + f].astype(f32) for f in range(6)]
+        for part in range(2):
+            near = values[3 * part : 3 * part + 3]
+            spare = jnp.zeros((3, 4, 128), f32)
+            to_west[edge, part] = jnp.concatenate([v[:, 0:4] for v in near] + [spare], axis=1).astype(half)
+            to_east[edge, part] = jnp.concatenate([v[:, 12:16] for v in near] + [spare], axis=1).astype(half)
+        level, onward, back = edges[edge]
+        start(level)
+        pl.when(has_next)(lambda: start(onward))
+        pl.when(has_prev)(lambda: start(back))
+
+    def passed(edge, done):
+        level, onward, back = edges[edge]
+        done(level)
+        if done is landed:
+            pl.when(has_prev)(lambda: done(onward))
+            pl.when(has_next)(lambda: done(back))
+        else:
+            pl.when(has_next)(lambda: done(onward))
+            pl.when(has_prev)(lambda: done(back))
 
     def start(copies):
         for copy in copies:
@@ -497,6 +528,10 @@
 
     pl.when(has_up)(lambda: start(upward))
     pl.when(has_down)(lambda: start(downward))
+    for line in range(8):
+        near = [tile[f, line].astype(f32) for f in range(12)]
+        left_send[line] = jnp.concatenate([v[0:4] for v in near], axis=0).astype(half)
+        right_send[line] = jnp.concatenate([v[12:16] for v in near], axis=0).astype(half)
     start(sideways)
 
     loads[1].wait()
@@ -504,14 +539,13 @@
     loads[2].wait()
     taps_in_lanes(second_ref, taps2)
 
-    def assemble(first_row, count, real, own, left, right):
+    def assemble(first_row, count, real, own, left, right, per):
         col = lax.broadcasted_iota(jnp.int32, (count, 32, 128), 1) + (16 * c - 8)
         shown = (col >= 0) & (col < 128) & real
-        for quad in range(3):
-            before = left[:, 16 * quad : 16 * (quad + 1)].astype(f32)
-            after = right[:, 16 * quad : 16 * (quad + 1)].astype(f32)
-            for k in range(4):
-                f, eight = 4 * quad + k, slice(8 * (k // 2), 8 * (k // 2) + 8)
+        for part in range(12 // per):
+            before, after = left(part).astype(f32), right(part).astype(f32)
+            for k in range(per):
+                f, eight = per * part + k, slice(8 * (k // 2), 8 * (k // 2) + 8)
                 one = before[:, eight].reshape(8 * count, 128)
                 two = after[:, eight].reshape(8 * count, 128)
                 if k % 2 == 0:
@@ -519,7 +553,9 @@
                 else:
                     two = pltpu.roll(two, 8 * count - 4, 0)
                 sides = [one.reshape(count, 8, 128), own(f).astype(f32), two.reshape(count, 8, 128)]
-                value = jnp.where(shown, jnp.concatenate(sides, axis=1), 0.0)
+                frame = 6 * g - 3 + f
+                here = shown & (frame >= 0) & (frame < 24)
+                value = jnp.where(here, jnp.concatenate(sides, axis=1), 0.0)
                 cells[f, first_row : first_row + count] = value.astype(half)
 
     row = lax.broadcasted_iota(jnp.int32, (6, 32, 128), 0)
@@ -531,19 +567,43 @@
         return jnp.where((frame >= 0) & (frame < 24), 1.0, 0.0)
 
     landed(sideways)
-    assemble(3, 8, True, lambda f: tile[f], left_in[...], right_in[...])
-
-    @pl.loop(0, 10)
-    def _(f):
+    assemble(
+        3, 8, r >= 0, lambda f: tile[f],
+        lambda part: left_in[:, 16 * part : 16 * (part + 1)],
+        lambda part: right_in[:, 16 * part : 16 * (part + 1)],
+        4,
+    )
+
+    def inner(f):
         value, slope = silu_parts(conv_rows(cells, f, (3,), 6, taps1))
         value = jnp.where(in_cols, value, 0.0) * in_frames(f)
         hidden_out[f, 3:9] = value.astype(half)
         slope1_out[f, 16:112] = slope[:, 8:24].reshape(96, 128)
 
-    pl.when(has_up)(lambda: landed(downward))
-    pl.when(has_down)(lambda: landed(upward))
-    assemble(0, 3, has_up, lambda f: top_in[f], corner_in[0], corner_in[1])
-    assemble(11, 3, has_down, lambda f: bottom_in[f], corner_in[2], corner_in[3])
+    pl.loop(0, 3)(inner)
+
+    @pl.when(has_up)
+    def _():
+        landed(downward)
+        pass_on(0)
+
+    @pl.when(has_down)
+    def _():
+        landed(upward)
+        pass_on(1)
+
+    pl.loop(3, 10)(inner)
+
+    pl.when(has_up)(lambda: passed(0, landed))
+    pl.when(has_down)(lambda: passed(1, landed))
+    for edge, real in ((0, has_up), (1, has_down)):
+        assemble(
+            11 * edge, 3, real,
+            lambda f, edge=edge: rows_in[edge, f],
+            lambda part, edge=edge: from_west[edge, part],
+            lambda part, edge=edge: from_east[edge, part],
+            3,
+        )
     image_row = jnp.where(row < 3, row, row + 6) + (8 * r - 2)
     in_image = in_cols & (image_row >= 0) & (image_row < 64)
 
@@ -631,6 +691,8 @@
     sent(sideways)
     pl.when(has_up)(lambda: sent(upward))
     pl.when(has_down)(lambda: sent(downward))
+    pl.when(has_up)(lambda: passed(0, sent))
+    pl.when(has_down)(lambda: passed(1, sent))
 
 
 def columns_in_lanes(source, frame0, row0, out_ref):
@@ -865,11 +927,10 @@
             vmem((12, 14, 32, 128), half), vmem((10, 12, 32, 128), half),
             vmem((10, 128, 128), f32), vmem((8, 10, 32, 128), f32), dma((3,)), dma((4,)),
             vmem((12, 8, 16, 128), half), vmem((8, 48, 128), half), vmem((8, 48, 128), half),
-            vmem((2, 12, 3, 16, 128), half), vmem((2, 3, 48, 128), half), vmem((2, 3, 48, 128), half),
-            vmem((2, 32, 128), half),
-            vmem((12, 3, 16, 128), half), vmem((12, 3, 16, 128), half),
-            vmem((8, 48, 128), half), vmem((8, 48, 128), half), vmem((4, 3, 48, 128), half),
-            dma((10,)), dma((10,)),
+            vmem((8, 48, 128), half), vmem((8, 48, 128), half), vmem((2, 12, 3, 16, 128), half),
+            vmem((2, 2, 3, 16, 128), half), vmem((2, 2, 3, 16, 128), half),
+            vmem((2, 4, 3, 16, 128), half), vmem((2, 4, 3, 16, 128), half),
+            dma((6,)), dma((6,)), dma((2, 8)), dma((2, 8)),
             vmem((1152, 384), half), vmem((1152, 384), half), vmem((6, 16, 128), half),
             dma((3, 6)), dma((3, 8)), dma(()),
         ],

time: 105 us -> 105 us (level)
    pallas_call x1, Pallas kernels: 27.6 us -> 24.2 us  [perceptual_strip(): pl.pallas_call(perceptual_kernel, out_shape=b16(8, 3, 16, 128), in_specs=...]
    pallas_call x2, Pallas kernels: 72.6 us -> 75.5 us  [talking_call(): pl.pallas_call(kernel, out_shape=tuple(outs), in_specs=places(in_places),...]
where the time goes in v5:
time: 105 us; the launch traced here: 104 us
  Pallas kernels  99.6 us (95%)
  local copies, waits for them, and re-layouts  3.76 us (4%)
    pallas_call x2, Pallas kernels, talking_call(): pl.pallas_call(kernel, out_shape=tuple(outs), in_specs=places(in_places),...  75.5 us
    pallas_call x1, Pallas kernels, perceptual_strip(): pl.pallas_call(perceptual_kernel, out_shape=b16(8, 3, 16, 128), in_specs=...  24.2 us
    unnamed x14, local copies, waits for them, and re-layouts  3.01 us

profile of v5, /device:TPU:32, one launch (start us, length us, event | category | flops | bytes accessed | tf_op | source)
XLA Modules:
  0.0 104.2 jit_solution(1315708472529356112)
XLA Ops:
  0.6 0.0 copy-start.5
  0.6 0.0 copy-start.1
  0.7 0.0 copy-start.3
  0.7 28.8 %shard_map.95 = (bf16[8,10,32,128]{3,2,1,0:T(8,128)(2,1)}, bf16[8,10,32,128]{3,2,1,0:T(8,128)(2,1)}, f32[6,128,128]{2,1,0:T(8,128)}, f32[8,10,32,128]{3,2,1,0:T(...) custom-call(bf16[24,8,16,128]{3,2,1,0:T(8,128)(2,1)} %bitcast.14, ...), custom_call_target="tpu_custom_call" | custom-call | tf_op jit(solution)/shard_map/pallas_call | solution.py:899
  29.5 0.0 copy-done.5
  29.5 0.1 pad_add_fusion
  29.7 0.0 copy-done.1
  29.7 0.0 copy-done.3
  29.7 0.0 copy-start.2
  29.7 0.9 copy-done.2
  30.6 0.0 copy-start.4
  30.6 0.7 copy-done.4
  31.3 24.2 %shard_map.96.pixel_ref = bf16[8,3,16,128]{3,2,1,0:T(8,128)(2,1)S(1)} custom-call(bf16[3,8,16,128]{3,2,1,0:T(8,128)(2,1)S(1)} %copy-done.2, bf16[3,32,128]{2,1,0:T(8,128)(2,1)S(1)} %copy-done.4, bf16[72,128]{1,0:T(8,128)(2,1)S(1)} %pad_bitcast_fusion.1.w1_ref, bf16[64,576]{1,0:T(8,128)(2,1)S(1)} %bitcast.13, bf16[576,128]{1,0:T(8,128)(2,1)S(1)} %copy-done.1, ...), custom_call_target="tpu_custom_call" | custom-call | tf_op jit(solution)/shard_map/pallas_call | solution.py:276
  55.5 0.0 copy-start
  55.5 0.6 copy-done
  56.1 46.6 %shard_map.97 = f32[2,16,128]{2,1,0:T(8,128)} custom-call(bf16[8,3,16,128]{3,2,1,0:T(8,128)(2,1)} %copy-done, bf16[8,10,32,128]{3,2,1,0:T(8,128)(2,1)} %get-tuple-element.10.cells_hbm, bf16[8,10,32,128]{3,2,1,0:T(8,128)(2,1)} %get-tuple-element.11.hidden_hbm, f32[6,128,128]{2,1,0:T(8,128)} %get-tuple-element.12.slope1_hbm, ...), custom_call_target="tpu_custom_call" | custom-call | tf_op jit(solution)/shard_map/pallas_call | solution.py:899
  102.8 0.7 slice_bitcast_fusion
  103.5 0.7 dynamic-slice_reduce_fusion
  (5 shorter events, 0.1 us)
Async XLA Ops:
  0.6 28.9 %copy-start.5 = (bf16[27,64]{1,0:T(8,128)(2,1)S(1)}, bf16[27,64]{1,0:T(8,128)(2,1)}, u32[]{:S(2)}) copy-start(bf16[27,64]{1,0:T(8,128)(2,1)} %param.13) | copy-start | bytes 10372
  0.6 29.0 %copy-start.1 = (bf16[576,128]{1,0:T(8,128)(2,1)S(1)}, bf16[576,128]{1,0:T(8,128)(2,1)}, u32[]{:S(2)}) copy-start(bf16[576,128]{1,0:T(8,128)(2,1)} %vgg_third_ref.1) | copy-start | bytes 442372
  0.7 29.0 %copy-start.3 = (bf16[576,64]{0,1:T(8,128)(2,1)S(1)}, bf16[576,64]{0,1:T(8,128)(2,1)}, u32[]{:S(2)}) copy-start(bf16[576,64]{0,1:T(8,128)(2,1)} %param.14) | copy-start | bytes 221188
  29.7 0.9 copy-start.2
  30.6 0.7 copy-start.4
  55.5 0.6 copy-start

commit v6 on v5

--- a/solution.py
+++ b/solution.py
@@ -369,11 +369,11 @@
 
 def forward_kernel(
     video_hbm, target_ref, first_hbm, second_hbm, rgb_ref,
-    cells_hbm, hidden_hbm, slope1_hbm, slope2_hbm, near_out, guide_out,
+    cells_hbm, hidden_hbm, slope1_hbm, slope2_hbm, turned_hbm, near_out, guide_out,
     video, first_ref, second_ref, rgb16, cells, hidden_out, slope1_out, slope2_out, load_sem, store_sem,
     tile, left_send, right_send, left_in, right_in, rows_in, to_west, to_east, from_east, from_west,
     halo_send, halo_recv, edge_send, edge_recv,
-    taps1, taps2, colours, send_sem, recv_sem, own_sem,
+    taps1, taps2, turned, cell_columns, hidden_columns, colours, send_sem, recv_sem, own_sem,
 ):
     loads = [
         pltpu.make_async_copy(video_hbm, video, load_sem.at[0]),
@@ -617,12 +617,13 @@
         slope1_out[f, 112:128] = slope[3, 8:24]
 
     stores = [
-        pltpu.make_async_copy(cells.at[pl.ds(2, 8), pl.ds(2, 10)], cells_hbm, store_sem.at[0]),
-        pltpu.make_async_copy(hidden_out.at[pl.ds(1, 8), pl.ds(1, 10)], hidden_hbm, store_sem.at[1]),
-        pltpu.make_async_copy(slope1_out.at[pl.ds(2, 6)], slope1_hbm, store_sem.at[2]),
-        pltpu.make_async_copy(slope2_out, slope2_hbm, store_sem.at[3]),
+        pltpu.make_async_copy(slope1_out.at[pl.ds(2, 6)], slope1_hbm, store_sem.at[0]),
+        pltpu.make_async_copy(slope2_out, slope2_hbm, store_sem.at[1]),
+        pltpu.make_async_copy(hidden_columns, hidden_hbm, store_sem.at[2]),
+        pltpu.make_async_copy(cell_columns, cells_hbm, store_sem.at[3]),
+        pltpu.make_async_copy(turned, turned_hbm, store_sem.at[4]),
     ]
-    start(stores[:3])
+    stores[0].start()
 
     def target(step, slot):
         frame = 6 * g + slot
@@ -678,7 +679,13 @@
     def _(end):
         slope2_out[7 * end] = silu_parts(conv_rows(hidden_out, 7 * end, (0,), 10, taps2))[1]
 
+    stores[1].start()
+    columns_in_lanes(hidden_out, 1, 1, hidden_columns)
+    stores[2].start()
+    columns_in_lanes(cells, 2, 2, cell_columns)
     stores[3].start()
+    turned_taps(second_ref, turned)
+    stores[4].start()
     sources(arrive)
 
     @pl.loop(0, 6)
@@ -705,15 +712,15 @@
             out_ref[f, :, :, 128 * k : 128 * (k + 1)] = own.astype(jnp.bfloat16)
 
 
-def weight_terms(columns, delta, terms):
-    @pl.loop(0, 9)
+def weight_terms(columns, delta, terms, low, high):
+    @pl.loop(low, high)
     def _(q):
         cells = columns[pl.ds(q // 3, 6), pl.ds(lax.rem(q, 3), 8)].reshape(768, 384)
         terms[pl.ds(pl.multiple_of(384 * q, 384), 384)] = transposed_dot(cells, delta[...])
 
 
-def by_chip(terms, out_ref, which):
-    @pl.loop(0, 8)
+def by_chip(terms, out_ref, which, low, high):
+    @pl.loop(low, high)
     def _(z):
         for chip in range(16):
             start = 432 * z + 27 * chip
@@ -722,9 +729,9 @@
 
 
 def backward_kernel(
-    pixel_ref, cells_hbm, hidden_hbm, slope1_hbm, slope2_hbm, second_hbm, rgb_ref, out_ref,
-    cells_ref, hidden_ref, slope1_ref, slope2_ref, second_ref, rgb16, load_sem,
-    taps, columns, field, delta, terms,
+    pixel_ref, cells_hbm, hidden_hbm, slope1_hbm, slope2_hbm, turned_hbm, rgb_ref, first_out, second_out,
+    cells_ref, hidden_ref, slope1_ref, slope2_ref, taps, rgb16, load_sem,
+    field, delta, terms,
     sending, core_in, held, x_in, y_in, mid_x, mid_y, yy_in, xx_in, last, z_in, send_sem, recv_sem,
 ):
     g, r, c = position()
@@ -732,7 +739,7 @@
         pltpu.make_async_copy(src, dst, load_sem.at[k])
         for k, (src, dst) in enumerate(
             (
-                (second_hbm, second_ref), (slope2_hbm, slope2_ref), (hidden_hbm, hidden_ref),
+                (slope2_hbm, slope2_ref), (hidden_hbm, hidden_ref), (turned_hbm, taps),
                 (slope1_hbm, slope1_ref), (cells_hbm, cells_ref),
             )
         )
@@ -780,34 +787,41 @@
             total += received[k].astype(f32)
         return total.astype(half)
 
-    def to_partner(which):
-        return send(sending.at[which, other], core_in.at[which], which, 0, partner)
-
-    def first_step(which, copy):
+    def to_partner(which, part):
+        some = pl.ds(4 * part, 4)
+        return send(sending.at[which, other, some], core_in.at[which, some], which, 20 * part, partner)
+
+    def first_step(which, part, copy):
         copy.wait()
 
-        @pl.loop(0, 8)
+        @pl.loop(4 * part, 4 * part + 4)
         def _(k):
             pair = sending[which, core, k].astype(f32) + core_in[which, k].astype(f32)
             held[which, k] = pair.astype(half)
 
-        low, high = held.at[which, pl.ds(0, 4)], held.at[which, pl.ds(4, 4)]
-        copies = []
-        for s in (1, 2, 3):
-            copies.append(send(low.at[:, lax.rem(x + s, 4)], x_in.at[which, s - 1], which, s, at_x(s)))
-            copies.append(send(high.at[:, :, lax.rem(y + s, 4)], y_in.at[which, s - 1], which, 3 + s, at_y(s)))
-        return copies
-
-    def second_step(which, copies):
+        some = held.at[which, pl.ds(4 * part, 4)]
+        if part == 0:
+            return [
+                send(some.at[:, lax.rem(x + s, 4)], x_in.at[which, s - 1], which, s, at_x(s)) for s in (1, 2, 3)
+            ]
+        return [
+            send(some.at[:, :, lax.rem(y + s, 4)], y_in.at[which, s - 1], which, 3 + s, at_y(s)) for s in (1, 2, 3)
+        ]
+
+    def second_step(which, part, copies):
         for copy in copies:
             copy.wait()
-        mid_x[which] = summed(held[which, 0:4, x], [x_in[which, k] for k in range(3)])
+        if part == 0:
+            mid_x[which] = summed(held[which, 0:4, x], [x_in[which, k] for k in range(3)])
+            return [
+                send(mid_x.at[which, :, lax.rem(y + s, 4)], yy_in.at[which, s - 1], which, 6 + s, at_y(s))
+                for s in (1, 2, 3)
+            ]
         mid_y[which] = summed(held[which, 4:8, :, y], [y_in[which, k] for k in range(3)])
-        after = []
-        for s in (1, 2, 3):
-            after.append(send(mid_x.at[which, :, lax.rem(y + s, 4)], yy_in.at[which, s - 1], which, 6 + s, at_y(s)))
-            after.append(send(mid_y.at[which, :, lax.rem(x + s, 4)], xx_in.at[which, s - 1], which, 9 + s, at_x(s)))
-        return after
+        return [
+            send(mid_y.at[which, :, lax.rem(x + s, 4)], xx_in.at[which, s - 1], which, 9 + s, at_x(s))
+            for s in (1, 2, 3)
+        ]
 
     def third_step(which, copies):
         for copy in copies:
@@ -819,19 +833,20 @@
             for s in range(1, 8)
         ]
 
-    def result(which, copies):
+    def result(which, copies, out_ref):
         for copy in copies:
             copy.wait()
         total = last[which, z].astype(f32)
         for k in range(7):
             total += z_in[which, k].astype(f32)
-        out_ref[which] = total
+        turned = pltpu.roll(total, 64, 1)
+        low_half = lax.broadcasted_iota(jnp.int32, (16, 128), 1) < 64
+        shifted = jnp.where(low_half, turned, pltpu.roll(turned, 15, 0))
+        out_ref[...] = jnp.where(core == 1, shifted, total)
 
     rgb16[...] = jnp.zeros((16, 128), f32)
     rgb16[0:3] = rgb_ref[...].astype(f32)
     loads[0].wait()
-    turned_taps(second_ref, taps)
-    loads[1].wait()
 
     lane = lax.broadcasted_iota(jnp.int32, (8, 128), 1)
     col = lax.rem(lane, 32) + (16 * c - 8)
@@ -857,34 +872,43 @@
         own = field[f + 1, 1:9].astype(f32)[:, 8:24].reshape(128, 128).astype(half)
         delta[pl.ds(pl.multiple_of(128 * f, 128), 128)] = own
 
+    loads[1].wait()
+    terms[pl.ds(3456, 8)] = jnp.zeros((8, 128), f32)
+    weight_terms(hidden_ref, delta, terms, 0, 5)
+    by_chip(terms, sending, 1, 0, 4)
+    pl.semaphore_wait(barrier, len(everyone))
+    swap_low = to_partner(1, 0)
+    weight_terms(hidden_ref, delta, terms, 5, 9)
+    by_chip(terms, sending, 1, 4, 8)
+    swap_high = to_partner(1, 1)
+    second_low = first_step(1, 0, swap_low)
     loads[2].wait()
-    columns_in_lanes(hidden_ref, 0, 0, columns)
-    terms[pl.ds(3456, 8)] = jnp.zeros((8, 128), f32)
-    weight_terms(columns, delta, terms)
-    by_chip(terms, sending, 1)
-    pl.semaphore_wait(barrier, len(everyone))
-    swap_second = to_partner(1)
     loads[3].wait()
 
-    @pl.loop(0, 6)
-    def _(f):
+    def back_frame(f):
         back = conv_rows(field, f, (0,), 8, taps)[:, 8:24].reshape(128, 128)
         value = (back * slope1_ref[f]).astype(half)
         delta[pl.ds(pl.multiple_of(128 * f, 128), 128)] = value
 
-    moves_second = first_step(1, swap_second)
+    pl.loop(0, 2)(back_frame)
+    second_high = first_step(1, 1, swap_high)
+    pl.loop(2, 6)(back_frame)
     loads[4].wait()
-    columns_in_lanes(cells_ref, 0, 0, columns)
-    weight_terms(columns, delta, terms)
-    moves_second = second_step(1, moves_second)
-    by_chip(terms, sending, 0)
-    swap_first = to_partner(0)
-    moves_second = third_step(1, moves_second)
-    moves_first = first_step(0, swap_first)
-    result(1, moves_second)
-    moves_first = second_step(0, moves_first)
-    moves_first = third_step(0, moves_first)
-    result(0, moves_first)
+    second_low = second_step(1, 0, second_low)
+    weight_terms(cells_ref, delta, terms, 0, 5)
+    by_chip(terms, sending, 0, 0, 4)
+    swap_low = to_partner(0, 0)
+    second_high = second_step(1, 1, second_high)
+    weight_terms(cells_ref, delta, terms, 5, 9)
+    by_chip(terms, sending, 0, 4, 8)
+    swap_high = to_partner(0, 1)
+    first_low = first_step(0, 0, swap_low)
+    moves_second = third_step(1, second_low + second_high)
+    first_high = first_step(0, 1, swap_high)
+    result(1, moves_second, second_out)
+    first_low = second_step(0, 0, first_low)
+    first_high = second_step(0, 1, first_high)
+    result(0, third_step(0, first_low + first_high), first_out)
 
 
 def f32_shape(*shape):
@@ -912,26 +936,28 @@
     g, r, c = position()
     channels = dec_input.shape[-1]
     half, f32, dma, vmem = jnp.bfloat16, jnp.float32, pltpu.SemaphoreType.DMA, pltpu.VMEM
-    cells, hidden, slope1, slope2, colour_near, guide_near = talking_call(
+    cells, hidden, slope1, slope2, turned, colour_near, guide_near = talking_call(
         forward_kernel,
         3,
         58,
         "hvhhv",
-        "hhhhvv",
+        "hhhhhvv",
         (
-            b16(8, 10, 32, 128), b16(8, 10, 32, 128), f32_shape(6, 128, 128), f32_shape(8, 10, 32, 128),
+            b16(8, 10, 16, 384), b16(8, 10, 16, 384), f32_shape(6, 128, 128), f32_shape(8, 10, 32, 128),
+            b16(1152, 384),
             b16(3, 8, 16, 128), b16(3, 32, 128),
         ),
         [
             vmem((24, 8, 16, 128), half), vmem((3456, 128), half), vmem((3456, 128), half), vmem((16, 128), f32),
             vmem((12, 14, 32, 128), half), vmem((10, 12, 32, 128), half),
-            vmem((10, 128, 128), f32), vmem((8, 10, 32, 128), f32), dma((3,)), dma((4,)),
+            vmem((10, 128, 128), f32), vmem((8, 10, 32, 128), f32), dma((3,)), dma((5,)),
             vmem((12, 8, 16, 128), half), vmem((8, 48, 128), half), vmem((8, 48, 128), half),
             vmem((8, 48, 128), half), vmem((8, 48, 128), half), vmem((2, 12, 3, 16, 128), half),
             vmem((2, 2, 3, 16, 128), half), vmem((2, 2, 3, 16, 128), half),
             vmem((2, 4, 3, 16, 128), half), vmem((2, 4, 3, 16, 128), half),
             dma((6,)), dma((6,)), dma((2, 8)), dma((2, 8)),
-            vmem((1152, 384), half), vmem((1152, 384), half), vmem((6, 16, 128), half),
+            vmem((1152, 384), half), vmem((1152, 384), half), vmem((1152, 384), half),
+            vmem((8, 10, 16, 384), half), vmem((8, 10, 16, 384), half), vmem((6, 16, 128), half),
             dma((3, 6)), dma((3, 8)), dma(()),
         ],
         dec_input.reshape(24, 8, 16, channels), target, conv_first, conv_second, rgb_weight,
@@ -944,13 +970,11 @@
         1,
         58,
         "vhhhhhv",
-        "v",
-        (f32_shape(2, 16, 128),),
+        "vv",
+        (f32_shape(16, 128), f32_shape(16, 128)),
         [
-            vmem((8, 10, 32, 128), half), vmem((8, 10, 32, 128), half), vmem((6, 128, 128), f32),
-            vmem((8, 10, 32, 128), f32), vmem((3456, 128), half), vmem((16, 128), f32), dma((5,)),
-            pltpu.VMEM((1152, 384), half),
-            pltpu.VMEM((8, 10, 16, 384), half),
+            vmem((8, 10, 16, 384), half), vmem((8, 10, 16, 384), half), vmem((6, 128, 128), f32),
+            vmem((8, 10, 32, 128), f32), vmem((1152, 384), half), vmem((16, 128), f32), dma((5,)),
             pltpu.VMEM((8, 10, 32, 128), half),
             pltpu.VMEM((768, 128), half),
             pltpu.VMEM((3464, 128), jnp.float32),
@@ -965,14 +989,12 @@
             pltpu.VMEM((2, 3, 4, 16, 128), half),
             pltpu.VMEM((2, 8, 16, 128), half),
             pltpu.VMEM((2, 7, 16, 128), half),
-            dma((2, 20)),
-            dma((2, 20)),
+            dma((2, 21)),
+            dma((2, 21)),
         ],
-        pixels, cells, hidden, slope1, slope2, conv_second, rgb_weight,
-    )[0]
-    flat = sums[:, :14].reshape(2, 14 * 128)
-    own_sums = lax.dynamic_slice_in_dim(flat, lax.rem(c, 2) * 64, 1728, axis=1)
-    return own_sums[0], own_sums[1]
+        pixels, cells, hidden, slope1, slope2, turned, rgb_weight,
+    )
+    return sums[0].reshape(2048)[:1728], sums[1].reshape(2048)[:1728]
 
 
 def solution(mesh):

time: 105 us -> 105 us (level)
  local copies, waits for them, and re-layouts: 3.76 us -> 5.61 us
  Pallas kernels: 99.6 us -> 98.5 us
    unnamed x14 -> x12, local copies, waits for them, and re-layouts: 3.01 us -> 4.87 us
where the time goes in v6:
time: 105 us
  Pallas kernels  98.5 us (94%)
  local copies, waits for them, and re-layouts  5.61 us (5%)
    pallas_call x2, Pallas kernels, talking_call(): pl.pallas_call(kernel, out_shape=tuple(outs), in_specs=places(in_places),...  75.1 us
    pallas_call x1, Pallas kernels, perceptual_strip(): pl.pallas_call(perceptual_kernel, out_shape=b16(8, 3, 16, 128), in_specs=...  23.5 us
    unnamed x12, local copies, waits for them, and re-layouts  4.87 us

profile of v6, /device:TPU:32, one launch (start us, length us, event | category | flops | bytes accessed | tf_op | source)
XLA Modules:
  0.0 104.9 jit_solution(1497476347713199378)
XLA Ops:
  0.6 0.7 reshape.23
  1.4 0.1 pad_add_fusion
  1.4 0.0 copy-start.1
  1.5 0.0 copy-start.3
  1.5 29.7 %shard_map.95 = (bf16[8,10,16,384]{3,2,1,0:T(8,128)(2,1)}, bf16[8,10,16,384]{3,2,1,0:T(8,128)(2,1)}, f32[6,128,128]{2,1,0:T(8,128)}, f32[8,10,32,128]{3,2,1,0:T(...) custom-call(bf16[24,8,16,128]{3,2,1,0:T(8,128)(2,1)} %bitcast.13, ...), custom_call_target="tpu_custom_call" | custom-call | tf_op jit(solution)/shard_map/pallas_call | solution.py:923
  31.2 0.0 copy-done.1
  31.2 0.0 copy-done.3
  31.2 0.0 copy-start.2
  31.2 0.9 copy-done.2
  32.1 0.0 copy-start.4
  32.1 0.7 copy-done.4
  32.9 23.5 %shard_map.96.pixel_ref = bf16[8,3,16,128]{3,2,1,0:T(8,128)(2,1)S(1)} custom-call(bf16[3,8,16,128]{3,2,1,0:T(8,128)(2,1)S(1)} %copy-done.2, bf16[3,32,128]{2,1,0:T(8,128)(2,1)S(1)} %copy-done.4, bf16[72,128]{1,0:T(8,128)(2,1)S(1)} %pad_bitcast_fusion.1.w1_ref, bf16[64,576]{1,0:T(8,128)(2,1)S(1)} %bitcast.12, bf16[576,128]{1,0:T(8,128)(2,1)S(1)} %copy-done.1, ...), custom_call_target="tpu_custom_call" | custom-call | tf_op jit(solution)/shard_map/pallas_call | solution.py:276
  56.3 0.0 copy-start
  56.4 0.6 copy-done
  57.0 45.3 %shard_map.97 = (f32[16,128]{1,0:T(8,128)}, f32[16,128]{1,0:T(8,128)}) custom-call(bf16[8,3,16,128]{3,2,1,0:T(8,128)(2,1)} %copy-done, bf16[8,10,16,384]{3,2,1,0:T(8,128)(2,1)} %get-tuple-element.13.cells_hbm, bf16[8,10,16,384]{3,2,1,0:T(8,128)(2,1)} %get-tuple-element.14.hidden_hbm, f32[6,128,128]{2,1,0:T(8,128)} %get-tuple-element.15.slope1_hbm, ...), custom_call_target="tpu_custom_call" | custom-call | tf_op jit(solution)/shard_map/pallas_call | solution.py:923
  102.3 1.3 %copy.12 = f32[1728]{0:T(1024)} copy(f32[1728]{0:T(1024)} %bitcast.15) | data formatting | bytes 13824
  103.6 1.3 %copy.13 = f32[1728]{0:T(1024)} copy(f32[1728]{0:T(1024)} %bitcast.14) | data formatting | bytes 13824
  (3 shorter events, 0.0 us)
Async XLA Ops:
  1.4 29.8 %copy-start.1 = (bf16[576,128]{1,0:T(8,128)(2,1)S(1)}, bf16[576,128]{1,0:T(8,128)(2,1)}, u32[]{:S(2)}) copy-start(bf16[576,128]{1,0:T(8,128)(2,1)} %vgg_third_ref.1) | copy-start | bytes 442372
  1.5 29.8 %copy-start.3 = (bf16[576,64]{0,1:T(8,128)(2,1)S(1)}, bf16[576,64]{0,1:T(8,128)(2,1)}, u32[]{:S(2)}) copy-start(bf16[576,64]{0,1:T(8,128)(2,1)} %param.14) | copy-start | bytes 221188
  31.2 0.9 copy-start.2
  32.1 0.7 copy-start.4
  56.3 0.7 copy-start

commit v7 on v6

--- a/solution.py
+++ b/solution.py
@@ -66,8 +66,8 @@
 
 
 def perceptual_kernel(
-    near_ref, guide_ref, w1_ref, vgg_second_ref, vgg_third_ref, w1_back_ref, out_ref,
-    planes_ref, guides,
+    near_hbm, guide_hbm, vgg_first_ref, vgg_second_ref, vgg_third_ref, out_ref,
+    near_ref, guide_ref, load_sem, first32, w1_ref, w1_back32, w1_back_ref, planes_ref, guides,
     taps, act1, slope1, pooled, delta3, diff2, slope2, delta2, delta1, tmp, pixels, strip,
     w2_ref, w3_ref, w3_back_ref, w2_back_ref, send_sem, recv_sem, own_sem,
 ):
@@ -96,9 +96,27 @@
     def greet(step, slot, source):
         pl.semaphore_signal(barrier, inc=1, device_id=source, device_id_type=MESH)
 
+    loads = [
+        pltpu.make_async_copy(near_hbm, near_ref, load_sem.at[0]),
+        pltpu.make_async_copy(guide_hbm, guide_ref, load_sem.at[1]),
+    ]
+    for load in loads:
+        load.start()
     sources(greet)
+    weight = vgg_first_ref[...].astype(jnp.float32)
+    first32[...] = jnp.zeros((72, 128), jnp.float32)
+    w1_back32[...] = jnp.zeros((8, 1152), jnp.float32)
+    for t in range(9):
+        block = weight[3 * t : 3 * t + 3]
+        first32[8 * t : 8 * t + 3, 0:64] = block
+        first32[8 * t + 3 : 8 * t + 6, 64:128] = block
+        w1_back32[0:3, 128 * (8 - t) : 128 * (8 - t) + 64] = block
+    w1_ref[...] = first32[...].astype(jnp.bfloat16)
+    w1_back_ref[...] = w1_back32[...].astype(jnp.bfloat16)
     lay_out_perceptual(vgg_second_ref, vgg_third_ref, w2_ref, w3_ref, w3_back_ref, w2_back_ref)
     row0 = 8 * r - 8
+    for load in loads:
+        load.wait()
     kind = lax.broadcasted_iota(jnp.int32, (8, 128), 0)
     block = lax.broadcasted_iota(jnp.int32, (8, 128), 1) // 16
     for part in range(3):
@@ -128,7 +146,7 @@
         return jnp.where(shown(row), value, 0.0)
 
     def first_rows(low, high, slope_too):
-        @pl.loop(low, high)
+        @pl.loop(low, high, unroll=2)
         def _(i):
             cells = taps[pl.ds(i, 3)].reshape(72, 128).astype(jnp.bfloat16)
             value, slope = gelu_both(transposed_dot(cells, w1_ref[...]), slope_too)
@@ -141,7 +159,7 @@
     first_rows(16, 22, False)
 
     def second_rows(low, high, slope_too):
-        @pl.loop(low, high)
+        @pl.loop(low, high, unroll=2)
         def _(p):
             plane = dot32(three_rows(act1, 2 * p, 2), w2_ref[...])
             value, slope = gelu_both(plane, slope_too)
@@ -158,7 +176,7 @@
     second_rows(2, 8, True)
     second_rows(8, 10, False)
 
-    @pl.loop(0, 4)
+    @pl.loop(0, 4, unroll=2)
     def _(half):
         j = 2 * half
         plane = dot32(three_rows(pooled, j, 2), w3_ref[...])
@@ -168,7 +186,7 @@
         delta3[j] = side_by_side(kept(2 * j + 4, delta[:64]))
         delta3[j + 1] = side_by_side(kept(2 * j + 6, delta[64:]))
 
-    @pl.loop(0, 6)
+    @pl.loop(0, 6, unroll=3)
     def _(m):
         grad = 0.25 * dot32(three_rows(delta3, m, 1), w3_back_ref[...])
         tmp[pl.ds(0, 64, 2)] = grad
@@ -178,7 +196,7 @@
             delta = (spread + diff2[2 * m + k]) * slope2[2 * m + k]
             delta2[2 * m + k] = side_by_side(kept(2 * m + 6, delta))
 
-    @pl.loop(0, 5)
+    @pl.loop(0, 5, unroll=5)
     def _(half):
         n = 2 * half
         grad = dot32(three_rows(delta2, n, 2), w2_back_ref[...])
@@ -186,7 +204,7 @@
             delta = grad[128 * k : 128 * (k + 1)] * slope1[n + k]
             delta1[n + k] = side_by_side(kept(n + k + 7, delta))
 
-    @pl.loop(0, 8)
+    @pl.loop(0, 8, unroll=4)
     def _(q):
         grad = lax.dot_general(
             w1_back_ref[...],
@@ -259,26 +277,21 @@
     targets(finish)
 
 
-def two_blocks(weight):
-    _, i, o = weight.shape
-    return jnp.pad(weight, ((0, 0), (0, i), (0, o))) + jnp.pad(weight, ((0, 0), (i, 0), (o, 0)))
-
-
-def first_weights(vgg_first):
-    first = vgg_first.reshape(9, 3, 64)
-    w1 = jnp.pad(two_blocks(first), ((0, 0), (0, 2), (0, 0))).reshape(72, 128)
-    w1_back = jnp.pad(jnp.transpose(first[::-1], (1, 0, 2)), ((0, 5), (0, 0), (0, 64))).reshape(8, 1152)
-    return w1, w1_back
-
-
-def perceptual_strip(near, guides, first, others):
+def perceptual_strip(near, guides, *weights):
     f32, half = jnp.float32, jnp.bfloat16
     return pl.pallas_call(
         perceptual_kernel,
         out_shape=b16(8, 3, 16, 128),
-        in_specs=in_vmem(6),
+        in_specs=places("hhvvv"),
         out_specs=in_vmem(1)[0],
         scratch_shapes=[
+            pltpu.VMEM((3, 8, 16, 128), half),
+            pltpu.VMEM((3, 32, 128), half),
+            pltpu.SemaphoreType.DMA((2,)),
+            pltpu.VMEM((72, 128), f32),
+            pltpu.VMEM((72, 128), half),
+            pltpu.VMEM((8, 1152), f32),
+            pltpu.VMEM((8, 1152), half),
             pltpu.VMEM((24, 8, 128), f32),
             pltpu.VMEM((32, 128), f32),
             pltpu.VMEM((24, 24, 128), f32),
@@ -302,9 +315,9 @@
             pltpu.SemaphoreType.DMA(()),
         ],
         compiler_params=pltpu.CompilerParams(
-            collective_id=4, has_side_effects=True, vmem_limit_bytes=24 * 2**20
+            collective_id=4, has_side_effects=True, vmem_limit_bytes=58 * 2**20
         ),
-    )(near, guides, first[0], *others, first[1])
+    )(near, guides, *weights)
 
 
 def taps_in_lanes(weight_ref, out_ref):
@@ -339,12 +352,12 @@
 
 
 def silu_parts(preact):
-    gate = 1.0 / (1.0 + jnp.exp(-preact))
+    gate = 0.5 * (1.0 + jnp.tanh(0.5 * preact))
     return preact * gate, gate * (1.0 + preact * (1.0 - gate))
 
 
 def on_rows(r, do):
-    for step in (-1, 0, 1):
+    for step in (-1, 1, 0):
         pl.when((r + step >= 0) & (r + step < 8))(functools.partial(do, step))
 
 
@@ -580,7 +593,7 @@
         hidden_out[f, 3:9] = value.astype(half)
         slope1_out[f, 16:112] = slope[:, 8:24].reshape(96, 128)
 
-    pl.loop(0, 3)(inner)
+    pl.loop(0, 2, unroll=2)(inner)
 
     @pl.when(has_up)
     def _():
@@ -592,7 +605,7 @@
         landed(upward)
         pass_on(1)
 
-    pl.loop(3, 10)(inner)
+    pl.loop(2, 10, unroll=2)(inner)
 
     pl.when(has_up)(lambda: passed(0, landed))
     pl.when(has_down)(lambda: passed(1, landed))
@@ -607,7 +620,7 @@
     image_row = jnp.where(row < 3, row, row + 6) + (8 * r - 2)
     in_image = in_cols & (image_row >= 0) & (image_row < 64)
 
-    @pl.loop(0, 10)
+    @pl.loop(0, 10, unroll=2)
     def _(f):
         value, slope = silu_parts(conv_rows(cells, f, (0, 9), 3, taps1))
         value = (jnp.where(in_image, value, 0.0) * in_frames(f)).astype(half)
@@ -729,8 +742,8 @@
 
 
 def backward_kernel(
-    pixel_ref, cells_hbm, hidden_hbm, slope1_hbm, slope2_hbm, turned_hbm, rgb_ref, first_out, second_out,
-    cells_ref, hidden_ref, slope1_ref, slope2_ref, taps, rgb16, load_sem,
+    pixel_hbm, cells_hbm, hidden_hbm, slope1_hbm, slope2_hbm, turned_hbm, rgb_ref, out_ref,
+    pixel_ref, cells_ref, hidden_ref, slope1_ref, slope2_ref, taps, rgb16, load_sem,
     field, delta, terms,
     sending, core_in, held, x_in, y_in, mid_x, mid_y, yy_in, xx_in, last, z_in, send_sem, recv_sem,
 ):
@@ -740,7 +753,7 @@
         for k, (src, dst) in enumerate(
             (
                 (slope2_hbm, slope2_ref), (hidden_hbm, hidden_ref), (turned_hbm, taps),
-                (slope1_hbm, slope1_ref), (cells_hbm, cells_ref),
+                (slope1_hbm, slope1_ref), (cells_hbm, cells_ref), (pixel_hbm, pixel_ref),
             )
         )
     ]
@@ -833,7 +846,7 @@
             for s in range(1, 8)
         ]
 
-    def result(which, copies, out_ref):
+    def result(which, copies):
         for copy in copies:
             copy.wait()
         total = last[which, z].astype(f32)
@@ -842,17 +855,18 @@
         turned = pltpu.roll(total, 64, 1)
         low_half = lax.broadcasted_iota(jnp.int32, (16, 128), 1) < 64
         shifted = jnp.where(low_half, turned, pltpu.roll(turned, 15, 0))
-        out_ref[...] = jnp.where(core == 1, shifted, total)
+        out_ref[which] = jnp.where(core == 1, shifted, total)
 
     rgb16[...] = jnp.zeros((16, 128), f32)
     rgb16[0:3] = rgb_ref[...].astype(f32)
     loads[0].wait()
+    loads[5].wait()
 
     lane = lax.broadcasted_iota(jnp.int32, (8, 128), 1)
     col = lax.rem(lane, 32) + (16 * c - 8)
     in_cols = (lane < 96) & (col >= 0) & (col < 128)
 
-    @pl.loop(0, 8)
+    @pl.loop(0, 8, unroll=2)
     def _(f):
         frame = 6 * g - 1 + f
         known = in_cols & (frame >= 0) & (frame < 24)
@@ -890,9 +904,9 @@
         value = (back * slope1_ref[f]).astype(half)
         delta[pl.ds(pl.multiple_of(128 * f, 128), 128)] = value
 
-    pl.loop(0, 2)(back_frame)
+    pl.loop(0, 2, unroll=2)(back_frame)
     second_high = first_step(1, 1, swap_high)
-    pl.loop(2, 6)(back_frame)
+    pl.loop(2, 6, unroll=2)(back_frame)
     loads[4].wait()
     second_low = second_step(1, 0, second_low)
     weight_terms(cells_ref, delta, terms, 0, 5)
@@ -905,10 +919,10 @@
     first_low = first_step(0, 0, swap_low)
     moves_second = third_step(1, second_low + second_high)
     first_high = first_step(0, 1, swap_high)
-    result(1, moves_second, second_out)
+    result(1, moves_second)
     first_low = second_step(0, 0, first_low)
     first_high = second_step(0, 1, first_high)
-    result(0, third_step(0, first_low + first_high), first_out)
+    result(0, third_step(0, first_low + first_high))
 
 
 def f32_shape(*shape):
@@ -962,19 +976,18 @@
         ],
         dec_input.reshape(24, 8, 16, channels), target, conv_first, conv_second, rgb_weight,
     )
-    pixels = perceptual_strip(
-        colour_near, guide_near, first_weights(vgg_first), (vgg_second.T, vgg_third)
-    )
+    pixels = perceptual_strip(colour_near, guide_near, vgg_first, vgg_second.T, vgg_third)
     sums = talking_call(
         backward_kernel,
         1,
         58,
-        "vhhhhhv",
-        "vv",
-        (f32_shape(16, 128), f32_shape(16, 128)),
+        "hhhhhhv",
+        "v",
+        (f32_shape(2, 16, 128),),
         [
+            vmem((8, 3, 16, 128), half),
             vmem((8, 10, 16, 384), half), vmem((8, 10, 16, 384), half), vmem((6, 128, 128), f32),
-            vmem((8, 10, 32, 128), f32), vmem((1152, 384), half), vmem((16, 128), f32), dma((5,)),
+            vmem((8, 10, 32, 128), f32), vmem((1152, 384), half), vmem((16, 128), f32), dma((6,)),
             pltpu.VMEM((8, 10, 32, 128), half),
             pltpu.VMEM((768, 128), half),
             pltpu.VMEM((3464, 128), jnp.float32),
@@ -994,7 +1007,8 @@
         ],
         pixels, cells, hidden, slope1, slope2, turned, rgb_weight,
     )
-    return sums[0].reshape(2048)[:1728], sums[1].reshape(2048)[:1728]
+    flat = sums[0].reshape(2, 2048)[:, :1728]
+    return flat[0], flat[1]
 
 
 def solution(mesh):

time: 105 us -> 96.4 us (0.918)
  Pallas kernels: 98.5 us -> 94.1 us
  local copies, waits for them, and re-layouts: 5.61 us -> 1.37 us
    unnamed x12 -> x1, local copies, waits for them, and re-layouts: 4.87 us -> 0.73 us
    pallas_call x1, Pallas kernels: 23.5 us -> 19.7 us  [perceptual_strip(): pl.pallas_call(perceptual_kernel, out_shape=b16(8, 3, 16, 128), in_specs=...]
where the time goes in v7:
time: 96.4 us; the launch traced here: 96.1 us
  Pallas kernels  94.1 us (98%)
  local copies, waits for them, and re-layouts  1.37 us (1%)
    pallas_call x2, Pallas kernels, talking_call(): pl.pallas_call(kernel, out_shape=tuple(outs), in_specs=places(in_places),...  74.4 us
    pallas_call x1, Pallas kernels, perceptual_strip(): pl.pallas_call(perceptual_kernel, out_shape=b16(8, 3, 16, 128), in_specs=...  19.7 us

profile of v7, /device:TPU:32, one launch (start us, length us, event | category | flops | bytes accessed | tf_op | source)
XLA Modules:
  0.0 96.1 jit_solution(9134837653354380924)
XLA Ops:
  0.6 28.5 %shard_map.95 = (bf16[8,10,16,384]{3,2,1,0:T(8,128)(2,1)}, bf16[8,10,16,384]{3,2,1,0:T(8,128)(2,1)}, f32[6,128,128]{2,1,0:T(8,128)}, f32[8,10,32,128]{3,2,1,0:T(...) custom-call(bf16[24,8,16,128]{3,2,1,0:T(8,128)(2,1)} %bitcast.6, ...), custom_call_target="tpu_custom_call" | custom-call | tf_op jit(solution)/shard_map/pallas_call | solution.py:937
  29.2 19.7 %shard_map.96.pixel_hbm = bf16[8,3,16,128]{3,2,1,0:T(8,128)(2,1)} custom-call(bf16[3,8,16,128]{3,2,1,0:T(8,128)(2,1)} %get-tuple-element.9.near_hbm, bf16[3,32,128]{2,1,0:T(8,128)(2,1)} %get-tuple-element.10.guide_hbm, bf16[27,64]{1,0:T(8,128)(2,1)} %vgg_first_ref.1, bf16[64,576]{1,0:T(8,128)(2,1)} %bitcast.7, bf16[576,128]{1,0:T(8,128)(2,1)} %vgg_third_ref.1), custom_call_target="tpu_custom_call" | custom-call | tf_op jit(solution)/shard_map/pallas_call | solution.py:282
  48.9 45.8 %shard_map.97 = f32[2,16,128]{2,1,0:T(8,128)} custom-call(bf16[8,3,16,128]{3,2,1,0:T(8,128)(2,1)} %shard_map.96.pixel_hbm, bf16[8,10,16,384]{3,2,1,0:T(8,128)(2,1)} %get-tuple-element.11.cells_hbm, bf16[8,10,16,384]{3,2,1,0:T(8,128)(2,1)} %get-tuple-element.12.hidden_hbm, f32[6,128,128]{2,1,0:T(8,128)} %get-tuple-element.13.slope1_hbm, ...), custom_call_target="tpu_custom_call" | custom-call | tf_op jit(solution)/shard_map/pallas_call | solution.py:937
  94.7 0.7 copy.12
  95.5 0.6 slice_reduce_fusion

commit v8 on v7

--- a/solution.py
+++ b/solution.py
@@ -65,9 +65,21 @@
     return value, half + preact * (1.0 - inner_tanh * inner_tanh) * bend
 
 
+def turned_columns(columns, out_ref):
+    @pl.loop(0, 8)
+    def _(f):
+        value = columns[f]
+        for dr in range(3):
+            for k in range(3):
+                block = value[dr : dr + 8, :, 128 * k : 128 * (k + 1)].reshape(128, 128)
+                place = pl.ds(pl.multiple_of(128 * f, 128), 128)
+                out_ref[dr, 128 * k : 128 * (k + 1), place] = block.T
+
+
 def perceptual_kernel(
-    near_hbm, guide_hbm, vgg_first_ref, vgg_second_ref, vgg_third_ref, out_ref,
-    near_ref, guide_ref, load_sem, first32, w1_ref, w1_back32, w1_back_ref, planes_ref, guides,
+    near_hbm, guide_hbm, vgg_first_ref, vgg_second_ref, vgg_third_ref, hidden_hbm, cells_hbm,
+    out_ref, hidden_turned_hbm, cells_turned_hbm,
+    hidden_ref, cells_ref, hidden_turned, cells_turned, store_sem, near_ref, guide_ref, load_sem, first32, w1_ref, w1_back32, w1_back_ref, planes_ref, guides,
     taps, act1, slope1, pooled, delta3, diff2, slope2, delta2, delta1, tmp, pixels, strip,
     w2_ref, w3_ref, w3_back_ref, w2_back_ref, send_sem, recv_sem, own_sem,
 ):
@@ -99,6 +111,12 @@
     loads = [
         pltpu.make_async_copy(near_hbm, near_ref, load_sem.at[0]),
         pltpu.make_async_copy(guide_hbm, guide_ref, load_sem.at[1]),
+        pltpu.make_async_copy(hidden_hbm, hidden_ref, load_sem.at[2]),
+        pltpu.make_async_copy(cells_hbm, cells_ref, load_sem.at[3]),
+    ]
+    stores = [
+        pltpu.make_async_copy(hidden_turned, hidden_turned_hbm, store_sem.at[0]),
+        pltpu.make_async_copy(cells_turned, cells_turned_hbm, store_sem.at[1]),
     ]
     for load in loads:
         load.start()
@@ -115,7 +133,7 @@
     w1_back_ref[...] = w1_back32[...].astype(jnp.bfloat16)
     lay_out_perceptual(vgg_second_ref, vgg_third_ref, w2_ref, w3_ref, w3_back_ref, w2_back_ref)
     row0 = 8 * r - 8
-    for load in loads:
+    for load in loads[:2]:
         load.wait()
     kind = lax.broadcasted_iota(jnp.int32, (8, 128), 0)
     block = lax.broadcasted_iota(jnp.int32, (8, 128), 1) // 16
@@ -273,21 +291,34 @@
         ).wait_recv()
 
     targets(start)
+    loads[2].wait()
+    turned_columns(hidden_ref, hidden_turned)
+    stores[0].start()
+    loads[3].wait()
+    turned_columns(cells_ref, cells_turned)
+    stores[1].start()
     sources(arrive)
     targets(finish)
-
-
-def perceptual_strip(near, guides, *weights):
+    for store in stores:
+        store.wait()
+
+
+def perceptual_strip(*operands):
     f32, half = jnp.float32, jnp.bfloat16
     return pl.pallas_call(
         perceptual_kernel,
-        out_shape=b16(8, 3, 16, 128),
-        in_specs=places("hhvvv"),
-        out_specs=in_vmem(1)[0],
+        out_shape=(b16(8, 3, 16, 128), b16(3, 384, 1024), b16(3, 384, 1024)),
+        in_specs=places("hhvvvhh"),
+        out_specs=tuple(places("vhh")),
         scratch_shapes=[
+            pltpu.VMEM((8, 10, 16, 384), half),
+            pltpu.VMEM((8, 10, 16, 384), half),
+            pltpu.VMEM((3, 384, 1024), half),
+            pltpu.VMEM((3, 384, 1024), half),
+            pltpu.SemaphoreType.DMA((2,)),
             pltpu.VMEM((3, 8, 16, 128), half),
             pltpu.VMEM((3, 32, 128), half),
-            pltpu.SemaphoreType.DMA((2,)),
+            pltpu.SemaphoreType.DMA((4,)),
             pltpu.VMEM((72, 128), f32),
             pltpu.VMEM((72, 128), half),
             pltpu.VMEM((8, 1152), f32),
@@ -317,7 +348,7 @@
         compiler_params=pltpu.CompilerParams(
             collective_id=4, has_side_effects=True, vmem_limit_bytes=58 * 2**20
         ),
-    )(near, guides, *weights)
+    )(*operands)
 
 
 def taps_in_lanes(weight_ref, out_ref):
@@ -726,10 +757,9 @@
 
 
 def weight_terms(columns, delta, terms, low, high):
-    @pl.loop(low, high)
-    def _(q):
-        cells = columns[pl.ds(q // 3, 6), pl.ds(lax.rem(q, 3), 8)].reshape(768, 384)
-        terms[pl.ds(pl.multiple_of(384 * q, 384), 384)] = transposed_dot(cells, delta[...])
+    for q in range(low, high):
+        cells = columns[q % 3, :, 128 * (q // 3) : 128 * (q // 3) + 768]
+        terms[384 * q : 384 * (q + 1)] = dot32(cells, delta[...])
 
 
 def by_chip(terms, out_ref, which, low, high):
@@ -757,7 +787,7 @@
             )
         )
     ]
-    for load in loads:
+    for load in loads[5:] + loads[:5]:
         load.start()
     zh, x, y, core = r // 4, lax.rem(r, 4), c // 2, lax.rem(c, 2)
     z = g * 2 + zh
@@ -976,7 +1006,9 @@
         ],
         dec_input.reshape(24, 8, 16, channels), target, conv_first, conv_second, rgb_weight,
     )
-    pixels = perceptual_strip(colour_near, guide_near, vgg_first, vgg_second.T, vgg_third)
+    pixels, hidden_turned, cells_turned = perceptual_strip(
+        colour_near, guide_near, vgg_first, vgg_second.T, vgg_third, hidden, cells
+    )
     sums = talking_call(
         backward_kernel,
         1,
@@ -986,7 +1018,7 @@
         (f32_shape(2, 16, 128),),
         [
             vmem((8, 3, 16, 128), half),
-            vmem((8, 10, 16, 384), half), vmem((8, 10, 16, 384), half), vmem((6, 128, 128), f32),
+            vmem((3, 384, 1024), half), vmem((3, 384, 1024), half), vmem((6, 128, 128), f32),
             vmem((8, 10, 32, 128), f32), vmem((1152, 384), half), vmem((16, 128), f32), dma((6,)),
             pltpu.VMEM((8, 10, 32, 128), half),
             pltpu.VMEM((768, 128), half),
@@ -1005,7 +1037,7 @@
             dma((2, 21)),
             dma((2, 21)),
         ],
-        pixels, cells, hidden, slope1, slope2, turned, rgb_weight,
+        pixels, cells_turned, hidden_turned, slope1, slope2, turned, rgb_weight,
     )
     flat = sums[0].reshape(2, 2048)[:, :1728]
     return flat[0], flat[1]

time: 96.4 us -> 94.3 us (0.978)
  Pallas kernels: 94.1 us -> 92 us
    pallas_call x2, Pallas kernels: 74.4 us -> 72.3 us  [talking_call(): pl.pallas_call(kernel, out_shape=tuple(outs), in_specs=places(in_places),...]
where the time goes in v8:
time: 94.3 us; the launch traced here: 94.1 us
  Pallas kernels  92 us (98%)
  local copies, waits for them, and re-layouts  1.37 us (1%)
    pallas_call x2, Pallas kernels, talking_call(): pl.pallas_call(kernel, out_shape=tuple(outs), in_specs=places(in_places),...  72.3 us
    pallas_call x1, Pallas kernels, perceptual_strip(): pl.pallas_call(perceptual_kernel, out_shape=(b16(8, 3, 16, 128), b16(3, 3...  19.7 us

profile of v8, /device:TPU:32, one launch (start us, length us, event | category | flops | bytes accessed | tf_op | source)
XLA Modules:
  0.0 94.1 jit_solution(4986510343700864674)
XLA Ops:
  0.6 28.6 %shard_map.95 = (bf16[8,10,16,384]{3,2,1,0:T(8,128)(2,1)}, bf16[8,10,16,384]{3,2,1,0:T(8,128)(2,1)}, f32[6,128,128]{2,1,0:T(8,128)}, f32[8,10,32,128]{3,2,1,0:T(...) custom-call(bf16[24,8,16,128]{3,2,1,0:T(8,128)(2,1)} %bitcast.6, ...), custom_call_target="tpu_custom_call" | custom-call | tf_op jit(solution)/shard_map/pallas_call | solution.py:967
  29.3 19.7 %shard_map.96 = (bf16[8,3,16,128]{3,2,1,0:T(8,128)(2,1)}, bf16[3,384,1024]{2,1,0:T(8,128)(2,1)}, bf16[3,384,1024]{2,1,0:T(8,128)(2,1)}) custom-call(bf16[3,8,16,128]{3,2,1,0:T(8,128)(2,1)} %get-tuple-element.12.near_hbm, bf16[3,32,128]{2,1,0:T(8,128)(2,1)} %get-tuple-element.13.guide_hbm, bf16[27,64]{1,0:T(8,128)(2,1)} %vgg_first_ref.1, ...), custom_call_target="tpu_custom_call" | custom-call | tf_op jit(solution)/shard_map/pallas_call | solution.py:308
  49.0 43.7 %shard_map.97 = f32[2,16,128]{2,1,0:T(8,128)} custom-call(bf16[8,3,16,128]{3,2,1,0:T(8,128)(2,1)} %get-tuple-element.16.pixel_hbm, bf16[3,384,1024]{2,1,0:T(8,128)(2,1)} %get-tuple-element.17.cells_hbm, bf16[3,384,1024]{2,1,0:T(8,128)(2,1)} %get-tuple-element.18.hidden_hbm, f32[6,128,128]{2,1,0:T(8,128)} %get-tuple-element.19.slope1_hbm, ...), custom_call_target="tpu_custom_call" | custom-call | tf_op jit(solution)/shard_map/pallas_call | solution.py:967
  92.7 0.7 copy.12
  93.4 0.6 slice_reduce_fusion

commit v9 on v8

--- a/solution.py
+++ b/solution.py
@@ -938,21 +938,22 @@
     second_high = first_step(1, 1, swap_high)
     pl.loop(2, 6, unroll=2)(back_frame)
     loads[4].wait()
-    second_low = second_step(1, 0, second_low)
     weight_terms(cells_ref, delta, terms, 0, 5)
     by_chip(terms, sending, 0, 0, 4)
     swap_low = to_partner(0, 0)
-    second_high = second_step(1, 1, second_high)
     weight_terms(cells_ref, delta, terms, 5, 9)
     by_chip(terms, sending, 0, 4, 8)
     swap_high = to_partner(0, 1)
     first_low = first_step(0, 0, swap_low)
+    first_high = first_step(0, 1, swap_high)
+    second_low = second_step(1, 0, second_low)
+    second_high = second_step(1, 1, second_high)
     moves_second = third_step(1, second_low + second_high)
-    first_high = first_step(0, 1, swap_high)
-    result(1, moves_second)
     first_low = second_step(0, 0, first_low)
     first_high = second_step(0, 1, first_high)
-    result(0, third_step(0, first_low + first_high))
+    moves_first = third_step(0, first_low + first_high)
+    result(1, moves_second)
+    result(0, moves_first)
 
 
 def f32_shape(*shape):

time: 94.3 us -> 90.2 us (0.957)
  Pallas kernels: 92 us -> 87.9 us
    pallas_call x2, Pallas kernels: 72.3 us -> 68.2 us  [talking_call(): pl.pallas_call(kernel, out_shape=tuple(outs), in_specs=places(in_places),...]
where the time goes in v9:
time: 90.2 us; the launch traced here: 89.9 us
  Pallas kernels  87.9 us (97%)
  local copies, waits for them, and re-layouts  1.37 us (2%)
    pallas_call x2, Pallas kernels, talking_call(): pl.pallas_call(kernel, out_shape=tuple(outs), in_specs=places(in_places),...  68.2 us
    pallas_call x1, Pallas kernels, perceptual_strip(): pl.pallas_call(perceptual_kernel, out_shape=(b16(8, 3, 16, 128), b16(3, 3...  19.7 us

profile of v9, /device:TPU:32, one launch (start us, length us, event | category | flops | bytes accessed | tf_op | source)
XLA Modules:
  0.0 89.9 jit_solution(10825121112590640817)
XLA Ops:
  0.6 28.6 %shard_map.95 = (bf16[8,10,16,384]{3,2,1,0:T(8,128)(2,1)}, bf16[8,10,16,384]{3,2,1,0:T(8,128)(2,1)}, f32[6,128,128]{2,1,0:T(8,128)}, f32[8,10,32,128]{3,2,1,0:T(...) custom-call(bf16[24,8,16,128]{3,2,1,0:T(8,128)(2,1)} %bitcast.6, ...), custom_call_target="tpu_custom_call" | custom-call | tf_op jit(solution)/shard_map/pallas_call | solution.py:968
  29.3 19.7 %shard_map.96 = (bf16[8,3,16,128]{3,2,1,0:T(8,128)(2,1)}, bf16[3,384,1024]{2,1,0:T(8,128)(2,1)}, bf16[3,384,1024]{2,1,0:T(8,128)(2,1)}) custom-call(bf16[3,8,16,128]{3,2,1,0:T(8,128)(2,1)} %get-tuple-element.12.near_hbm, bf16[3,32,128]{2,1,0:T(8,128)(2,1)} %get-tuple-element.13.guide_hbm, bf16[27,64]{1,0:T(8,128)(2,1)} %vgg_first_ref.1, ...), custom_call_target="tpu_custom_call" | custom-call | tf_op jit(solution)/shard_map/pallas_call | solution.py:308
  49.0 39.5 %shard_map.97 = f32[2,16,128]{2,1,0:T(8,128)} custom-call(bf16[8,3,16,128]{3,2,1,0:T(8,128)(2,1)} %get-tuple-element.16.pixel_hbm, bf16[3,384,1024]{2,1,0:T(8,128)(2,1)} %get-tuple-element.17.cells_hbm, bf16[3,384,1024]{2,1,0:T(8,128)(2,1)} %get-tuple-element.18.hidden_hbm, f32[6,128,128]{2,1,0:T(8,128)} %get-tuple-element.19.slope1_hbm, ...), custom_call_target="tpu_custom_call" | custom-call | tf_op jit(solution)/shard_map/pallas_call | solution.py:968
  88.5 0.7 copy.12
  89.2 0.6 slice_reduce_fusion

commit v10 on v9

--- a/solution.py
+++ b/solution.py
@@ -925,7 +925,6 @@
     weight_terms(hidden_ref, delta, terms, 5, 9)
     by_chip(terms, sending, 1, 4, 8)
     swap_high = to_partner(1, 1)
-    second_low = first_step(1, 0, swap_low)
     loads[2].wait()
     loads[3].wait()
 
@@ -935,8 +934,9 @@
         delta[pl.ds(pl.multiple_of(128 * f, 128), 128)] = value
 
     pl.loop(0, 2, unroll=2)(back_frame)
+    second_low = first_step(1, 0, swap_low)
+    pl.loop(2, 6, unroll=2)(back_frame)
     second_high = first_step(1, 1, swap_high)
-    pl.loop(2, 6, unroll=2)(back_frame)
     loads[4].wait()
     weight_terms(cells_ref, delta, terms, 0, 5)
     by_chip(terms, sending, 0, 0, 4)

time: 90.2 us -> 89.8 us (level)
  no operation moved by 1% of the time
where the time goes in v10:
time: 89.8 us; the launch traced here: 89.5 us
  Pallas kernels  87.5 us (97%)
  local copies, waits for them, and re-layouts  1.37 us (2%)
    pallas_call x2, Pallas kernels, talking_call(): pl.pallas_call(kernel, out_shape=tuple(outs), in_specs=places(in_places),...  67.8 us
    pallas_call x1, Pallas kernels, perceptual_strip(): pl.pallas_call(perceptual_kernel, out_shape=(b16(8, 3, 16, 128), b16(3, 3...  19.7 us

profile of v10, /device:TPU:32, one launch (start us, length us, event | category | flops | bytes accessed | tf_op | source)
XLA Modules:
  0.0 89.5 jit_solution(1233451833106873529)
XLA Ops:
  0.6 28.6 %shard_map.95 = (bf16[8,10,16,384]{3,2,1,0:T(8,128)(2,1)}, bf16[8,10,16,384]{3,2,1,0:T(8,128)(2,1)}, f32[6,128,128]{2,1,0:T(8,128)}, f32[8,10,32,128]{3,2,1,0:T(...) custom-call(bf16[24,8,16,128]{3,2,1,0:T(8,128)(2,1)} %bitcast.6, ...), custom_call_target="tpu_custom_call" | custom-call | tf_op jit(solution)/shard_map/pallas_call | solution.py:968
  29.3 19.7 %shard_map.96 = (bf16[8,3,16,128]{3,2,1,0:T(8,128)(2,1)}, bf16[3,384,1024]{2,1,0:T(8,128)(2,1)}, bf16[3,384,1024]{2,1,0:T(8,128)(2,1)}) custom-call(bf16[3,8,16,128]{3,2,1,0:T(8,128)(2,1)} %get-tuple-element.12.near_hbm, bf16[3,32,128]{2,1,0:T(8,128)(2,1)} %get-tuple-element.13.guide_hbm, bf16[27,64]{1,0:T(8,128)(2,1)} %vgg_first_ref.1, ...), custom_call_target="tpu_custom_call" | custom-call | tf_op jit(solution)/shard_map/pallas_call | solution.py:308
  49.0 39.2 %shard_map.97 = f32[2,16,128]{2,1,0:T(8,128)} custom-call(bf16[8,3,16,128]{3,2,1,0:T(8,128)(2,1)} %get-tuple-element.16.pixel_hbm, bf16[3,384,1024]{2,1,0:T(8,128)(2,1)} %get-tuple-element.17.cells_hbm, bf16[3,384,1024]{2,1,0:T(8,128)(2,1)} %get-tuple-element.18.hidden_hbm, f32[6,128,128]{2,1,0:T(8,128)} %get-tuple-element.19.slope1_hbm, ...), custom_call_target="tpu_custom_call" | custom-call | tf_op jit(solution)/shard_map/pallas_call | solution.py:968
  88.1 0.7 copy.12
  88.9 0.6 slice_reduce_fusion
